TPU v7x, 32 devices: a whole 2x2x4 slice. The times are simulated.
32 devices in a mesh: rep: 4 (over y, x), shard: 8 (over z, core).
Axes of the slice: x: 2, y: 2, z: 4, core: 2. Of those that a mesh axis runs over, the one named last changes fastest.
Arguments:
- tokens: bfloat16 [16384, 1536], P(('rep', 'shard')), may hold values from -6 to 6
- lengths: int32 [32], P(('rep', 'shard')), may hold values from 128 to 512, as said below
- buckets: int32 [1023], replicated, may hold values from 0 to 31, as said below
- w_query: bfloat16 [1536, 768], P('shard'), may hold values from -0.0390625 to 0.0390625
- w_key: bfloat16 [1536, 768], P('shard'), may hold values from -0.15625 to 0.15625
- w_value: bfloat16 [1536, 768], P('shard'), may hold values from -0.15625 to 0.15625
- w_out: bfloat16 [768, 1536], P('shard'), may hold values from -1.25 to 1.25
- w_gate: bfloat16 [1536, 3968], P('shard'), may hold values from -0.15625 to 0.15625
- w_up: bfloat16 [1536, 3968], P('shard'), may hold values from -0.15625 to 0.15625
- w_down: bfloat16 [3968, 1536], P('shard'), may hold values from -0.09375 to 0.09375
- bias_table: bfloat16 [32, 12], P('shard'), may hold values from -4 to 4
- norm_attn: bfloat16 [1536], P('shard'), may hold values from 0.099609375 to 1.8984375
- norm_ffn: bfloat16 [1536], P('shard'), may hold values from 0.099609375 to 1.8984375
- cotangent: bfloat16 [16384, 1536], P(('rep', 'shard')), may hold values from -6 to 6
Outputs:
- output: bfloat16 [16384, 1536], P(('rep', 'shard'))
- grad_tokens: bfloat16 [16384, 1536], P(('rep', 'shard'))
- grad_query: float32 [1536, 768], P('shard')
- grad_key: float32 [1536, 768], P('shard')
- grad_value: float32 [1536, 768], P('shard')
- grad_out: float32 [768, 1536], P('shard')
- grad_gate: float32 [1536, 3968], P('shard')
- grad_up: float32 [1536, 3968], P('shard')
- grad_down: float32 [3968, 1536], P('shard')
- grad_table: float32 [32, 12], P('shard')
- grad_norm_attn: float32 [1536], P('shard')
- grad_norm_ffn: float32 [1536], P('shard')
Inputs may be any that keep to these rules, and one draw needn't show every extreme that they name: `lengths`: some sequence has exactly 512 valid bytes. `buckets`: non-decreasing in the absolute distance on each side; buckets 0 to 15 for distances of 0 or less, 16 to 31 for positive ones.
All inputs are finite; a program needn't handle non-finite values.
Results may differ from a plain program's by a relative error of at most 0.02.
Values may be sent and summed in bfloat16 or wider, within the bound.
No kernel may reach another device: no remote copies, remote signals or barrier semaphores. Data moves between devices by JAX's collectives and lax.ppermute only.
A program may use at most 320 MiB of HBM per device.

v0:
```python
import jax
import jax.numpy as jnp
from jax import lax
from jax.sharding import PartitionSpec as P

EPSILON = 1e-06
NEG_FILL = -1000000000.0


def toeplitz_rows(rel_bias, length):
    head_count = rel_bias.shape[0]
    padded = jnp.pad(rel_bias, ((0, 0), (0, 1)))
    repeated = jnp.broadcast_to(padded[:, None, :], (head_count, length, 2 * length))
    flattened = repeated.reshape(head_count, 2 * length * length)[:, : length * (2 * length - 1)]
    return flattened.reshape(head_count, length, 2 * length - 1)[:, :, length - 1 :]


def diagonal_sums(grad_scores):
    head_count = grad_scores.shape[0]
    length = grad_scores.shape[1]
    flipped = grad_scores[:, ::-1, :]
    padded = jnp.pad(flipped, ((0, 0), (0, 0), (0, length)))
    flattened = padded.reshape(head_count, 2 * length * length)[:, : length * (2 * length - 1)]
    return jnp.sum(flattened.reshape(head_count, length, 2 * length - 1), axis=1)


def norm_back(upstream, unit_rows, scale_rows, gain_rows):
    scaled = upstream * gain_rows
    return scale_rows * (scaled - unit_rows * jnp.mean(scaled * unit_rows, axis=-1, keepdims=True))


def shards(
    tokens,
    lengths,
    buckets,
    w_query,
    w_key,
    w_value,
    w_out,
    w_gate,
    w_up,
    w_down,
    bias_table,
    norm_attn,
    norm_ffn,
    cotangent,
):
    full = (
        lax.all_gather(w_query, "shard", axis=0, tiled=True),
        lax.all_gather(w_key, "shard", axis=0, tiled=True),
        lax.all_gather(w_value, "shard", axis=0, tiled=True),
        lax.all_gather(w_out, "shard", axis=0, tiled=True),
        lax.all_gather(w_gate, "shard", axis=0, tiled=True),
        lax.all_gather(w_up, "shard", axis=0, tiled=True),
        lax.all_gather(w_down, "shard", axis=0, tiled=True),
        lax.all_gather(bias_table, "shard", axis=0, tiled=True),
        lax.all_gather(norm_attn, "shard", axis=0, tiled=True),
        lax.all_gather(norm_ffn, "shard", axis=0, tiled=True),
    )
    f_query, f_key, f_value, f_out, f_gate, f_up, f_down, f_table, f_attn, f_ffn = full
    length = tokens.shape[0]
    head_count = f_table.shape[1]
    inner_width = f_query.shape[1]
    head_size = inner_width // head_count
    bucket_count = f_table.shape[0]
    positions = jnp.arange(length, dtype=jnp.int32)
    one_hot = (buckets[:, None] == jnp.arange(bucket_count, dtype=jnp.int32)[None, :]).astype(
        jnp.float32
    )
    rel_bias = jnp.dot(f_table.astype(jnp.float32).T, one_hot.T, precision=lax.Precision.HIGHEST)
    mask_row = jnp.where(positions < lengths[0], 0.0, NEG_FILL).astype(jnp.float32)
    bias_full = toeplitz_rows(rel_bias, length) + mask_row[None, None, :]
    floats_in = tokens.astype(jnp.float32)
    gain_one = f_attn.astype(jnp.float32)
    gain_two = f_ffn.astype(jnp.float32)
    scale_one = lax.rsqrt(jnp.mean(floats_in * floats_in, axis=-1, keepdims=True) + EPSILON)
    unit_one = floats_in * scale_one
    normed_one = (unit_one * gain_one).astype(jnp.bfloat16)
    queries = (
        jnp.dot(normed_one, f_query, preferred_element_type=jnp.float32)
        .astype(jnp.bfloat16)
        .reshape(length, head_count, head_size)
    )
    key_rows = (
        jnp.dot(normed_one, f_key, preferred_element_type=jnp.float32)
        .astype(jnp.bfloat16)
        .reshape(length, head_count, head_size)
    )
    value_rows = (
        jnp.dot(normed_one, f_value, preferred_element_type=jnp.float32)
        .astype(jnp.bfloat16)
        .reshape(length, head_count, head_size)
    )

    def scores_of():
        return (
            jnp.einsum("qhd,khd->hqk", queries, key_rows, preferred_element_type=jnp.float32)
            + bias_full
        )

    scores = scores_of()
    row_max = jnp.max(scores, axis=-1, keepdims=True)
    exp_terms = jnp.exp(scores - row_max)
    row_total = jnp.sum(exp_terms, axis=-1, keepdims=True)
    log_total = row_max + jnp.log(row_total)
    prob_low = (exp_terms / row_total).astype(jnp.bfloat16)
    context = jnp.einsum("hqk,khd->qhd", prob_low, value_rows, preferred_element_type=jnp.float32)
    context = context.reshape(length, inner_width).astype(jnp.bfloat16)
    attended = floats_in + jnp.dot(context, f_out, preferred_element_type=jnp.float32)
    scale_two = lax.rsqrt(jnp.mean(attended * attended, axis=-1, keepdims=True) + EPSILON)
    unit_two = attended * scale_two
    normed_two = (unit_two * gain_two).astype(jnp.bfloat16)
    gate_pre = jnp.dot(normed_two, f_gate, preferred_element_type=jnp.float32)
    up_pre = jnp.dot(normed_two, f_up, preferred_element_type=jnp.float32)
    gelu_out, gelu_pull = jax.vjp(
        lambda inner_in: jax.nn.gelu(inner_in, approximate=True), gate_pre
    )
    hidden = (gelu_out * up_pre).astype(jnp.bfloat16)
    output = (attended + jnp.dot(hidden, f_down, preferred_element_type=jnp.float32)).astype(
        jnp.bfloat16
    )
    again = (
        lax.all_gather(w_query, "shard", axis=0, tiled=True),
        lax.all_gather(w_key, "shard", axis=0, tiled=True),
        lax.all_gather(w_value, "shard", axis=0, tiled=True),
        lax.all_gather(w_out, "shard", axis=0, tiled=True),
        lax.all_gather(w_gate, "shard", axis=0, tiled=True),
        lax.all_gather(w_up, "shard", axis=0, tiled=True),
        lax.all_gather(w_down, "shard", axis=0, tiled=True),
        lax.all_gather(bias_table, "shard", axis=0, tiled=True),
        lax.all_gather(norm_attn, "shard", axis=0, tiled=True),
        lax.all_gather(norm_ffn, "shard", axis=0, tiled=True),
    )
    b_query, b_key, b_value, b_out, b_gate, b_up, b_down, b_table, b_attn, b_ffn = again
    gain_one = b_attn.astype(jnp.float32)
    gain_two = b_ffn.astype(jnp.float32)
    grad_in = cotangent.astype(jnp.float32)
    down_term = jnp.dot(hidden.T, cotangent, preferred_element_type=jnp.float32)
    d_hidden = jnp.dot(cotangent, b_down.T, preferred_element_type=jnp.float32)
    d_gate = gelu_pull(d_hidden * up_pre)[0].astype(jnp.bfloat16)
    d_up = (d_hidden * gelu_out).astype(jnp.bfloat16)
    gate_term = jnp.dot(normed_two.T, d_gate, preferred_element_type=jnp.float32)
    up_term = jnp.dot(normed_two.T, d_up, preferred_element_type=jnp.float32)
    d_normed_two = jnp.dot(d_gate, b_gate.T, preferred_element_type=jnp.float32) + jnp.dot(
        d_up, b_up.T, preferred_element_type=jnp.float32
    )
    ffn_gain_term = jnp.sum(d_normed_two * unit_two, axis=0)
    d_attended = grad_in + norm_back(d_normed_two, unit_two, scale_two, gain_two)
    d_branch = d_attended.astype(jnp.bfloat16)
    out_term = jnp.dot(context.T, d_branch, preferred_element_type=jnp.float32)
    d_context = (
        jnp.dot(d_branch, b_out.T, preferred_element_type=jnp.float32)
        .astype(jnp.bfloat16)
        .reshape(length, head_count, head_size)
    )
    scores = scores_of()
    prob_full = jnp.exp(scores - log_total)
    prob_low = prob_full.astype(jnp.bfloat16)
    d_probs = jnp.einsum("qhd,khd->hqk", d_context, value_rows, preferred_element_type=jnp.float32)
    d_scores = (
        prob_full * (d_probs - jnp.sum(d_probs * prob_full, axis=-1, keepdims=True))
    ).astype(jnp.bfloat16)
    d_values = (
        jnp.einsum("hqk,qhd->khd", prob_low, d_context, preferred_element_type=jnp.float32)
        .astype(jnp.bfloat16)
        .reshape(length, inner_width)
    )
    d_queries = (
        jnp.einsum("hqk,khd->qhd", d_scores, key_rows, preferred_element_type=jnp.float32)
        .astype(jnp.bfloat16)
        .reshape(length, inner_width)
    )
    d_keys = (
        jnp.einsum("hqk,qhd->khd", d_scores, queries, preferred_element_type=jnp.float32)
        .astype(jnp.bfloat16)
        .reshape(length, inner_width)
    )
    d_relative = diagonal_sums(d_scores.astype(jnp.float32))
    table_term = jnp.dot(one_hot.T, d_relative.T, precision=lax.Precision.HIGHEST)
    query_term = jnp.dot(normed_one.T, d_queries, preferred_element_type=jnp.float32)
    key_term = jnp.dot(normed_one.T, d_keys, preferred_element_type=jnp.float32)
    value_term = jnp.dot(normed_one.T, d_values, preferred_element_type=jnp.float32)
    d_normed_one = (
        jnp.dot(d_queries, b_query.T, preferred_element_type=jnp.float32)
        + jnp.dot(d_keys, b_key.T, preferred_element_type=jnp.float32)
        + jnp.dot(d_values, b_value.T, preferred_element_type=jnp.float32)
    )
    attn_gain_term = jnp.sum(d_normed_one * unit_one, axis=0)
    grad_tokens = (d_attended + norm_back(d_normed_one, unit_one, scale_one, gain_one)).astype(
        jnp.bfloat16
    )
    (
        shard_query,
        shard_key,
        shard_value,
        shard_out,
        shard_gate,
        shard_up,
        shard_down,
        shard_table,
        shard_attn,
        shard_ffn,
    ) = (
        lax.psum_scatter(
            query_term.astype(jnp.bfloat16), "shard", scatter_dimension=0, tiled=True
        ).astype(jnp.float32),
        lax.psum_scatter(
            key_term.astype(jnp.bfloat16), "shard", scatter_dimension=0, tiled=True
        ).astype(jnp.float32),
        lax.psum_scatter(
            value_term.astype(jnp.bfloat16), "shard", scatter_dimension=0, tiled=True
        ).astype(jnp.float32),
        lax.psum_scatter(
            out_term.astype(jnp.bfloat16), "shard", scatter_dimension=0, tiled=True
        ).astype(jnp.float32),
        lax.psum_scatter(
            gate_term.astype(jnp.bfloat16), "shard", scatter_dimension=0, tiled=True
        ).astype(jnp.float32),
        lax.psum_scatter(
            up_term.astype(jnp.bfloat16), "shard", scatter_dimension=0, tiled=True
        ).astype(jnp.float32),
        lax.psum_scatter(
            down_term.astype(jnp.bfloat16), "shard", scatter_dimension=0, tiled=True
        ).astype(jnp.float32),
        lax.psum_scatter(
            table_term.astype(jnp.bfloat16), "shard", scatter_dimension=0, tiled=True
        ).astype(jnp.float32),
        lax.psum_scatter(
            attn_gain_term.astype(jnp.bfloat16), "shard", scatter_dimension=0, tiled=True
        ).astype(jnp.float32),
        lax.psum_scatter(
            ffn_gain_term.astype(jnp.bfloat16), "shard", scatter_dimension=0, tiled=True
        ).astype(jnp.float32),
    )
    summed = (
        lax.psum(shard_query.astype(jnp.bfloat16), "rep").astype(jnp.float32),
        lax.psum(shard_key.astype(jnp.bfloat16), "rep").astype(jnp.float32),
        lax.psum(shard_value.astype(jnp.bfloat16), "rep").astype(jnp.float32),
        lax.psum(shard_out.astype(jnp.bfloat16), "rep").astype(jnp.float32),
        lax.psum(shard_gate.astype(jnp.bfloat16), "rep").astype(jnp.float32),
        lax.psum(shard_up.astype(jnp.bfloat16), "rep").astype(jnp.float32),
        lax.psum(shard_down.astype(jnp.bfloat16), "rep").astype(jnp.float32),
        lax.psum(shard_table.astype(jnp.bfloat16), "rep").astype(jnp.float32),
        lax.psum(shard_attn.astype(jnp.bfloat16), "rep").astype(jnp.float32),
        lax.psum(shard_ffn.astype(jnp.bfloat16), "rep").astype(jnp.float32),
    )
    return (
        output,
        grad_tokens,
        summed[0],
        summed[1],
        summed[2],
        summed[3],
        summed[4],
        summed[5],
        summed[6],
        summed[7],
        summed[8],
        summed[9],
    )


def solution(mesh):
    placed = (
        P(("rep", "shard"), None),
        P(("rep", "shard")),
        P(),
        P("shard", None),
        P("shard", None),
        P("shard", None),
        P("shard", None),
        P("shard", None),
        P("shard", None),
        P("shard", None),
        P("shard", None),
        P("shard"),
        P("shard"),
        P(("rep", "shard"), None),
    )
    return jax.shard_map(
        shards,
        mesh=mesh,
        in_specs=placed,
        out_specs=(
            P(("rep", "shard"), None),
            P(("rep", "shard"), None),
            P("shard", None),
            P("shard", None),
            P("shard", None),
            P("shard", None),
            P("shard", None),
            P("shard", None),
            P("shard", None),
            P("shard", None),
            P("shard"),
            P("shard"),
        ),
        check_vma=False,
    )
```

profile of v0, /device:TPU:10, one launch (start us, length us, event | category | flops | bytes accessed | tf_op | source)
XLA Modules:
  0.0 1411.2 jit_solution(12198402217847426835)
XLA Ops:
  13.8 13.4 all-reduce.8
  27.3 12.9 all-gather
  40.5 11.9 broadcast_in_dim.10
  52.4 11.0 pad.10
  63.4 39.7 %copy.64 = f32[2,8,512,1024]{3,1,2,0:T(8,128)} copy(f32[2,8,512,1024]{3,2,1,0:T(8,128)S(1)} %bitcast.78) | data formatting | bytes 67108864
  103.2 22.9 %slice.12 = f32[12,523776]{1,0:T(8,128)} slice(f32[12,524288]{1,0:T(8,128)} %bitcast.80), slice={[0:12], [0:523776]} | slice | bytes 50282496 | tf_op jit(solution)/shard_map/slice | solution.py:14
  126.1 51.5 %reshape.107 = f32[12,512,1023]{2,1,0:T(8,128)} reshape(f32[12,523776]{1,0:T(8,128)} %slice.12) | data formatting | bytes 50282496 | tf_op jit(solution)/shard_map/reshape | solution.py:15
  177.5 13.4 slice.13
  190.9 12.8 copy.62
  208.3 4.3 convolution_convert_fusion.11
  214.1 4.2 convolution_convert_fusion.10
  219.7 6.3 fusion.44
  234.0 4.0 multiply_reduce_fusion.3
  239.8 11.7 all-gather.17.cloned.1.call-done
  251.5 13.8 fusion.45
  265.3 99.4 %all-gather.19.cloned.1.call-done = bf16[1536,3968]{1,0:T(8,128)(2,1)} async-done(((bf16[192,3968]{1,0:T(8,128)(2,1)}), bf16[1536,3968]{1,0:T(8,128)(2,1)}) %all-gather.19.cloned.1.call-update) | async-done | bytes 12189712 | tf_op jit(solution)/shard_map/all_gather | solution.py:54
  364.8 13.8 fusion.46
  378.5 99.7 %all-gather.21.cloned.1.call-done = bf16[3968,1536]{1,0:T(8,128)(2,1)} async-done(((bf16[496,1536]{1,0:T(8,128)(2,1)}), bf16[3968,1536]{1,0:T(8,128)(2,1)}) %all-gather.21.cloned.1.call-update) | async-done | bytes 12189712 | tf_op jit(solution)/shard_map/all_gather | solution.py:55
  478.2 21.0 %multiply_convert_fusion.1 = (bf16[512,3968]{1,0:T(8,128)(2,1)}, bf16[512,3968]{1,0:T(8,128)(2,1)}, bf16[512,3968]{1,0:T(8,128)(2,1)}) fusion(f32[512,3968]{1,0:T(8,128)} %fusion.45, f32[512,3968]{1,0:T(8,128)} %fusion.46, bf16[512,1536]{1,0:T(8,128)(2,1)} %param.27, bf16[3968,1536]{1,0:T(8,128)(2,1)} %all-gather.21.cloned.1.call-done), kind=kOutput, calls=%fused_computation.20 | convolution fusion | flops 6293946368 | bytes 42205184 | tf_op jit(solution)/shard_map/dot_general | solution.py:139
  499.2 12.1 fusion.47
  511.3 11.3 multiply_reduce_fusion.1
  527.0 10.6 multiply_reduce_fusion
  539.6 6.9 multiply_convert_fusion
  553.2 4.8 convolution_convert_fusion.7
  561.9 6.7 fusion.26
  573.1 4.7 convolution_convert_fusion.3
  577.9 11.7 convolution_convert_fusion.2
  589.7 11.7 convolution_convert_fusion.1
  602.8 11.8 convolution_convert_fusion
  614.7 10.6 reduce-scatter.10.cloned.1.call-done
  625.3 38.2 %reduce-scatter.12.cloned.1.call-done = bf16[192,768]{1,0:T(8,128)(2,1)} async-done(((bf16[1536,768]{1,0:T(8,128)(2,1)}), bf16[192,768]{1,0:T(8,128)(2,1)}) %reduce-scatter.12.cloned.1.call-update) | async-done | bytes 294928 | tf_op jit(solution)/shard_map/reduce_scatter | solution.py:210
  663.5 37.9 %reduce-scatter.14.cloned.1.call-done = bf16[96,1536]{1,0:T(8,128)(2,1)} async-done(((bf16[768,1536]{1,0:T(8,128)(2,1)}), bf16[96,1536]{1,0:T(8,128)(2,1)}) %reduce-scatter.14.cloned.1.call-update) | async-done | bytes 294928 | tf_op jit(solution)/shard_map/reduce_scatter | solution.py:213
  701.5 127.8 %reduce-scatter.16.cloned.1.call-done = bf16[192,3968]{1,0:T(8,128)(2,1)} async-done(((bf16[1536,3968]{1,0:T(8,128)(2,1)}), bf16[192,3968]{1,0:T(8,128)(2,1)}) %reduce-scatter.16.cloned.1.call-update) | async-done | bytes 1523728 | tf_op jit(solution)/shard_map/reduce_scatter | solution.py:216
  829.3 126.3 %reduce-scatter.18.cloned.1.call-done = bf16[192,3968]{1,0:T(8,128)(2,1)} async-done(((bf16[1536,3968]{1,0:T(8,128)(2,1)}), bf16[192,3968]{1,0:T(8,128)(2,1)}) %reduce-scatter.18.cloned.1.call-update) | async-done | bytes 1523728 | tf_op jit(solution)/shard_map/reduce_scatter | solution.py:219
  955.6 126.1 %reduce-scatter.20.cloned.1.call-done = bf16[496,1536]{1,0:T(8,128)(2,1)} async-done(((bf16[3968,1536]{1,0:T(8,128)(2,1)}), bf16[496,1536]{1,0:T(8,128)(2,1)}) %reduce-scatter.20.cloned.1.call-update) | async-done | bytes 1523728 | tf_op jit(solution)/shard_map/reduce_scatter | solution.py:222
  1082.9 95.2 %rev.3 = f32[12,512,512]{1,2,0:T(8,128)} reverse(bf16[12,512,512]{1,2,0:T(8,128)(2,1)} %copy-done.1), dimensions={1} | reverse | bytes 18874368 | tf_op jit(solution)/shard_map/rev | solution.py:21
  1178.2 13.0 copy.63
  1191.2 14.9 %pad.9.clone = f32[12,512,1024]{2,1,0:T(8,128)} pad(f32[12,512,512]{2,1,0:T(8,128)} %copy.63, f32[]{:T(128)} %constant.6.clone.1), padding=0_0x0_0x0_512 | pad | bytes 37748740 | tf_op jit(solution)/shard_map/jit(_pad)/pad | solution.py:22
  1206.1 10.9 pad.11
  1217.0 39.7 %copy.65 = f32[2,8,512,1024]{3,1,2,0:T(8,128)} copy(f32[2,8,512,1024]{3,2,1,0:T(8,128)S(1)} %bitcast.79) | data formatting | bytes 67108864
  1256.7 22.6 %slice.14 = f32[12,523776]{1,0:T(8,128)} slice(f32[12,524288]{1,0:T(8,128)} %bitcast.81), slice={[0:12], [0:523776]} | slice | bytes 50282496 | tf_op jit(solution)/shard_map/slice | solution.py:23
  1279.3 41.5 %reshape.113 = f32[12,512,1023]{2,1,0:T(8,128)} reshape(f32[12,523776]{1,0:T(8,128)} %slice.14) | data formatting | bytes 50282496 | tf_op jit(solution)/shard_map/reshape | solution.py:24
  1320.9 9.1 reduce_sum.87
  1336.3 3.7 fusion.23
  1340.0 25.1 %all-reduce.7 = (bf16[32,12]{1,0:T(8,128)(2,1)S(1)}, bf16[1536]{0:T(1024)(128)(2,1)S(1)}, bf16[1536]{0:T(1024)(128)(2,1)S(1)}) all-reduce(bf16[32,12]{1,0:T(8,128)(2,1)S(1)} %convolution_convert_fusion.13, bf16[1536]{0:T(1024)(128)(2,1)S(1)} %get-tuple-element.14, ...), channel_id=9, replica_groups=mesh['rep'=4,'shard'=8] {'shard'}, use_global_device_ids=true, to_apply=%region_22.23.clone | all-reduce | flops 3456 | bytes 13824
  1365.3 8.0 all-reduce.9
  1375.1 5.0 fusion.22
  1380.3 10.7 fusion.25
  (175 shorter events, 67.0 us)
Async XLA Ops:
  7.2 4.8 copy-start.34
  7.2 6.1 copy-start.39
  7.2 6.3 copy-start.40
  7.2 20.0 %copy-start.35 = (bf16[4,12]{1,0:T(4,128)(2,1)S(1)}, bf16[4,12]{1,0:T(4,128)(2,1)}, u32[]{:S(2)}) copy-start(bf16[4,12]{1,0:T(4,128)(2,1)} %param.24) | copy-start | bytes 292
  7.2 32.9 %copy-start.37 = (s32[1023]{0:T(1024)S(1)}, s32[1023]{0:T(1024)}, u32[]{:S(2)}) copy-start(s32[1023]{0:T(1024)} %param.16) | copy-start | bytes 12280
  7.2 197.7 %all-gather.9.cloned.1.call-start = ((), (), s32[]{:S(2)}) async-start(), calls=%async_computation.7 | async-start | bytes 2654208 | tf_op jit(solution)/shard_map/all_gather | solution.py:51
  8.0 200.4 %all-gather.11.cloned.1.call-start = ((), (), s32[]{:S(2)}) async-start(), calls=%async_computation.8 | async-start | bytes 2654208 | tf_op jit(solution)/shard_map/all_gather | solution.py:49
  8.7 205.3 %all-gather.13.cloned.1.call-start = ((), (), s32[]{:S(2)}) async-start(), calls=%async_computation.9 | async-start | bytes 2654208 | tf_op jit(solution)/shard_map/all_gather | solution.py:50
  9.5 224.6 %all-gather.15.cloned.1.call-start = ((), (), s32[]{:S(2)}) async-start(), calls=%async_computation.10 | async-start | bytes 2654208 | tf_op jit(solution)/shard_map/all_gather | solution.py:52
  10.0 241.5 %all-gather.17.cloned.1.call-start = ((), (), s32[]{:S(2)}) async-start(), calls=%async_computation.11 | async-start | bytes 13713408 | tf_op jit(solution)/shard_map/all_gather | solution.py:53
  10.6 354.2 %all-gather.19.cloned.1.call-start = ((), (), s32[]{:S(2)}) async-start(), calls=%async_computation.12 | async-start | bytes 13713408 | tf_op jit(solution)/shard_map/all_gather | solution.py:54
  11.2 467.0 %all-gather.21.cloned.1.call-start = ((), (), s32[]{:S(2)}) async-start(), calls=%async_computation.13 | async-start | bytes 13713408 | tf_op jit(solution)/shard_map/all_gather | solution.py:55
  11.9 602.8 %reduce-scatter.8.cloned.1.call-start = ((), (), s32[]{:S(2)}) async-start(), calls=%async_computation.14 | async-start | bytes 2654208 | tf_op jit(solution)/shard_map/reduce_scatter | solution.py:204
  27.2 541.4 %copy-start.29 = (f32[1536]{0:T(1024)}, f32[1536]{0:T(1024)S(1)}, u32[]{:S(2)}) copy-start(f32[1536]{0:T(1024)S(1)} %convert_element_type.176) | copy-start | bytes 18436
  190.9 13.5 copy-start.4
  204.9 363.8 %copy-start.31 = (f32[512]{0:T(512)}, f32[512]{0:T(512)S(1)}, u32[]{:S(2)}) copy-start(f32[512]{0:T(512)S(1)} %add_rsqrt_fusion.1) | copy-start | bytes 6148
  208.3 19.6 %copy-start.12 = (bf16[512,768]{0,1:T(8,128)(2,1)}, bf16[512,768]{0,1:T(8,128)(2,1)S(1)}, u32[]{:S(2)}) copy-start(bf16[512,768]{0,1:T(8,128)(2,1)S(1)} %copy.48) | copy-start | bytes 2359300
  214.0 5.7 copy-start.10
  219.7 6.3 copy-start.8
  226.1 4.5 copy-start
  238.0 284.6 %copy-start.2 = (f32[512,1536]{1,0:T(8,128)}, f32[512,1536]{1,0:T(8,128)S(1)}, u32[]{:S(2)}) copy-start(f32[512,1536]{1,0:T(8,128)S(1)} %get-tuple-element.39) | copy-start | bytes 9437188
  499.2 12.1 copy-start.41
  511.3 11.3 copy-start.21
  527.0 10.7 slice-start
  527.0 10.8 slice-start.1
  527.0 12.6 slice-start.2
  539.6 6.9 copy-start.9
  546.5 2.7 copy-start.1
  546.5 3.5 copy-start.5
  550.1 3.1 copy-start.11
  553.1 72.2 %reduce-scatter.10.cloned.1.call-start = ((), (), s32[]{:S(2)}) async-start(), calls=%async_computation.15 | async-start | bytes 2654208 | tf_op jit(solution)/shard_map/reduce_scatter | solution.py:207
  561.9 101.7 %reduce-scatter.12.cloned.1.call-start = ((), (), s32[]{:S(2)}) async-start(), calls=%async_computation.16 | async-start | bytes 2654208 | tf_op jit(solution)/shard_map/reduce_scatter | solution.py:210
  569.6 3.5 copy-start.28
  572.6 5.3 copy-start.20
  572.6 128.8 %reduce-scatter.14.cloned.1.call-start = ((), (), s32[]{:S(2)}) async-start(), calls=%async_computation.17 | async-start | bytes 2654208 | tf_op jit(solution)/shard_map/reduce_scatter | solution.py:213
  577.8 251.4 %reduce-scatter.16.cloned.1.call-start = ((), (), s32[]{:S(2)}) async-start(), calls=%async_computation.18 | async-start | bytes 13713408 | tf_op jit(solution)/shard_map/reduce_scatter | solution.py:216
  589.7 365.9 %reduce-scatter.18.cloned.1.call-start = ((), (), s32[]{:S(2)}) async-start(), calls=%async_computation.19 | async-start | bytes 13713408 | tf_op jit(solution)/shard_map/reduce_scatter | solution.py:219
  601.4 480.2 %reduce-scatter.20.cloned.1.call-start = ((), (), s32[]{:S(2)}) async-start(), calls=%async_computation.20 | async-start | bytes 13713408 | tf_op jit(solution)/shard_map/reduce_scatter | solution.py:222
  614.7 776.3 %all-reduce.13.cloned.1.call-start = ((), (), s32[]{:S(2)}) async-start(), calls=%async_computation.21 | async-start | bytes 11501568 | tf_op jit(solution)/shard_map/psum | solution.py:236
  1320.9 9.1 copy-start.38
  1320.9 9.7 copy-start.17
  1330.6 3.3 copy-start.15
  1330.6 3.3 copy-start.18
  1336.3 3.7 copy-start.33
  1375.1 5.0 copy-start.3
  1375.1 5.2 copy-start.42
  1391.0 7.5 copy-start.25
  1394.7 5.6 copy-start.24
  (13 other events, 20.9 us)
Sparse Core Ops, SparseCore 0:
  9.7 32.6 all-gather.8
  44.1 30.8 all-gather.10
  76.6 30.7 all-gather.12
  108.8 30.7 all-gather.14
  141.1 110.3 all-gather.16
  253.0 111.7 all-gather.18
  366.4 111.7 all-gather.20
  553.2 33.5 reduce-scatter.7
  589.8 35.5 reduce-scatter.9
  628.1 35.4 reduce-scatter.11
  665.9 35.5 reduce-scatter.13
  703.6 125.5 reduce-scatter.15
  831.7 123.8 reduce-scatter.17
  957.7 123.8 reduce-scatter.19
  1086.7 133.0 all-reduce.12
where the time goes:
time: 1440 us; the launch traced here: 1410 us
  waiting for transfers between devices  682 us (47%)
  local copies, waits for them, and re-layouts  419 us (29%)
  matrix products  191 us (13%)
  blocking collectives  59.5 us (4%)
  other arithmetic  40.7 us (3%)
  between operations  17.6 us (1%)
    unnamed x106, local copies, waits for them, and re-layouts  142 us
    reduce_scatter x1, waiting for transfers between devices, shards(): lax.psum_scatter(gate_term.astype(jnp.bfloat16), 'shard', scatter_dimensi...  128 us
    reduce_scatter x1, waiting for transfers between devices, shards(): lax.psum_scatter(up_term.astype(jnp.bfloat16), 'shard', scatter_dimension...  126 us
    reduce_scatter x1, waiting for transfers between devices, shards(): lax.psum_scatter(down_term.astype(jnp.bfloat16), 'shard', scatter_dimensi...  126 us
    all_gather x1, waiting for transfers between devices, shards(): lax.all_gather(w_down, 'shard', axis=0, tiled=True)  99.7 us
    all_gather x1, waiting for transfers between devices, shards(): lax.all_gather(w_up, 'shard', axis=0, tiled=True)  99.4 us
    rev x1, local copies, waits for them, and re-layouts, diagonal_sums(): flipped = grad_scores[:, ::-1, :]  95.2 us
    reshape x1, local copies, waits for them, and re-layouts, toeplitz_rows(): flattened.reshape(head_count, length, 2 * length - 1)[:, :, length - 1:]  51.5 us
  transfers between devices with their start and end apart: 15, of which 9 were waited for; matrix products, arithmetic and copies ran while one was open for 39% of the time, Pallas kernels for 0%

commit v1 on v0

v1 whole, which is shorter than its diff:
```python
import functools

import jax
import jax.numpy as jnp
from jax import lax
from jax.experimental import pallas as pl
from jax.experimental.pallas import tpu as pltpu
from jax.sharding import PartitionSpec as P

NEG_FILL = -1000000000.0
VMEM_LIMIT = 56 * 1024 * 1024
TOEP = 128


def dot_nn(a, b):
    return lax.dot_general(a, b, (((1,), (0,)), ((), ())), preferred_element_type=jnp.float32)


def dot_nt(a, b):
    return lax.dot_general(a, b, (((1,), (1,)), ((), ())), preferred_element_type=jnp.float32)


def dot_tn(a, b):
    return lax.dot_general(a, b, (((0,), (0,)), ((), ())), preferred_element_type=jnp.float32)


def biased_scores(rows_k, rows_q, bias_row, valid, length):
    steps = length // TOEP
    raw = dot_nt(rows_k, rows_q)
    width = bias_row.shape[-1]
    spread = jnp.broadcast_to(bias_row, (TOEP, width))
    table = pltpu.roll(spread, width - (TOEP - 1), 1, stride=1, stride_axis=0)
    blocks = []
    for step in range(steps):
        start = TOEP * (steps - 1 - step)
        row_at = lax.broadcasted_iota(jnp.int32, (TOEP, length), 0) + step * TOEP
        mask = jnp.where(row_at < valid, 0.0, NEG_FILL)
        blocks.append(
            raw[step * TOEP : (step + 1) * TOEP] + table[:, start : start + length] + mask
        )
    return jnp.concatenate(blocks, axis=0)


def attention_forward(valid_ref, bias_ref, q_ref, k_ref, v_ref, ctx_ref, lse_ref, *, head_size):
    length = q_ref.shape[1]
    pair = q_ref.shape[2] // head_size
    q, k, v = q_ref[0], k_ref[0], v_ref[0]
    lane_head = lax.broadcasted_iota(jnp.int32, q.shape, 1) // head_size
    v_turned = v.T
    outs = []
    for head in range(pair):
        own_q = jnp.where(lane_head == head, q, jnp.zeros_like(q))
        scores = biased_scores(k, own_q, bias_ref[0, head : head + 1], valid_ref[0], length)
        top = jnp.max(scores, axis=0, keepdims=True)
        terms = jnp.exp(scores - top)
        total = jnp.sum(terms, axis=0, keepdims=True)
        probs = (terms * (1.0 / total)).astype(jnp.bfloat16)
        lse_ref[0, head : head + 1] = top + jnp.log(total)
        outs.append(dot_nn(v_turned, probs)[head * head_size : (head + 1) * head_size])
    ctx_ref[...] = jnp.concatenate(outs, axis=0).T.astype(jnp.bfloat16)


def attention_backward(
    valid_ref, bias_ref, q_ref, k_ref, v_ref, dctx_ref, lse_ref, dq_ref, dk_ref, dv_ref, rel_ref, *, head_size
):
    length = q_ref.shape[1]
    pair = q_ref.shape[2] // head_size
    steps = length // TOEP
    q, k, v, dctx = q_ref[0], k_ref[0], v_ref[0], dctx_ref[...]
    lane_head = lax.broadcasted_iota(jnp.int32, q.shape, 1) // head_size
    k_turned = k.T
    width = bias_ref.shape[-1]
    flip = (
        lax.broadcasted_iota(jnp.int32, (TOEP, TOEP), 0)
        + lax.broadcasted_iota(jnp.int32, (TOEP, TOEP), 1)
        == TOEP - 1
    ).astype(jnp.bfloat16)
    dq_parts = []
    dk = dv = None
    for head in range(pair):
        mine = lane_head == head
        own_q = jnp.where(mine, q, jnp.zeros_like(q))
        own_d = jnp.where(mine, dctx, jnp.zeros_like(dctx))
        scores = biased_scores(k, own_q, bias_ref[0, head : head + 1], valid_ref[0], length)
        probs = jnp.exp(scores - lse_ref[0, head : head + 1])
        d_probs = dot_nt(v, own_d)
        inner = jnp.sum(d_probs * probs, axis=0, keepdims=True)
        d_scores = (probs * (d_probs - inner)).astype(jnp.bfloat16)
        part_v = dot_nn(probs.astype(jnp.bfloat16), own_d)
        part_k = dot_nn(d_scores, own_q)
        dv = part_v if dv is None else dv + part_v
        dk = part_k if dk is None else dk + part_k
        dq_parts.append(dot_nn(k_turned, d_scores)[head * head_size : (head + 1) * head_size])
        fold = None
        for step in range(steps):
            start = TOEP * (steps - 1 - step)
            turned = dot_nn(flip, d_scores[step * TOEP : (step + 1) * TOEP])
            pieces = []
            if start:
                pieces.append(jnp.zeros((TOEP, start), jnp.float32))
            pieces.append(turned)
            if width - start - length:
                pieces.append(jnp.zeros((TOEP, width - start - length), jnp.float32))
            padded = jnp.concatenate(pieces, axis=1)
            fold = padded if fold is None else fold + padded
        lined = pltpu.roll(fold, 0, 1, stride=1, stride_axis=0)
        rel_ref[0, head : head + 1] = jnp.sum(lined, axis=0, keepdims=True)
    dq_ref[0] = jnp.concatenate(dq_parts, axis=0).T.astype(jnp.bfloat16)
    dk_ref[0] = dk.astype(jnp.bfloat16)
    dv_ref[0] = dv.astype(jnp.bfloat16)


def run_forward(valid, bias_rows, qkv, head_size):
    halves, length, wide = qkv.shape
    half = wide // 3
    per = half // 128
    pairs = halves * per
    width = bias_rows.shape[-1]
    spec = lambda kind: pl.BlockSpec((1, length, 128), lambda p: (p // per, 0, kind * per + p % per))
    return pl.pallas_call(
        functools.partial(attention_forward, head_size=head_size),
        grid=(pairs,),
        in_specs=[
            pl.BlockSpec(memory_space=pltpu.SMEM),
            pl.BlockSpec((1, 2, width), lambda p: (p, 0, 0)),
            spec(0), spec(1), spec(2),
        ],
        out_specs=[
            pl.BlockSpec((length, 128), lambda p: (0, p)),
            pl.BlockSpec((1, 2, length), lambda p: (p, 0, 0)),
        ],
        out_shape=[
            jax.ShapeDtypeStruct((length, halves * half), jnp.bfloat16),
            jax.ShapeDtypeStruct((pairs, 2, length), jnp.float32),
        ],
        compiler_params=pltpu.CompilerParams(vmem_limit_bytes=VMEM_LIMIT),
        cost_estimate=pl.CostEstimate(
            flops=8 * pairs * 2 * length * length * 128,
            bytes_accessed=2 * qkv.size * 2,
            transcendentals=pairs * 2 * length * length,
        ),
    )(valid, bias_rows, qkv, qkv, qkv)


def run_backward(valid, bias_rows, qkv, d_context, lse, head_size):
    halves, length, wide = qkv.shape
    half = wide // 3
    per = half // 128
    pairs = halves * per
    width = bias_rows.shape[-1]
    spec = lambda kind: pl.BlockSpec((1, length, 128), lambda p: (p // per, 0, kind * per + p % per))
    out_spec = pl.BlockSpec((1, length, 128), lambda p: (p // per, 0, p % per))
    grad = jax.ShapeDtypeStruct((halves, length, half), jnp.bfloat16)
    row = pl.BlockSpec((1, 2, width), lambda p: (p, 0, 0))
    return pl.pallas_call(
        functools.partial(attention_backward, head_size=head_size),
        grid=(pairs,),
        in_specs=[
            pl.BlockSpec(memory_space=pltpu.SMEM),
            row,
            spec(0), spec(1), spec(2),
            pl.BlockSpec((length, 128), lambda p: (0, p)),
            pl.BlockSpec((1, 2, length), lambda p: (p, 0, 0)),
        ],
        out_specs=[out_spec, out_spec, out_spec, row],
        out_shape=[grad, grad, grad, jax.ShapeDtypeStruct((pairs, 2, width), jnp.float32)],
        compiler_params=pltpu.CompilerParams(vmem_limit_bytes=VMEM_LIMIT),
        cost_estimate=pl.CostEstimate(
            flops=16 * pairs * 2 * length * length * 128,
            bytes_accessed=4 * qkv.size * 2,
            transcendentals=pairs * 2 * length * length,
        ),
    )(valid, bias_rows, qkv, qkv, qkv, d_context, lse)


EPSILON = 1e-06
AXES = ("rep", "shard")


def split_kernel(core_ref, w_ref, keep_ref, send_ref, *, cuts, piece, padded):
    rows = w_ref.shape[0]
    first = core_ref[0] == 0
    w = w_ref[...].astype(jnp.float32)
    filler = jnp.zeros((rows, padded - piece), jnp.float32)
    for cut in range(cuts):
        even, odd = [
            jnp.concatenate(
                [w[:, (2 * cut + side) * piece : (2 * cut + side + 1) * piece], filler], axis=1
            )
            for side in (0, 1)
        ]
        keep_ref[:, cut * padded : (cut + 1) * padded] = jnp.where(first, even, odd).astype(
            jnp.bfloat16
        )
        send_ref[:, cut * padded : (cut + 1) * padded] = jnp.where(first, odd, even).astype(
            jnp.bfloat16
        )


def split_columns(core, w, piece, padded):
    rows, wide = w.shape
    cuts = wide // (2 * piece)
    out = jax.ShapeDtypeStruct((rows, cuts * padded), jnp.bfloat16)
    return pl.pallas_call(
        functools.partial(split_kernel, cuts=cuts, piece=piece, padded=padded),
        in_specs=[
            pl.BlockSpec(memory_space=pltpu.SMEM),
            pl.BlockSpec(memory_space=pltpu.VMEM),
        ],
        out_specs=[pl.BlockSpec(memory_space=pltpu.VMEM)] * 2,
        out_shape=[out, out],
        compiler_params=pltpu.CompilerParams(vmem_limit_bytes=VMEM_LIMIT),
        cost_estimate=pl.CostEstimate(flops=w.size, bytes_accessed=4 * w.size, transcendentals=0),
    )(core[None], w)


def join_kernel(core_ref, keep_ref, recv_ref, out_ref, *, cuts, piece, padded):
    first = core_ref[0] == 0
    for cut in range(cuts):
        mine = keep_ref[:, cut * padded : (cut + 1) * padded].astype(jnp.float32)
        other = recv_ref[:, cut * padded : (cut + 1) * padded].astype(jnp.float32)
        even = jnp.where(first, mine, other)
        odd = jnp.where(first, other, mine)
        out_ref[:, 2 * cut * piece : (2 * cut + 1) * piece] = even[:, :piece]
        out_ref[:, (2 * cut + 1) * piece : (2 * cut + 2) * piece] = odd[:, :piece]


def join_columns(core, keep, recv, piece, padded):
    rows = keep.shape[0]
    cuts = keep.shape[1] // padded
    return pl.pallas_call(
        functools.partial(join_kernel, cuts=cuts, piece=piece, padded=padded),
        in_specs=[
            pl.BlockSpec(memory_space=pltpu.SMEM),
            pl.BlockSpec(memory_space=pltpu.VMEM),
            pl.BlockSpec(memory_space=pltpu.VMEM),
        ],
        out_specs=pl.BlockSpec(memory_space=pltpu.VMEM),
        out_shape=jax.ShapeDtypeStruct((rows, 2 * cuts * piece), jnp.float32),
        compiler_params=pltpu.CompilerParams(vmem_limit_bytes=VMEM_LIMIT),
        cost_estimate=pl.CostEstimate(
            flops=keep.size, bytes_accessed=12 * keep.size, transcendentals=0
        ),
    )(core[None], keep, recv)


def place_kernel(at_ref, *refs, cuts):
    sources, out_ref, sems = refs[:-2], refs[-2], refs[-1]
    copies = []
    for number, (source, start, rows) in enumerate(cuts):
        to = pl.multiple_of(at_ref[number], 16)
        copies.append(
            pltpu.make_async_copy(
                sources[source].at[pl.ds(start, rows)],
                out_ref.at[pl.ds(to, rows)],
                sems.at[number],
            )
        )
    for copy in copies:
        copy.start()
    for copy in copies:
        copy.wait()


def place_rows(sources, cuts, total):
    wide = sources[0].shape[1]
    if any(cut[2] % 16 or cut[1] % 16 for cut in cuts):
        out = jnp.zeros((total, wide), sources[0].dtype)
        for source, start, rows, to in cuts:
            out = lax.dynamic_update_slice(out, sources[source][start : start + rows], (to, 0))
        return out
    places = jnp.stack([jnp.asarray(cut[3], jnp.int32) for cut in cuts])
    return pl.pallas_call(
        functools.partial(place_kernel, cuts=[cut[:3] for cut in cuts]),
        in_specs=[pl.BlockSpec(memory_space=pltpu.SMEM)]
        + [pl.BlockSpec(memory_space=pl.ANY)] * len(sources),
        out_specs=pl.BlockSpec(memory_space=pltpu.VMEM),
        out_shape=jax.ShapeDtypeStruct((total, wide), sources[0].dtype),
        scratch_shapes=[pltpu.SemaphoreType.DMA((len(cuts),))],
        compiler_params=pltpu.CompilerParams(vmem_limit_bytes=VMEM_LIMIT),
        cost_estimate=pl.CostEstimate(
            flops=0, bytes_accessed=4 * total * wide, transcendentals=0
        ),
    )(places, *sources)


def norm_back(upstream, unit_rows, scale_rows, gain_rows):
    scaled = upstream * gain_rows
    return scale_rows * (scaled - unit_rows * jnp.mean(scaled * unit_rows, axis=-1, keepdims=True))


def tied(value, *after):
    return lax.optimization_barrier((value, *after))[0]


class Links:
    def __init__(self, reps, group):
        self.reps, self.group, self.planes = reps, group, group // 2
        self.stages = reps.bit_length() - 1
        self.q = lax.axis_index("rep")
        self.place = lax.axis_index("shard")
        self.core = self.place % 2
        self.plane = self.place // 2

    def move(self, value, target):
        pairs = []
        for r in range(self.reps):
            for s in range(self.group):
                to_r, to_s = target(r, s)
                pairs.append((r * self.group + s, to_r * self.group + to_s))
        return lax.ppermute(value, AXES, pairs)

    def across(self, value):
        return self.move(value, lambda r, s: (r, s ^ 1))

    def along(self, value, step):
        return self.move(value, lambda r, s: (r, (s + 2 * step) % self.group))

    def bit_of(self, stage, core):
        return 1 << (stage if core == 0 else self.stages - 1 - stage)

    def swap(self, value, stage):
        return self.move(value, lambda r, s: (r ^ self.bit_of(stage, s % 2), s))

    def bit(self, stage):
        return jnp.where(self.core == 0, self.bit_of(stage, 0), self.bit_of(stage, 1))

    def gathered(self, value):
        parts, offsets = [value], [jnp.int32(0)]
        for stage in range(self.stages):
            parts += [self.swap(part, stage) for part in parts]
            offsets += [offset ^ self.bit(stage) for offset in offsets]
        return parts, [self.q ^ offset for offset in offsets]

    def slot_owners(self):
        owners = []
        for slot in range(self.reps):
            owner = self.q
            for stage in range(self.stages):
                if (slot >> (self.stages - 1 - stage)) & 1:
                    owner = owner ^ self.bit(stage)
            owners.append(owner)
        return owners

    def in_slots(self, value):
        wide = value.shape[1] // self.reps
        blocks = [value[:, k * wide : (k + 1) * wide] for k in range(self.reps)]
        return jnp.concatenate([pick(blocks, owner) for owner in self.slot_owners()], axis=1)

    def from_other_core(self, value, axis):
        blocks = jnp.split(value, self.reps, axis=axis)
        turned = []
        for slot in range(self.reps):
            other = sum(((slot >> k) & 1) << (self.stages - 1 - k) for k in range(self.stages))
            turned.append(blocks[other])
        return jnp.concatenate(turned, axis=axis)

    def scattered(self, make, axis, rows):
        low, high = self.reps // 2, self.reps
        arrived = []

        def summed(first, last):
            value = make(first, last)
            for block in arrived:
                size = value.shape[axis] // (last - first)
                value = value + lax.slice_in_dim(
                    block, first * size, last * size, axis=axis
                ).astype(jnp.float32)
            return value.astype(jnp.bfloat16)

        for stage in range(self.stages):
            arrived.append(self.swap(summed(low, high), stage))
            low, high = low // 2, low
        mine = summed(0, 1)
        total = lax.dynamic_slice_in_dim(mine, self.plane * rows, rows).astype(jnp.float32)
        for step in range(1, self.planes):
            to = (self.plane + step) % self.planes
            part = lax.dynamic_slice_in_dim(mine, to * rows, rows)
            total = total + self.along(part, step).astype(jnp.float32)
        parts, owners = self.gathered(total.astype(jnp.bfloat16))
        return in_order(parts, owners)

    def summed_everywhere(self, value):
        step = 1
        while step < self.reps:
            value = value + self.move(value, lambda r, s: (r ^ step, s))
            step *= 2
        step = 1
        while step < self.group:
            value = value + self.move(value, lambda r, s: (r, s ^ step))
            step *= 2
        return value


def pick(blocks, index):
    value = blocks[0]
    for k in range(1, len(blocks)):
        value = jnp.where(index == k, blocks[k], value)
    return value


def in_order(parts, owners):
    ordered = []
    for k in range(len(parts)):
        value = parts[0]
        for part, owner in zip(parts[1:], owners[1:]):
            value = jnp.where(owner == k, part, value)
        ordered.append(value)
    return ordered


def nn(left, right):
    return jnp.dot(left, right, preferred_element_type=jnp.float32)


def nt(left, right):
    return lax.dot_general(
        left, right, (((1,), (1,)), ((), ())), preferred_element_type=jnp.float32
    )


def tn(left, right):
    return lax.dot_general(
        left, right, (((0,), (0,)), ((), ())), preferred_element_type=jnp.float32
    )


def layer(
    reps,
    group,
    tokens,
    lengths,
    buckets,
    w_query,
    w_key,
    w_value,
    w_out,
    w_gate,
    w_up,
    w_down,
    bias_table,
    norm_attn,
    norm_ffn,
    cotangent,
):
    links = Links(reps, group)
    planes, core, plane, q = links.planes, links.core, links.plane, links.q
    first_core = core == 0
    length, width = tokens.shape
    shard_rows, inner = w_query.shape
    head_count = bias_table.shape[1]
    head_size = inner // head_count
    bucket_count = bias_table.shape[0] * group
    half = inner // 2
    piece = w_down.shape[0]
    unit = max(128, 16 * reps)
    padded = (piece + unit - 1) // unit * unit

    def by_core(zero, one):
        return jnp.where(first_core, zero, one)

    def gather_planes(share):
        return [links.along(share, step) for step in range(1, planes)]

    def gather_rows(share, own_plane, plane_rows, after=()):
        share = tied(share, *after) if after else share
        rows = share.shape[0]
        others = jnp.concatenate(gather_planes(share), axis=0)
        parts, owners = links.gathered(others)
        sources, cuts = list(parts), []
        for value, at in own_plane:
            sources.append(value)
            cuts.append((len(sources) - 1, 0, value.shape[0], plane * plane_rows + at))
        for number, owner in enumerate(owners):
            for step in range(1, planes):
                start = (plane + planes - step) % planes * plane_rows
                cuts.append((number, (step - 1) * rows, rows, start + owner * rows))
        return place_rows(sources, cuts, planes * plane_rows), others

    def gather_halved(keep, send, after=()):
        recv = links.across(tied(send, *after) if after else send)
        rows = 2 * shard_rows // reps
        per = reps // 2
        share = lax.dynamic_slice_in_dim(
            jnp.where(q // per == core, keep, recv), q % per * rows, rows
        )
        own = [(keep, core * shard_rows), (recv, (1 - core) * shard_rows)]
        return gather_rows(share, own, 2 * shard_rows, after)

    small = jnp.concatenate([norm_attn, norm_ffn, bias_table.reshape(-1)])
    small_size = small.shape[0]
    small = jnp.pad(small, (0, -small_size % 128)).reshape(1, -1)
    small = lax.all_gather(small, "shard", axis=0, tiled=True)[:, :small_size]
    gain_one = small[:, :shard_rows].reshape(1, width).astype(jnp.float32)
    gain_two = small[:, shard_rows : 2 * shard_rows].reshape(1, width).astype(jnp.float32)
    full_table = small[:, 2 * shard_rows :].reshape(bucket_count, head_count)

    def column_half(side):
        return jnp.concatenate(
            [w[:, side * half : (side + 1) * half] for w in (w_query, w_key, w_value)], axis=1
        )

    half_zero, half_one = column_half(0), column_half(1)
    qkv_half, qkv_seen = gather_halved(
        by_core(half_zero, half_one), by_core(half_one, half_zero)
    )
    qkv_other = links.across(qkv_half)

    out_share = tied(w_out, qkv_seen)
    out_mine = jnp.concatenate([out_share] + gather_planes(out_share), axis=0)
    out_theirs = links.across(out_mine)
    out_rows = w_out.shape[0]
    f_out = place_rows(
        [out_mine, out_theirs],
        [
            (
                side,
                step * out_rows,
                out_rows,
                ((plane + planes - step) % planes * 2 + (core if side == 0 else 1 - core))
                * out_rows,
            )
            for side in (0, 1)
            for step in range(planes)
        ],
        inner,
    )

    f_gate, gate_seen = gather_halved(*split_columns(core, w_gate, piece, padded), (qkv_seen,))
    f_up, up_seen = gather_halved(*split_columns(core, w_up, piece, padded), (gate_seen,))
    down_rows = jnp.pad(w_down, ((0, padded - piece), (0, 0)))
    down_share = lax.dynamic_slice_in_dim(down_rows, q * (padded // reps), padded // reps)
    f_down, down_seen = gather_rows(down_share, [(down_rows, 0)], padded, (up_seen,))

    positions = lax.broadcasted_iota(jnp.int32, (bucket_count, buckets.shape[0]), 0)
    one_hot = (buckets[None, :] == positions).astype(jnp.float32)
    rel_bias = lax.dot_general(
        full_table.astype(jnp.float32),
        one_hot,
        (((0,), (0,)), ((), ())),
        precision=lax.Precision.HIGHEST,
    )
    bias_rows = jnp.pad(rel_bias[:, ::-1], ((0, 0), (0, 1))).reshape(head_count // 2, 2, -1)

    floats_in = tokens.astype(jnp.float32)
    scale_one = lax.rsqrt(jnp.mean(floats_in * floats_in, axis=-1, keepdims=True) + EPSILON)
    normed_one = (floats_in * scale_one * gain_one).astype(jnp.bfloat16)
    own_qkv = nn(normed_one, qkv_half).astype(jnp.bfloat16)
    other_qkv = nn(normed_one, qkv_other).astype(jnp.bfloat16)
    qkv = jnp.stack([by_core(own_qkv, other_qkv), by_core(other_qkv, own_qkv)])
    context, lse = run_forward(lengths, bias_rows, qkv, head_size)
    attended = floats_in + nn(context, f_out)
    scale_two = lax.rsqrt(jnp.mean(attended * attended, axis=-1, keepdims=True) + EPSILON)
    unit_two = attended * scale_two
    normed_two = (unit_two * gain_two).astype(jnp.bfloat16)

    both = jnp.concatenate([normed_two, links.across(normed_two)], axis=0)
    both_up = jnp.concatenate([cotangent, links.across(cotangent)], axis=0)
    gate_pre = nn(both, f_gate)
    up_pre = nn(both, f_up)
    gelu_out, gelu_pull = jax.vjp(lambda v: jax.nn.gelu(v, approximate=True), gate_pre)
    hidden = (gelu_out * up_pre).astype(jnp.bfloat16)
    gate_slope = gelu_pull(up_pre)[0].astype(jnp.bfloat16)
    up_slope = gelu_out.astype(jnp.bfloat16)
    ffn_out = nn(hidden, f_down)
    ffn_theirs = links.across(ffn_out[length:].astype(jnp.bfloat16))
    output = (attended + ffn_out[:length] + ffn_theirs.astype(jnp.float32)).astype(jnp.bfloat16)

    columns = width // reps
    up_slots = links.in_slots(both_up)
    down_parts = links.scattered(
        lambda first, last: tn(hidden, up_slots[:, first * columns : last * columns]), 1, padded
    )
    grad_down = jnp.concatenate(down_parts, axis=1)[:piece].astype(jnp.float32)

    owners = links.slot_owners()
    share_rows = 2 * shard_rows // reps
    inside = jnp.arange(share_rows, dtype=jnp.int32)
    order = jnp.concatenate(
        [p * 2 * shard_rows + owner * share_rows + inside for owner in owners for p in range(planes)]
    )
    ordering = (lax.broadcasted_iota(jnp.int32, (width, width), 0) == order[None, :]).astype(
        jnp.bfloat16
    )
    slot_rows = width // reps

    def width_scattered(left, right):
        return links.scattered(
            lambda first, last: nn(left[first * slot_rows : last * slot_rows], right),
            0,
            share_rows,
        )

    def own_rows(parts):
        per = reps // 2
        low = jnp.concatenate(parts[:per], axis=0)
        high = jnp.concatenate(parts[per:], axis=0)
        return by_core(low, high), links.across(by_core(high, low))

    d_hidden = nt(both_up, f_down)
    d_gate = (d_hidden * gate_slope.astype(jnp.float32)).astype(jnp.bfloat16)
    d_up = (d_hidden * up_slope.astype(jnp.float32)).astype(jnp.bfloat16)
    both_turned = nt(ordering.T, both).astype(jnp.bfloat16)
    gate_parts = own_rows(width_scattered(both_turned, d_gate))
    up_parts = own_rows(width_scattered(both_turned, d_up))
    grad_gate = join_columns(core, *gate_parts, piece, padded)
    grad_up = join_columns(core, *up_parts, piece, padded)
    d_both = nt(d_gate, f_gate) + nt(d_up, f_up)
    d_theirs = links.across(d_both[length:].astype(jnp.bfloat16))
    d_normed_two = d_both[:length] + d_theirs.astype(jnp.float32)
    ffn_gain_term = jnp.sum(d_normed_two * unit_two, axis=0)
    grad_in = cotangent.astype(jnp.float32)
    d_attended = grad_in + norm_back(d_normed_two, unit_two, scale_two, gain_two)
    d_branch = d_attended.astype(jnp.bfloat16)

    out_term = tn(context, links.in_slots(d_branch)).astype(jnp.bfloat16)
    out_term = out_term.reshape(planes, 2, out_rows, width)
    out_keep = by_core(out_term[:, 0], out_term[:, 1]).reshape(planes * out_rows, width)
    out_send = by_core(out_term[:, 1], out_term[:, 0]).reshape(planes * out_rows, width)
    out_sum = out_keep.astype(jnp.float32) + links.across(
        links.from_other_core(out_send, 1)
    ).astype(jnp.float32)
    out_parts = links.scattered(
        lambda first, last: out_sum[:, first * columns : last * columns], 1, out_rows
    )
    grad_out = jnp.concatenate(out_parts, axis=1).astype(jnp.float32)

    d_context = nt(d_branch, f_out).astype(jnp.bfloat16)
    d_query, d_key, d_value, d_lined = run_backward(
        lengths, bias_rows, qkv, d_context, lse, head_size
    )
    d_qkv = jnp.concatenate([d_query, d_key, d_value], axis=2)
    d_own = by_core(d_qkv[0], d_qkv[1])
    d_other = by_core(d_qkv[1], d_qkv[0])
    one_turned = nt(ordering.T, normed_one).astype(jnp.bfloat16)
    qkv_theirs = links.across(
        links.from_other_core(nn(one_turned, d_other), 0).astype(jnp.bfloat16)
    )
    qkv_parts = links.scattered(
        lambda first, last: nn(one_turned[first * slot_rows : last * slot_rows], d_own)
        + qkv_theirs[first * slot_rows : last * slot_rows].astype(jnp.float32),
        0,
        share_rows,
    )
    qkv_mine, qkv_recv = own_rows(qkv_parts)
    grad_halves = (by_core(qkv_mine, qkv_recv), by_core(qkv_recv, qkv_mine))
    grad_query, grad_key, grad_value = [
        jnp.concatenate(
            [value[:, kind * half : (kind + 1) * half] for value in grad_halves], axis=1
        ).astype(jnp.float32)
        for kind in range(3)
    ]

    d_normed_one = nt(d_own, qkv_half) + nt(d_other, qkv_other)
    unit_one = floats_in * scale_one
    attn_gain_term = jnp.sum(d_normed_one * unit_one, axis=0)
    grad_tokens = (d_attended + norm_back(d_normed_one, unit_one, scale_one, gain_one)).astype(
        jnp.bfloat16
    )

    d_relative = d_lined.reshape(head_count, -1)[:, : buckets.shape[0]][:, ::-1]
    table_term = lax.dot_general(
        one_hot, d_relative, (((1,), (1,)), ((), ())), precision=lax.Precision.HIGHEST
    )
    terms = jnp.concatenate([attn_gain_term, ffn_gain_term, table_term.reshape(-1)])
    terms = jnp.pad(terms, (0, -terms.shape[0] % 1024)).reshape(-1, 128)
    terms = links.summed_everywhere(terms).reshape(-1)
    grad_norm_attn = lax.dynamic_slice_in_dim(terms, links.place * shard_rows, shard_rows)
    grad_norm_ffn = lax.dynamic_slice_in_dim(terms, width + links.place * shard_rows, shard_rows)
    table_size = bias_table.size
    grad_table = lax.dynamic_slice_in_dim(
        terms, 2 * width + links.place * table_size, table_size
    ).reshape(bias_table.shape)
    return (
        output,
        grad_tokens,
        grad_query,
        grad_key,
        grad_value,
        grad_out,
        grad_gate,
        grad_up,
        grad_down,
        grad_table,
        grad_norm_attn,
        grad_norm_ffn,
    )


def solution(mesh):
    rows, group = P("shard", None), P("shard")
    tokens = P(("rep", "shard"), None)
    return jax.shard_map(
        functools.partial(layer, mesh.shape["rep"], mesh.shape["shard"]),
        mesh=mesh,
        in_specs=(tokens, P(AXES), P()) + (rows,) * 8 + (group, group, tokens),
        out_specs=(tokens, tokens) + (rows,) * 8 + (group, group),
        check_vma=False,
    )
```

time: 1440 us -> 772 us (0.54); the launches traced: 1410 us -> 761 us
  local copies, waits for them, and re-layouts: 419 us -> 53.2 us
  waiting for transfers between devices: 682 us -> 323 us
  starting transfers between devices: 1 us -> 87.1 us
  Pallas kernels: 0 us -> 67.9 us
  blocking collectives: 59.5 us -> 12.6 us
  matrix products: 191 us -> 161 us
  between operations: 17.6 us -> 3.05 us
    reduce_scatter x7 -> x0, waiting for transfers between devices: 467 us -> none  [the longest x1 128 us: shards(): lax.psum_scatter(gate_term.astype(jnp.bfloat16), 'shard', scatter_dimensi...]
    ppermute x0 -> x86, waiting for transfers between devices: none -> 323 us  [move(): return lax.ppermute(value, AXES, pairs)]
    all_gather x7 -> x0, waiting for transfers between devices: 211 us -> none  [the longest x1 99.7 us: shards(): lax.all_gather(w_down, 'shard', axis=0, tiled=True)]
    unnamed x106 -> x167, local copies, waits for them, and re-layouts: 142 us -> 28.5 us
    rev x1 -> x0, local copies, waits for them, and re-layouts: 95.2 us -> none  [diagonal_sums(): flipped = grad_scores[:, ::-1, :]]
    ppermute x0 -> x86, starting transfers between devices: none -> 87.1 us  [move(): return lax.ppermute(value, AXES, pairs)]
    reshape x2 -> x6, local copies, waits for them, and re-layouts: 93 us -> 6.51 us  [the longest x1 1.49 us: layer(): jnp.pad(rel_bias[:, ::-1], ((0, 0), (0, 1))).reshape(head_count // 2, 2, -1)]
    pallas_call x0 -> x11, Pallas kernels: none -> 67.9 us  [the longest x5 27.1 us: place_rows(): pl.pallas_call(functools.partial(place_kernel, cuts=[cut[:3] for cut in c...]
  transfers between devices with their start and end apart: 15 -> 86, of which waited for: 9 -> 40; matrix products, arithmetic and copies ran while one was open for 39% -> 26% of each run, Pallas kernels for 0% -> 9%
where the time goes in v1:
time: 772 us; the launch traced here: 761 us
  waiting for transfers between devices  323 us (42%)
  matrix products  161 us (21%)
  starting transfers between devices  87.1 us (11%)
  Pallas kernels  67.9 us (9%)
  local copies, waits for them, and re-layouts  53.2 us (7%)
  other arithmetic  52.3 us (7%)
  blocking collectives  12.6 us (2%)
    ppermute x86, waiting for transfers between devices, move(): return lax.ppermute(value, AXES, pairs)  323 us
    ppermute x86, starting transfers between devices, move(): return lax.ppermute(value, AXES, pairs)  87.1 us
    dot_general x16, matrix products, nn(): return jnp.dot(left, right, preferred_element_type=jnp.float32)  77.4 us
    dot_general x8, matrix products, nt(): lax.dot_general(left, right, (((1,), (1,)), ((), ())), preferred_element_...  61.4 us
    unnamed x167, local copies, waits for them, and re-layouts  28.5 us
    pallas_call x5, Pallas kernels, place_rows(): pl.pallas_call(functools.partial(place_kernel, cuts=[cut[:3] for cut in c...  27.1 us
    dot_general x4, matrix products, tn(): lax.dot_general(left, right, (((0,), (0,)), ((), ())), preferred_element_...  19.3 us
    pallas_call x1, Pallas kernels, run_backward(): pl.pallas_call(functools.partial(attention_backward, head_size=head_size)...  16.7 us
  transfers between devices with their start and end apart: 86, of which 40 were waited for; matrix products, arithmetic and copies ran while one was open for 26% of the time, Pallas kernels for 9%

profile of v1, /device:TPU:10, one launch (start us, length us, event | category | flops | bytes accessed | tf_op | source)
XLA Modules:
  0.0 760.9 jit_solution(15176767521284177700)
XLA Ops:
  14.4 12.3 %collective-permute-done.2 = bf16[96,1152]{1,0:T(8,128)(2,1)S(1)} collective-permute-done((bf16[96,1152]{1,0:T(8,128)(2,1)S(1)}, bf16[96,1152]{1,0:T(8,128)(2,1)S(1)}, u32[]{:S(2)}, u32[]{:S(2)}) %collective-permute-start.2) | collective-permute-done | bytes 221216 | tf_op jit(solution)/shard_map/ppermute | solution.py:311
  29.4 12.6 %all-gather.1 = bf16[8,1,512]{2,1,0:T(2,128)(2,1)S(1)} all-gather(bf16[1,1,512]{2,1,0:T(2,128)(2,1)S(1)} %reshape.130), channel_id=2, replica_groups=mesh['rep'=4,'shard'=8] {'shard'}, dimensions={0}, use_global_device_ids=true | all-gather | bytes 9216 | tf_op jit(solution)/shard_map/all_gather | solution.py:493
  50.4 7.1 collective-permute-done.4.refs_1_
  66.5 16.8 %collective-permute-done.15 = bf16[96,2048]{1,0:T(8,128)(2,1)S(1)} collective-permute-done((bf16[96,2048]{1,0:T(8,128)(2,1)}, bf16[96,2048]{1,0:T(8,128)(2,1)S(1)}, u32[]{:S(2)}, u32[]{:S(2)}) %collective-permute-start.15) | collective-permute-done | bytes 393248 | tf_op jit(solution)/shard_map/ppermute | solution.py:311
  84.9 4.6 shard_map.229
  104.1 13.8 %collective-permute-done.9 = bf16[96,1536]{1,0:T(8,128)(2,1)S(1)} collective-permute-done((bf16[96,1536]{1,0:T(8,128)(2,1)S(1)}, bf16[96,1536]{1,0:T(8,128)(2,1)S(1)}, u32[]{:S(2)}, u32[]{:S(2)}) %collective-permute-start.9) | collective-permute-done | bytes 294944 | tf_op jit(solution)/shard_map/ppermute | solution.py:311
  121.3 16.6 %collective-permute-done.10 = bf16[96,1536]{1,0:T(8,128)(2,1)S(1)} collective-permute-done((bf16[96,1536]{1,0:T(8,128)(2,1)S(1)}, bf16[96,1536]{1,0:T(8,128)(2,1)S(1)}, u32[]{:S(2)}, u32[]{:S(2)}) %collective-permute-start.10) | collective-permute-done | bytes 294944 | tf_op jit(solution)/shard_map/ppermute | solution.py:311
  144.0 7.0 collective-permute-done.22
  161.1 4.3 reverse
  175.7 13.3 %collective-permute-done.28 = bf16[128,1536]{1,0:T(8,128)(2,1)S(1)} collective-permute-done((bf16[128,1536]{1,0:T(8,128)(2,1)}, bf16[128,1536]{1,0:T(8,128)(2,1)S(1)}, u32[]{:S(2)}, u32[]{:S(2)}) %collective-permute-start.28) | collective-permute-done | bytes 393248 | tf_op jit(solution)/shard_map/ppermute | solution.py:311
  196.4 4.3 convolution_convert_fusion.5
  204.7 10.9 %shard_map.230 = (bf16[512,768]{1,0:T(8,128)(2,1)}, f32[6,2,512]{2,1,0:T(2,128)}) custom-call(s32[1]{0:T(128)S(6)} %copy.50.valid_ref, f32[6,2,1024]{2,1,0:T(2,128)} %reshape.119.bias_ref, bf16[2,512,1152]{2,1,0:T(8,128)(2,1)} %pad_maximum_fusion.2.q_ref.k_ref.v_ref, bf16[2,512,1152]{2,1,0:T(8,128)(2,1)} %pad_maximum_fusion.2.q_ref.k_ref.v_ref, ...), custom_call_target="tpu_custom_call" | custom-call | flops 3221225472 | bytes 4718592 | tf_op jit(solution)/shard_map/pallas_call | solution.py:120
  224.5 16.6 %collective-permute-done.19.refs_3_ = bf16[288,2048]{1,0:T(8,128)(2,1)} collective-permute-done((bf16[288,2048]{1,0:T(8,128)(2,1)}, bf16[288,2048]{1,0:T(8,128)(2,1)}, u32[]{:S(2)}, u32[]{:S(2)}) %collective-permute-start.19) | collective-permute-done | bytes 1179680 | tf_op jit(solution)/shard_map/ppermute | solution.py:311
  249.8 5.6 fusion.31
  258.5 6.2 shard_map.233
  264.8 14.2 %collective-permute-done.26.refs_3_ = bf16[288,2048]{1,0:T(8,128)(2,1)} collective-permute-done((bf16[288,2048]{1,0:T(8,128)(2,1)}, bf16[288,2048]{1,0:T(8,128)(2,1)}, u32[]{:S(2)}, u32[]{:S(2)}) %collective-permute-start.26) | collective-permute-done | bytes 1179680 | tf_op jit(solution)/shard_map/ppermute | solution.py:311
  279.0 6.2 shard_map.235
  285.3 6.4 collective-permute-done.32.refs_3_
  291.6 6.3 shard_map.236
  297.9 11.7 %fusion.59 = f32[1024,2048]{1,0:T(8,128)} fusion(bf16[1536,2048]{1,0:T(8,128)(2,1)} %shard_map.235, bf16[512,1536]{1,0:T(8,128)(2,1)} %collective-permute-done.12, bf16[512,1536]{1,0:T(8,128)(2,1)} %multiply_convert_fusion.3), kind=kOutput, calls=%fused_computation.104 | convolution fusion | flops 6448742400 | bytes 17825792 | tf_op jit(solution)/shard_map/dot_general | solution.py:413
  309.6 11.7 %fusion.60 = f32[1024,2048]{1,0:T(8,128)} fusion(bf16[1536,2048]{1,0:T(8,128)(2,1)} %shard_map.233, bf16[512,1536]{1,0:T(8,128)(2,1)} %collective-permute-done.12, bf16[512,1536]{1,0:T(8,128)(2,1)} %multiply_convert_fusion.3), kind=kOutput, calls=%fused_computation.105 | convolution fusion | flops 6448742400 | bytes 17825792 | tf_op jit(solution)/shard_map/dot_general | solution.py:413
  321.4 19.1 %multiply_convert_fusion.1 = (bf16[1024,2048]{1,0:T(8,128)(2,1)}, bf16[1024,2048]{1,0:T(8,128)(2,1)}, bf16[1024,2048]{1,0:T(8,128)(2,1)}) fusion(f32[1024,2048]{1,0:T(8,128)} %fusion.60, f32[1024,2048]{1,0:T(8,128)} %fusion.59, bf16[1024,1536]{1,0:T(8,128)(2,1)S(1)} %constant_dynamic-update-slice_fusion.16, bf16[2048,1536]{1,0:T(8,128)(2,1)} %shard_map.236), kind=kOutput, calls=%fused_computation.12 | convolution fusion | flops 6505365504 | bytes 38797312 | tf_op jit(solution)/shard_map/dot_general | solution.py:417
  340.5 10.2 %fusion.134 = f32[1024,1536]{1,0:T(8,128)S(1)} fusion(bf16[1024,2048]{1,0:T(8,128)(2,1)} %get-tuple-element.51, bf16[2048,1536]{1,0:T(8,128)(2,1)} %shard_map.236), kind=kOutput, calls=%fused_computation.290 | convolution fusion | flops 6442450944 | bytes 16777216 | tf_op jit(solution)/shard_map/dot_general | solution.py:413
  351.9 10.7 %fusion.135 = f32[1024,1536]{1,0:T(8,128)} fusion(bf16[1024,2048]{1,0:T(8,128)(2,1)S(1)} %copy-done.66, bf16[1536,2048]{1,0:T(8,128)(2,1)} %shard_map.235), kind=kOutput, calls=%fused_computation.291 | convolution fusion | flops 6442450944 | bytes 16777216 | tf_op jit(solution)/shard_map/dot_general | solution.py:417
  362.6 7.2 fusion.18
  369.9 5.0 convolution_convert_fusion.2
  374.9 4.8 convolution_convert_fusion.3
  379.7 9.4 %convolution_add_fusion = f32[1024,1536]{1,0:T(8,128)S(1)} fusion(f32[1024,1536]{1,0:T(8,128)} %fusion.135, bf16[1024,2048]{1,0:T(8,128)(2,1)} %get-tuple-element.50, bf16[1536,2048]{1,0:T(8,128)(2,1)S(1)} %bitcast.110), kind=kOutput, calls=%fused_computation.27 | convolution fusion | flops 6444023808 | bytes 23068672 | tf_op jit(solution)/shard_map/dot_general | solution.py:417
  390.5 7.6 %convolution_convert_fusion.1 = bf16[2048,768]{1,0:T(8,128)(2,1)} fusion(bf16[1024,2048]{1,0:T(8,128)(2,1)} %get-tuple-element.51, bf16[1024,384]{1,0:T(8,128)(2,1)S(1)} %copy-done.24, bf16[1024,384]{1,0:T(8,128)(2,1)S(1)} %copy-done.23), kind=kOutput, calls=%fused_computation.31 | convolution fusion | flops 3225944064 | bytes 8912896 | tf_op jit(solution)/shard_map/dot_general | solution.py:423
  401.4 4.6 fusion.83
  406.0 4.8 fusion.85
  416.1 5.5 fusion.122
  424.9 16.7 %shard_map.237 = (bf16[2,512,384]{2,1,0:T(8,128)(2,1)}, bf16[2,512,384]{2,1,0:T(8,128)(2,1)}, bf16[2,512,384]{2,1,0:T(8,128)(2,1)}, f32[6,2,1024]{2,1,0:T(2,128)}) custom-call(s32[1]{0:T(128)S(6)} %copy.50.valid_ref, f32[6,2,1024]{2,1,0:T(2,128)} %reshape.119.bias_ref, bf16[2,512,1152]{2,1,0:T(8,128)(2,1)} %pad_maximum_fusion.2.q_ref.k_ref.v_ref, ...), custom_call_target="tpu_custom_call" | custom-call | flops 6442450944 | bytes 9437184 | tf_op jit(solution)/shard_map/pallas_call | solution.py:155
  446.0 4.3 reverse.1
  453.4 4.4 fusion.48
  467.2 36.2 %collective-permute-done.81 = f32[32,128]{1,0:T(8,128)S(1)} collective-permute-done((f32[32,128]{1,0:T(8,128)S(1)}, f32[32,128]{1,0:T(8,128)S(1)}, u32[]{:S(2)}, u32[]{:S(2)}) %collective-permute-start.81) | collective-permute-done | bytes 16416 | tf_op jit(solution)/shard_map/ppermute | solution.py:311
  510.3 7.9 %pad_maximum_fusion = bf16[1536,1152]{1,0:T(8,128)(2,1)} fusion(bf16[384,1152]{1,0:T(8,128)(2,1)S(1)} %get-tuple-element.54, bf16[384,1152]{1,0:T(8,128)(2,1)S(1)} %get-tuple-element.55, bf16[384,1152]{1,0:T(8,128)(2,1)S(1)} %get-tuple-element.56, bf16[384,1152]{1,0:T(8,128)(2,1)S(1)} %get-tuple-element.53), kind=kLoop, calls=%fused_computation.29 | loop fusion | flops 14155776 | bytes 7077888 | tf_op jit(solution)/shard_map/concatenate | solution.py:356
  539.7 6.0 add_convert_fusion.2
  557.9 26.0 %collective-permute-done.54 = bf16[96,384]{1,0:T(8,128)(2,1)S(1)} collective-permute-done((bf16[96,384]{1,0:T(8,128)(2,1)S(1)}, bf16[96,384]{1,0:T(8,128)(2,1)S(1)}, u32[]{:S(2)}, u32[]{:S(2)}) %collective-permute-start.54) | collective-permute-done | bytes 73760 | tf_op jit(solution)/shard_map/ppermute | solution.py:311
  598.9 17.1 %collective-permute-done.56 = bf16[384,2048]{1,0:T(8,128)(2,1)S(1)} collective-permute-done((bf16[384,2048]{1,0:T(8,128)(2,1)S(1)}, bf16[384,2048]{1,0:T(8,128)(2,1)S(1)}, u32[]{:S(2)}, u32[]{:S(2)}) %collective-permute-start.56) | collective-permute-done | bytes 1572896 | tf_op jit(solution)/shard_map/ppermute | solution.py:311
  618.2 7.2 collective-permute-done.66
  625.4 16.9 %collective-permute-done.67 = bf16[96,2048]{1,0:T(8,128)(2,1)S(1)} collective-permute-done((bf16[96,2048]{1,0:T(8,128)(2,1)S(1)}, bf16[96,2048]{1,0:T(8,128)(2,1)S(1)}, u32[]{:S(2)}, u32[]{:S(2)}) %collective-permute-start.67) | collective-permute-done | bytes 393248 | tf_op jit(solution)/shard_map/ppermute | solution.py:311
  644.6 5.3 collective-permute-start.58
  649.9 9.3 %collective-permute-done.76 = bf16[512,384]{1,0:T(8,128)(2,1)S(1)} collective-permute-done((bf16[512,384]{1,0:T(8,128)(2,1)S(1)}, bf16[512,384]{1,0:T(8,128)(2,1)S(1)}, u32[]{:S(2)}, u32[]{:S(2)}) %collective-permute-start.76) | collective-permute-done | bytes 393248 | tf_op jit(solution)/shard_map/ppermute | solution.py:311
  659.5 13.0 %collective-permute-done.77 = bf16[512,384]{1,0:T(8,128)(2,1)S(1)} collective-permute-done((bf16[512,384]{1,0:T(8,128)(2,1)S(1)}, bf16[512,384]{1,0:T(8,128)(2,1)S(1)}, u32[]{:S(2)}, u32[]{:S(2)}) %collective-permute-start.77) | collective-permute-done | bytes 393248 | tf_op jit(solution)/shard_map/ppermute | solution.py:311
  692.3 13.5 %collective-permute-done.38 = bf16[384,1152]{1,0:T(8,128)(2,1)S(1)} collective-permute-done((bf16[384,1152]{1,0:T(8,128)(2,1)S(1)}, bf16[384,1152]{1,0:T(8,128)(2,1)S(1)}, u32[]{:S(2)}, u32[]{:S(2)}) %collective-permute-start.38) | collective-permute-done | bytes 884768 | tf_op jit(solution)/shard_map/ppermute | solution.py:311
  717.2 10.4 %collective-permute-done.40 = bf16[96,1152]{1,0:T(8,128)(2,1)S(1)} collective-permute-done((bf16[96,1152]{1,0:T(8,128)(2,1)S(1)}, bf16[96,1152]{1,0:T(8,128)(2,1)S(1)}, u32[]{:S(2)}, u32[]{:S(2)}) %collective-permute-start.40) | collective-permute-done | bytes 221216 | tf_op jit(solution)/shard_map/ppermute | solution.py:311
  729.8 7.9 %collective-permute-done.61 = bf16[96,2048]{1,0:T(8,128)(2,1)S(1)} collective-permute-done((bf16[96,2048]{1,0:T(8,128)(2,1)S(1)}, bf16[96,2048]{1,0:T(8,128)(2,1)S(1)}, u32[]{:S(2)}, u32[]{:S(2)}) %collective-permute-start.61) | collective-permute-done | bytes 393248 | tf_op jit(solution)/shard_map/ppermute | solution.py:311
  (437 shorter events, 258.5 us)
Async XLA Ops:
  48.8 35.3 %collective-permute-start.5 = (bf16[288,1152]{1,0:T(8,128)(2,1)}, bf16[288,1152]{1,0:T(8,128)(2,1)S(1)}, u32[]{:S(2)}, u32[]{:S(2)}) collective-permute-start(bf16[288,1152]{1,0:T(8,128)(2,1)} %constant_dynamic-update-slice_fusion.refs_0_), channel_id=1, source_target_pairs={{0,16},{1,9},{2,18},{3,11},{4,20},{5,13},{6,22},{7,15},{8,24},{9,1... | collective-permute-start | bytes 1990664 | tf_op jit(solution)/shard_map/ppermute | solution.py:311
  57.4 26.7 %collective-permute-start.6 = (bf16[288,1152]{1,0:T(8,128)(2,1)S(1)}, bf16[288,1152]{1,0:T(8,128)(2,1)}, u32[]{:S(2)}, u32[]{:S(2)}) collective-permute-start(bf16[288,1152]{1,0:T(8,128)(2,1)S(1)} %collective-permute-done.4.refs_1_), channel_id=1, source_target_pairs={{0,16},{1,9},{2,18},{3,11},{4,20},{5,13},{6,22},{7,15},{8,24},{9,1... | collective-permute-start | bytes 1990664 | tf_op jit(solution)/shard_map/ppermute | solution.py:311
  60.0 23.4 %collective-permute-start.15 = (bf16[96,2048]{1,0:T(8,128)(2,1)}, bf16[96,2048]{1,0:T(8,128)(2,1)S(1)}, u32[]{:S(2)}, u32[]{:S(2)}) collective-permute-start(bf16[96,2048]{1,0:T(8,128)(2,1)} %dynamic-slice_select_fusion.1), channel_id=1, source_target_pairs={{0,4},{1,5},{2,6},{3,7},{4,0},{5,1},{6,2},{7,3},{8,12},{9,13},{10,... | collective-permute-start | bytes 1179656 | tf_op jit(solution)/shard_map/ppermute | solution.py:311
  64.8 24.9 %collective-permute-start.16 = (bf16[96,2048]{1,0:T(8,128)(2,1)}, bf16[96,2048]{1,0:T(8,128)(2,1)S(1)}, u32[]{:S(2)}, u32[]{:S(2)}) collective-permute-start(bf16[96,2048]{1,0:T(8,128)(2,1)} %dynamic-slice_select_fusion.1), channel_id=1, source_target_pairs={{0,6},{1,7},{2,0},{3,1},{4,2},{5,3},{6,4},{7,5},{8,14},{9,15},{10,... | collective-permute-start | bytes 1179656 | tf_op jit(solution)/shard_map/ppermute | solution.py:311
  89.5 105.9 %collective-permute-start.7 = (bf16[1536,1152]{1,0:T(8,128)(2,1)}, bf16[1536,1152]{1,0:T(8,128)(2,1)}, u32[]{:S(2)}, u32[]{:S(2)}) collective-permute-start(bf16[1536,1152]{1,0:T(8,128)(2,1)} %shard_map.229), channel_id=1, source_target_pairs={{0,1},{1,0},{2,3},{3,2},{4,5},{5,4},{6,7},{7,6},{8,9},{9,8},{10,11... | collective-permute-start | bytes 10616840 | tf_op jit(solution)/shard_map/ppermute | solution.py:311
  92.1 25.8 %collective-permute-start.9 = (bf16[96,1536]{1,0:T(8,128)(2,1)S(1)}, bf16[96,1536]{1,0:T(8,128)(2,1)S(1)}, u32[]{:S(2)}, u32[]{:S(2)}) collective-permute-start(bf16[96,1536]{1,0:T(8,128)(2,1)S(1)} %copy-done.33), channel_id=1, source_target_pairs={{0,4},{1,5},{2,6},{3,7},{4,0},{5,1},{6,2},{7,3},{8,12},{9,13},{10,... | collective-permute-start | bytes 884744 | tf_op jit(solution)/shard_map/ppermute | solution.py:311
  95.4 42.5 %collective-permute-start.10 = (bf16[96,1536]{1,0:T(8,128)(2,1)S(1)}, bf16[96,1536]{1,0:T(8,128)(2,1)S(1)}, u32[]{:S(2)}, u32[]{:S(2)}) collective-permute-start(bf16[96,1536]{1,0:T(8,128)(2,1)S(1)} %copy-done.33), channel_id=1, source_target_pairs={{0,6},{1,7},{2,0},{3,1},{4,2},{5,3},{6,4},{7,5},{8,14},{9,15},{10,... | collective-permute-start | bytes 884744 | tf_op jit(solution)/shard_map/ppermute | solution.py:311
  102.4 40.8 %collective-permute-start.21 = (bf16[96,2048]{1,0:T(8,128)(2,1)}, bf16[96,2048]{1,0:T(8,128)(2,1)S(1)}, u32[]{:S(2)}, u32[]{:S(2)}) collective-permute-start(bf16[96,2048]{1,0:T(8,128)(2,1)} %dynamic-slice_select_fusion), channel_id=1, source_target_pairs={{0,2},{1,3},{2,4},{3,5},{4,6},{5,7},{6,0},{7,1},{8,10},{9,11},{10,... | collective-permute-start | bytes 1179656 | tf_op jit(solution)/shard_map/ppermute | solution.py:311
  117.9 33.2 %collective-permute-start.22 = (bf16[96,2048]{1,0:T(8,128)(2,1)}, bf16[96,2048]{1,0:T(8,128)(2,1)S(1)}, u32[]{:S(2)}, u32[]{:S(2)}) collective-permute-start(bf16[96,2048]{1,0:T(8,128)(2,1)} %dynamic-slice_select_fusion), channel_id=1, source_target_pairs={{0,4},{1,5},{2,6},{3,7},{4,0},{5,1},{6,2},{7,3},{8,12},{9,13},{10,... | collective-permute-start | bytes 1179656 | tf_op jit(solution)/shard_map/ppermute | solution.py:311
  138.0 33.1 %collective-permute-start.11 = (bf16[384,1536]{1,0:T(8,128)(2,1)S(1)}, bf16[384,1536]{1,0:T(8,128)(2,1)}, u32[]{:S(2)}, u32[]{:S(2)}) collective-permute-start(bf16[384,1536]{1,0:T(8,128)(2,1)S(1)} %constant_dynamic-update-slice_fusion.3.refs_0_), channel_id=1, source_target_pairs={{0,1},{1,0},{2,3},{3,2},{4,5},{5,4},{6,7},{7,6},{8,9},{9,8},{10,11... | collective-permute-start | bytes 3538952 | tf_op jit(solution)/shard_map/ppermute | solution.py:311
  138.7 51.8 %collective-permute-start.17 = (bf16[288,2048]{1,0:T(8,128)(2,1)}, bf16[288,2048]{1,0:T(8,128)(2,1)}, u32[]{:S(2)}, u32[]{:S(2)}) collective-permute-start(bf16[288,2048]{1,0:T(8,128)(2,1)} %constant_dynamic-update-slice_fusion.7.refs_0_), channel_id=1, source_target_pairs={{0,8},{1,17},{2,10},{3,19},{4,12},{5,21},{6,14},{7,23},{8,0},{9,25... | collective-permute-start | bytes 3538952 | tf_op jit(solution)/shard_map/ppermute | solution.py:311
  157.8 31.2 %collective-permute-start.28 = (bf16[128,1536]{1,0:T(8,128)(2,1)}, bf16[128,1536]{1,0:T(8,128)(2,1)S(1)}, u32[]{:S(2)}, u32[]{:S(2)}) collective-permute-start(bf16[128,1536]{1,0:T(8,128)(2,1)} %constant_dynamic-slice_fusion.15), channel_id=1, source_target_pairs={{0,4},{1,5},{2,6},{3,7},{4,0},{5,1},{6,2},{7,3},{8,12},{9,13},{10,... | collective-permute-start | bytes 1179656 | tf_op jit(solution)/shard_map/ppermute | solution.py:311
  171.0 48.6 %collective-permute-start.34 = (bf16[512,1536]{1,0:T(8,128)(2,1)}, bf16[512,1536]{1,0:T(8,128)(2,1)}, u32[]{:S(2)}, u32[]{:S(2)}) collective-permute-start(bf16[512,1536]{1,0:T(8,128)(2,1)} %param.27), channel_id=1, source_target_pairs={{0,1},{1,0},{2,3},{3,2},{4,5},{5,4},{6,7},{7,6},{8,9},{9,8},{10,11... | collective-permute-start | bytes 4718600 | tf_op jit(solution)/shard_map/ppermute | solution.py:311
  189.0 33.5 %collective-permute-start.18 = (bf16[288,2048]{1,0:T(8,128)(2,1)}, bf16[288,2048]{1,0:T(8,128)(2,1)}, u32[]{:S(2)}, u32[]{:S(2)}) collective-permute-start(bf16[288,2048]{1,0:T(8,128)(2,1)} %constant_dynamic-update-slice_fusion.7.refs_0_), channel_id=1, source_target_pairs={{0,16},{1,9},{2,18},{3,11},{4,20},{5,13},{6,22},{7,15},{8,24},{9,1... | collective-permute-start | bytes 3538952 | tf_op jit(solution)/shard_map/ppermute | solution.py:311
  190.5 33.2 %collective-permute-start.24 = (bf16[288,2048]{1,0:T(8,128)(2,1)}, bf16[288,2048]{1,0:T(8,128)(2,1)}, u32[]{:S(2)}, u32[]{:S(2)}) collective-permute-start(bf16[288,2048]{1,0:T(8,128)(2,1)} %constant_dynamic-update-slice_fusion.10.refs_0_), channel_id=1, source_target_pairs={{0,8},{1,17},{2,10},{3,19},{4,12},{5,21},{6,14},{7,23},{8,0},{9,25... | collective-permute-start | bytes 3538952 | tf_op jit(solution)/shard_map/ppermute | solution.py:311
  193.8 47.3 %collective-permute-start.19 = (bf16[288,2048]{1,0:T(8,128)(2,1)}, bf16[288,2048]{1,0:T(8,128)(2,1)}, u32[]{:S(2)}, u32[]{:S(2)}) collective-permute-start(bf16[288,2048]{1,0:T(8,128)(2,1)} %collective-permute-done.17.refs_1_), channel_id=1, source_target_pairs={{0,16},{1,9},{2,18},{3,11},{4,20},{5,13},{6,22},{7,15},{8,24},{9,1... | collective-permute-start | bytes 3538952 | tf_op jit(solution)/shard_map/ppermute | solution.py:311
  195.4 49.6 %collective-permute-start.30 = (bf16[384,1536]{1,0:T(8,128)(2,1)}, bf16[384,1536]{1,0:T(8,128)(2,1)}, u32[]{:S(2)}, u32[]{:S(2)}) collective-permute-start(bf16[384,1536]{1,0:T(8,128)(2,1)} %constant_dynamic-update-slice_fusion.13.refs_0_), channel_id=1, source_target_pairs={{0,8},{1,17},{2,10},{3,19},{4,12},{5,21},{6,14},{7,23},{8,0},{9,25... | collective-permute-start | bytes 3538952 | tf_op jit(solution)/shard_map/ppermute | solution.py:311
  219.7 78.3 %collective-permute-start.12 = (bf16[512,1536]{1,0:T(8,128)(2,1)}, bf16[512,1536]{1,0:T(8,128)(2,1)}, u32[]{:S(2)}, u32[]{:S(2)}) collective-permute-start(bf16[512,1536]{1,0:T(8,128)(2,1)} %multiply_convert_fusion.3), channel_id=1, source_target_pairs={{0,1},{1,0},{2,3},{3,2},{4,5},{5,4},{6,7},{7,6},{8,9},{9,8},{10,11... | collective-permute-start | bytes 4718600 | tf_op jit(solution)/shard_map/ppermute | solution.py:311
  222.5 42.3 %collective-permute-start.25 = (bf16[288,2048]{1,0:T(8,128)(2,1)}, bf16[288,2048]{1,0:T(8,128)(2,1)}, u32[]{:S(2)}, u32[]{:S(2)}) collective-permute-start(bf16[288,2048]{1,0:T(8,128)(2,1)} %constant_dynamic-update-slice_fusion.10.refs_0_), channel_id=1, source_target_pairs={{0,16},{1,9},{2,18},{3,11},{4,20},{5,13},{6,22},{7,15},{8,24},{9,1... | collective-permute-start | bytes 3538952 | tf_op jit(solution)/shard_map/ppermute | solution.py:311
  223.7 61.5 %collective-permute-start.31 = (bf16[384,1536]{1,0:T(8,128)(2,1)}, bf16[384,1536]{1,0:T(8,128)(2,1)}, u32[]{:S(2)}, u32[]{:S(2)}) collective-permute-start(bf16[384,1536]{1,0:T(8,128)(2,1)} %constant_dynamic-update-slice_fusion.13.refs_0_), channel_id=1, source_target_pairs={{0,16},{1,9},{2,18},{3,11},{4,20},{5,13},{6,22},{7,15},{8,24},{9,1... | collective-permute-start | bytes 3538952 | tf_op jit(solution)/shard_map/ppermute | solution.py:311
  241.1 37.9 %collective-permute-start.26 = (bf16[288,2048]{1,0:T(8,128)(2,1)}, bf16[288,2048]{1,0:T(8,128)(2,1)}, u32[]{:S(2)}, u32[]{:S(2)}) collective-permute-start(bf16[288,2048]{1,0:T(8,128)(2,1)} %collective-permute-done.24.refs_1_), channel_id=1, source_target_pairs={{0,16},{1,9},{2,18},{3,11},{4,20},{5,13},{6,22},{7,15},{8,24},{9,1... | collective-permute-start | bytes 3538952 | tf_op jit(solution)/shard_map/ppermute | solution.py:311
  245.0 46.6 %collective-permute-start.32 = (bf16[384,1536]{1,0:T(8,128)(2,1)}, bf16[384,1536]{1,0:T(8,128)(2,1)}, u32[]{:S(2)}, u32[]{:S(2)}) collective-permute-start(bf16[384,1536]{1,0:T(8,128)(2,1)} %collective-permute-done.30.refs_1_), channel_id=1, source_target_pairs={{0,16},{1,9},{2,18},{3,11},{4,20},{5,13},{6,22},{7,15},{8,24},{9,1... | collective-permute-start | bytes 3538952 | tf_op jit(solution)/shard_map/ppermute | solution.py:311
  351.9 64.1 %collective-permute-start.33 = (bf16[512,1536]{1,0:T(8,128)(2,1)}, bf16[512,1536]{1,0:T(8,128)(2,1)}, u32[]{:S(2)}, u32[]{:S(2)}) collective-permute-start(bf16[512,1536]{1,0:T(8,128)(2,1)} %slice.423), channel_id=1, source_target_pairs={{0,1},{1,0},{2,3},{3,2},{4,5},{5,4},{6,7},{7,6},{8,9},{9,8},{10,11... | collective-permute-start | bytes 4718600 | tf_op jit(solution)/shard_map/ppermute | solution.py:311
  389.4 25.7 %collective-permute-start.35 = (bf16[512,1536]{1,0:T(8,128)(2,1)S(1)}, bf16[512,1536]{1,0:T(8,128)(2,1)S(1)}, u32[]{:S(2)}, u32[]{:S(2)}) collective-permute-start(bf16[512,1536]{1,0:T(8,128)(2,1)S(1)} %slice.422), channel_id=1, source_target_pairs={{0,1},{1,0},{2,3},{3,2},{4,5},{5,4},{6,7},{7,6},{8,9},{9,8},{10,11... | collective-permute-start | bytes 4718600 | tf_op jit(solution)/shard_map/ppermute | solution.py:311
  398.2 135.2 %collective-permute-start.73 = (bf16[2048,768]{1,0:T(8,128)(2,1)}, bf16[2048,768]{1,0:T(8,128)(2,1)}, u32[]{:S(2)}, u32[]{:S(2)}) collective-permute-start(bf16[2048,768]{1,0:T(8,128)(2,1)} %convolution_convert_fusion.1), channel_id=1, source_target_pairs={{0,8},{1,17},{2,10},{3,19},{4,12},{5,21},{6,14},{7,23},{8,0},{9,25... | collective-permute-start | bytes 9437192 | tf_op jit(solution)/shard_map/ppermute | solution.py:311
  399.4 148.5 %collective-permute-start.64 = (bf16[768,2048]{1,0:T(8,128)(2,1)}, bf16[768,2048]{1,0:T(8,128)(2,1)}, u32[]{:S(2)}, u32[]{:S(2)}) collective-permute-start(bf16[768,2048]{1,0:T(8,128)(2,1)} %convolution_convert_fusion.2), channel_id=1, source_target_pairs={{0,8},{1,17},{2,10},{3,19},{4,12},{5,21},{6,14},{7,23},{8,0},{9,25... | collective-permute-start | bytes 9437192 | tf_op jit(solution)/shard_map/ppermute | solution.py:311
  400.2 152.3 %collective-permute-start.55 = (bf16[768,2048]{1,0:T(8,128)(2,1)}, bf16[768,2048]{1,0:T(8,128)(2,1)}, u32[]{:S(2)}, u32[]{:S(2)}) collective-permute-start(bf16[768,2048]{1,0:T(8,128)(2,1)} %convolution_convert_fusion.3), channel_id=1, source_target_pairs={{0,8},{1,17},{2,10},{3,19},{4,12},{5,21},{6,14},{7,23},{8,0},{9,25... | collective-permute-start | bytes 9437192 | tf_op jit(solution)/shard_map/ppermute | solution.py:311
  460.6 42.8 %collective-permute-start.81 = (f32[32,128]{1,0:T(8,128)S(1)}, f32[32,128]{1,0:T(8,128)S(1)}, u32[]{:S(2)}, u32[]{:S(2)}) collective-permute-start(f32[32,128]{1,0:T(8,128)S(1)} %fusion.108), channel_id=1, source_target_pairs={{0,8},{1,9},{2,10},{3,11},{4,12},{5,13},{6,14},{7,15},{8,0},{9,1},... | collective-permute-start | bytes 49160 | tf_op jit(solution)/shard_map/ppermute | solution.py:311
  463.5 45.3 %collective-permute-start.46 = (bf16[384,1536]{1,0:T(8,128)(2,1)S(1)}, bf16[384,1536]{1,0:T(8,128)(2,1)S(1)}, u32[]{:S(2)}, u32[]{:S(2)}) collective-permute-start(bf16[384,1536]{1,0:T(8,128)(2,1)S(1)} %pad_maximum_fusion.6), channel_id=1, source_target_pairs={{0,1},{1,0},{2,3},{3,2},{4,5},{5,4},{6,7},{7,6},{8,9},{9,8},{10,11... | collective-permute-start | bytes 3538952 | tf_op jit(solution)/shard_map/ppermute | solution.py:311
  525.8 64.6 %collective-permute-start.36 = (bf16[1536,1152]{1,0:T(8,128)(2,1)}, bf16[1536,1152]{1,0:T(8,128)(2,1)}, u32[]{:S(2)}, u32[]{:S(2)}) collective-permute-start(bf16[1536,1152]{1,0:T(8,128)(2,1)} %pad_maximum_fusion), channel_id=1, source_target_pairs={{0,1},{1,0},{2,3},{3,2},{4,5},{5,4},{6,7},{7,6},{8,9},{9,8},{10,11... | collective-permute-start | bytes 10616840 | tf_op jit(solution)/shard_map/ppermute | solution.py:311
  545.8 39.8 %collective-permute-start.74 = (bf16[2048,384]{1,0:T(8,128)(2,1)S(1)}, bf16[2048,384]{1,0:T(8,128)(2,1)S(1)}, u32[]{:S(2)}, u32[]{:S(2)}) collective-permute-start(bf16[2048,384]{1,0:T(8,128)(2,1)S(1)} %add_convert_fusion.2), channel_id=1, source_target_pairs={{0,16},{1,9},{2,18},{3,11},{4,20},{5,13},{6,22},{7,15},{8,24},{9,1... | collective-permute-start | bytes 4718600 | tf_op jit(solution)/shard_map/ppermute | solution.py:311
  551.2 36.9 %collective-permute-start.65 = (bf16[384,2048]{1,0:T(8,128)(2,1)S(1)}, bf16[384,2048]{1,0:T(8,128)(2,1)S(1)}, u32[]{:S(2)}, u32[]{:S(2)}) collective-permute-start(bf16[384,2048]{1,0:T(8,128)(2,1)S(1)} %add_convert_fusion.4), channel_id=1, source_target_pairs={{0,16},{1,9},{2,18},{3,11},{4,20},{5,13},{6,22},{7,15},{8,24},{9,1... | collective-permute-start | bytes 4718600 | tf_op jit(solution)/shard_map/ppermute | solution.py:311
  552.5 31.4 %collective-permute-start.54 = (bf16[96,384]{1,0:T(8,128)(2,1)S(1)}, bf16[96,384]{1,0:T(8,128)(2,1)S(1)}, u32[]{:S(2)}, u32[]{:S(2)}) collective-permute-start(bf16[96,384]{1,0:T(8,128)(2,1)S(1)} %add_convert_fusion.13), channel_id=1, source_target_pairs={{0,16},{1,9},{2,18},{3,11},{4,20},{5,13},{6,22},{7,15},{8,24},{9,1... | collective-permute-start | bytes 221192 | tf_op jit(solution)/shard_map/ppermute | solution.py:311
  553.3 31.4 %collective-permute-start.53 = (bf16[96,384]{1,0:T(8,128)(2,1)S(1)}, bf16[96,384]{1,0:T(8,128)(2,1)S(1)}, u32[]{:S(2)}, u32[]{:S(2)}) collective-permute-start(bf16[96,384]{1,0:T(8,128)(2,1)S(1)} %collective-permute-done.52), channel_id=1, source_target_pairs={{0,16},{1,9},{2,18},{3,11},{4,20},{5,13},{6,22},{7,15},{8,24},{9,1... | collective-permute-start | bytes 221192 | tf_op jit(solution)/shard_map/ppermute | solution.py:311
  583.9 32.0 %collective-permute-start.56 = (bf16[384,2048]{1,0:T(8,128)(2,1)S(1)}, bf16[384,2048]{1,0:T(8,128)(2,1)S(1)}, u32[]{:S(2)}, u32[]{:S(2)}) collective-permute-start(bf16[384,2048]{1,0:T(8,128)(2,1)S(1)} %add_convert_fusion.6), channel_id=1, source_target_pairs={{0,16},{1,9},{2,18},{3,11},{4,20},{5,13},{6,22},{7,15},{8,24},{9,1... | collective-permute-start | bytes 4718600 | tf_op jit(solution)/shard_map/ppermute | solution.py:311
  587.8 56.7 %collective-permute-start.75 = (bf16[512,384]{1,0:T(8,128)(2,1)S(1)}, bf16[512,384]{1,0:T(8,128)(2,1)S(1)}, u32[]{:S(2)}, u32[]{:S(2)}) collective-permute-start(bf16[512,384]{1,0:T(8,128)(2,1)S(1)} %get-tuple-element.68), channel_id=1, source_target_pairs={{0,2},{1,3},{2,4},{3,5},{4,6},{5,7},{6,0},{7,1},{8,10},{9,11},{10,... | collective-permute-start | bytes 1179656 | tf_op jit(solution)/shard_map/ppermute | solution.py:311
  593.3 80.5 %collective-permute-start.37 = (bf16[768,1152]{1,0:T(8,128)(2,1)S(1)}, bf16[768,1152]{1,0:T(8,128)(2,1)S(1)}, u32[]{:S(2)}, u32[]{:S(2)}) collective-permute-start(bf16[768,1152]{1,0:T(8,128)(2,1)S(1)} %add_convert_fusion), channel_id=1, source_target_pairs={{0,8},{1,17},{2,10},{3,19},{4,12},{5,21},{6,14},{7,23},{8,0},{9,25... | collective-permute-start | bytes 5308424 | tf_op jit(solution)/shard_map/ppermute | solution.py:311
  594.6 30.8 %collective-permute-start.66 = (bf16[96,2048]{1,0:T(8,128)(2,1)S(1)}, bf16[96,2048]{1,0:T(8,128)(2,1)S(1)}, u32[]{:S(2)}, u32[]{:S(2)}) collective-permute-start(bf16[96,2048]{1,0:T(8,128)(2,1)S(1)} %get-tuple-element.77), channel_id=1, source_target_pairs={{0,2},{1,3},{2,4},{3,5},{4,6},{5,7},{6,0},{7,1},{8,10},{9,11},{10,... | collective-permute-start | bytes 1179656 | tf_op jit(solution)/shard_map/ppermute | solution.py:311
  594.7 47.5 %collective-permute-start.67 = (bf16[96,2048]{1,0:T(8,128)(2,1)S(1)}, bf16[96,2048]{1,0:T(8,128)(2,1)S(1)}, u32[]{:S(2)}, u32[]{:S(2)}) collective-permute-start(bf16[96,2048]{1,0:T(8,128)(2,1)S(1)} %get-tuple-element.79), channel_id=1, source_target_pairs={{0,4},{1,5},{2,6},{3,7},{4,0},{5,1},{6,2},{7,3},{8,12},{9,13},{10,... | collective-permute-start | bytes 1179656 | tf_op jit(solution)/shard_map/ppermute | solution.py:311
  615.9 27.1 %collective-permute-start.68 = (bf16[96,2048]{1,0:T(8,128)(2,1)S(1)}, bf16[96,2048]{1,0:T(8,128)(2,1)S(1)}, u32[]{:S(2)}, u32[]{:S(2)}) collective-permute-start(bf16[96,2048]{1,0:T(8,128)(2,1)S(1)} %get-tuple-element.78), channel_id=1, source_target_pairs={{0,6},{1,7},{2,0},{3,1},{4,2},{5,3},{6,4},{7,5},{8,14},{9,15},{10,... | collective-permute-start | bytes 1179656 | tf_op jit(solution)/shard_map/ppermute | solution.py:311
  625.4 33.7 %collective-permute-start.76 = (bf16[512,384]{1,0:T(8,128)(2,1)S(1)}, bf16[512,384]{1,0:T(8,128)(2,1)S(1)}, u32[]{:S(2)}, u32[]{:S(2)}) collective-permute-start(bf16[512,384]{1,0:T(8,128)(2,1)S(1)} %get-tuple-element.70), channel_id=1, source_target_pairs={{0,4},{1,5},{2,6},{3,7},{4,0},{5,1},{6,2},{7,3},{8,12},{9,13},{10,... | collective-permute-start | bytes 1179656 | tf_op jit(solution)/shard_map/ppermute | solution.py:311
  642.3 30.2 %collective-permute-start.77 = (bf16[512,384]{1,0:T(8,128)(2,1)S(1)}, bf16[512,384]{1,0:T(8,128)(2,1)S(1)}, u32[]{:S(2)}, u32[]{:S(2)}) collective-permute-start(bf16[512,384]{1,0:T(8,128)(2,1)S(1)} %get-tuple-element.69), channel_id=1, source_target_pairs={{0,6},{1,7},{2,0},{3,1},{4,2},{5,3},{6,4},{7,5},{8,14},{9,15},{10,... | collective-permute-start | bytes 1179656 | tf_op jit(solution)/shard_map/ppermute | solution.py:311
  643.0 37.2 %collective-permute-start.57 = (bf16[96,2048]{1,0:T(8,128)(2,1)S(1)}, bf16[96,2048]{1,0:T(8,128)(2,1)S(1)}, u32[]{:S(2)}, u32[]{:S(2)}) collective-permute-start(bf16[96,2048]{1,0:T(8,128)(2,1)S(1)} %get-tuple-element.86), channel_id=1, source_target_pairs={{0,2},{1,3},{2,4},{3,5},{4,6},{5,7},{6,0},{7,1},{8,10},{9,11},{10,... | collective-permute-start | bytes 1179656 | tf_op jit(solution)/shard_map/ppermute | solution.py:311
  644.6 41.8 %collective-permute-start.58 = (bf16[96,2048]{1,0:T(8,128)(2,1)S(1)}, bf16[96,2048]{1,0:T(8,128)(2,1)S(1)}, u32[]{:S(2)}, u32[]{:S(2)}) collective-permute-start(bf16[96,2048]{1,0:T(8,128)(2,1)S(1)} %get-tuple-element.88), channel_id=1, source_target_pairs={{0,4},{1,5},{2,6},{3,7},{4,0},{5,1},{6,2},{7,3},{8,12},{9,13},{10,... | collective-permute-start | bytes 1179656 | tf_op jit(solution)/shard_map/ppermute | solution.py:311
  659.1 30.2 %collective-permute-start.59 = (bf16[96,2048]{1,0:T(8,128)(2,1)S(1)}, bf16[96,2048]{1,0:T(8,128)(2,1)S(1)}, u32[]{:S(2)}, u32[]{:S(2)}) collective-permute-start(bf16[96,2048]{1,0:T(8,128)(2,1)S(1)} %get-tuple-element.87), channel_id=1, source_target_pairs={{0,6},{1,7},{2,0},{3,1},{4,2},{5,3},{6,4},{7,5},{8,14},{9,15},{10,... | collective-permute-start | bytes 1179656 | tf_op jit(solution)/shard_map/ppermute | solution.py:311
  680.2 30.6 %collective-permute-start.78 = (bf16[512,384]{1,0:T(8,128)(2,1)S(1)}, bf16[512,384]{1,0:T(8,128)(2,1)S(1)}, u32[]{:S(2)}, u32[]{:S(2)}) collective-permute-start(bf16[512,384]{1,0:T(8,128)(2,1)S(1)} %add_convert_fusion.9), channel_id=1, source_target_pairs={{0,8},{1,17},{2,10},{3,19},{4,12},{5,21},{6,14},{7,23},{8,0},{9,25... | collective-permute-start | bytes 1179656 | tf_op jit(solution)/shard_map/ppermute | solution.py:311
  710.8 35.8 %collective-permute-start.80 = (bf16[512,384]{1,0:T(8,128)(2,1)S(1)}, bf16[512,384]{1,0:T(8,128)(2,1)S(1)}, u32[]{:S(2)}, u32[]{:S(2)}) collective-permute-start(bf16[512,384]{1,0:T(8,128)(2,1)S(1)} %add_convert_fusion.9), channel_id=1, source_target_pairs={{0,16},{1,9},{2,18},{3,11},{4,20},{5,13},{6,22},{7,15},{8,24},{9,1... | collective-permute-start | bytes 1179656 | tf_op jit(solution)/shard_map/ppermute | solution.py:311
  715.9 30.8 %collective-permute-start.79 = (bf16[512,384]{1,0:T(8,128)(2,1)S(1)}, bf16[512,384]{1,0:T(8,128)(2,1)S(1)}, u32[]{:S(2)}, u32[]{:S(2)}) collective-permute-start(bf16[512,384]{1,0:T(8,128)(2,1)S(1)} %collective-permute-done.78), channel_id=1, source_target_pairs={{0,16},{1,9},{2,18},{3,11},{4,20},{5,13},{6,22},{7,15},{8,24},{9,1... | collective-permute-start | bytes 1179656 | tf_op jit(solution)/shard_map/ppermute | solution.py:311
  (112 other events, 1912.2 us)

commit v2 on v1

v2 whole, which is shorter than its diff:
```python
import functools

import jax
import jax.numpy as jnp
from jax import lax
from jax.experimental import pallas as pl
from jax.experimental.pallas import tpu as pltpu
from jax.sharding import PartitionSpec as P

NEG_FILL = -1000000000.0
VMEM_LIMIT = 56 * 1024 * 1024
TOEP = 128
COST_SHARE = 0.25


def cost(flops):
    flops = int(flops * COST_SHARE)
    return pl.CostEstimate(flops=flops, bytes_accessed=flops // 512, transcendentals=0)


def dot_nn(a, b):
    return lax.dot_general(a, b, (((1,), (0,)), ((), ())), preferred_element_type=jnp.float32)


def dot_nt(a, b):
    return lax.dot_general(a, b, (((1,), (1,)), ((), ())), preferred_element_type=jnp.float32)


def dot_tn(a, b):
    return lax.dot_general(a, b, (((0,), (0,)), ((), ())), preferred_element_type=jnp.float32)


def biased_scores(rows_k, rows_q, bias_row, valid, length):
    steps = length // TOEP
    raw = dot_nt(rows_k, rows_q)
    width = bias_row.shape[-1]
    spread = jnp.broadcast_to(bias_row, (TOEP, width))
    table = pltpu.roll(spread, width - (TOEP - 1), 1, stride=1, stride_axis=0)
    blocks = []
    for step in range(steps):
        start = TOEP * (steps - 1 - step)
        row_at = lax.broadcasted_iota(jnp.int32, (TOEP, length), 0) + step * TOEP
        mask = jnp.where(row_at < valid, 0.0, NEG_FILL)
        blocks.append(
            raw[step * TOEP : (step + 1) * TOEP] + table[:, start : start + length] + mask
        )
    return jnp.concatenate(blocks, axis=0)


def attention_forward(valid_ref, bias_ref, q_ref, k_ref, v_ref, ctx_ref, turned_ref, lse_ref, *, head_size):
    length = q_ref.shape[1]
    pair = q_ref.shape[2] // head_size
    q, k, v = q_ref[0], k_ref[0], v_ref[0]
    lane_head = lax.broadcasted_iota(jnp.int32, q.shape, 1) // head_size
    v_turned = v.T
    outs = []
    for head in range(pair):
        own_q = jnp.where(lane_head == head, q, jnp.zeros_like(q))
        scores = biased_scores(k, own_q, bias_ref[0, head : head + 1], valid_ref[0], length)
        top = jnp.max(scores, axis=0, keepdims=True)
        terms = jnp.exp(scores - top)
        total = jnp.sum(terms, axis=0, keepdims=True)
        probs = (terms * (1.0 / total)).astype(jnp.bfloat16)
        lse_ref[0, head : head + 1] = top + jnp.log(total)
        outs.append(dot_nn(v_turned, probs)[head * head_size : (head + 1) * head_size])
    turned = jnp.concatenate(outs, axis=0)
    turned_ref[...] = turned.astype(jnp.bfloat16)
    ctx_ref[...] = turned.T.astype(jnp.bfloat16)


def attention_backward(
    valid_ref, bias_ref, q_ref, k_ref, v_ref, dctx_ref, lse_ref, dq_ref, dk_ref, dv_ref, rel_ref, *, head_size
):
    length = q_ref.shape[1]
    pair = q_ref.shape[2] // head_size
    steps = length // TOEP
    q, k, v, dctx = q_ref[0], k_ref[0], v_ref[0], dctx_ref[...]
    lane_head = lax.broadcasted_iota(jnp.int32, q.shape, 1) // head_size
    k_turned = k.T
    width = bias_ref.shape[-1]
    flip = (
        lax.broadcasted_iota(jnp.int32, (TOEP, TOEP), 0)
        + lax.broadcasted_iota(jnp.int32, (TOEP, TOEP), 1)
        == TOEP - 1
    ).astype(jnp.bfloat16)
    dq_parts = []
    dk = dv = None
    for head in range(pair):
        mine = lane_head == head
        own_q = jnp.where(mine, q, jnp.zeros_like(q))
        own_d = jnp.where(mine, dctx, jnp.zeros_like(dctx))
        scores = biased_scores(k, own_q, bias_ref[0, head : head + 1], valid_ref[0], length)
        probs = jnp.exp(scores - lse_ref[0, head : head + 1])
        d_probs = dot_nt(v, own_d)
        inner = jnp.sum(d_probs * probs, axis=0, keepdims=True)
        d_scores = (probs * (d_probs - inner)).astype(jnp.bfloat16)
        part_v = dot_nn(probs.astype(jnp.bfloat16), own_d)
        part_k = dot_nn(d_scores, own_q)
        dv = part_v if dv is None else dv + part_v
        dk = part_k if dk is None else dk + part_k
        dq_parts.append(dot_nn(k_turned, d_scores)[head * head_size : (head + 1) * head_size])
        fold = None
        for step in range(steps):
            start = TOEP * (steps - 1 - step)
            turned = dot_nn(flip, d_scores[step * TOEP : (step + 1) * TOEP])
            pieces = []
            if start:
                pieces.append(jnp.zeros((TOEP, start), jnp.float32))
            pieces.append(turned)
            if width - start - length:
                pieces.append(jnp.zeros((TOEP, width - start - length), jnp.float32))
            padded = jnp.concatenate(pieces, axis=1)
            fold = padded if fold is None else fold + padded
        lined = pltpu.roll(fold, 0, 1, stride=1, stride_axis=0)
        rel_ref[0, head : head + 1] = jnp.sum(lined, axis=0, keepdims=True)
    dq_ref[0] = jnp.concatenate(dq_parts, axis=0).T.astype(jnp.bfloat16)
    dk_ref[0] = dk.astype(jnp.bfloat16)
    dv_ref[0] = dv.astype(jnp.bfloat16)


def run_forward(valid, bias_rows, qkv, head_size):
    halves, length, wide = qkv.shape
    half = wide // 3
    per = half // 128
    pairs = halves * per
    width = bias_rows.shape[-1]
    spec = lambda kind: pl.BlockSpec((1, length, 128), lambda p: (p // per, 0, kind * per + p % per))
    return pl.pallas_call(
        functools.partial(attention_forward, head_size=head_size),
        grid=(pairs,),
        in_specs=[
            pl.BlockSpec(memory_space=pltpu.SMEM),
            pl.BlockSpec((1, 2, width), lambda p: (p, 0, 0)),
            spec(0), spec(1), spec(2),
        ],
        out_specs=[
            pl.BlockSpec((length, 128), lambda p: (0, p)),
            pl.BlockSpec((128, length), lambda p: (p, 0)),
            pl.BlockSpec((1, 2, length), lambda p: (p, 0, 0)),
        ],
        out_shape=[
            jax.ShapeDtypeStruct((length, halves * half), jnp.bfloat16),
            jax.ShapeDtypeStruct((halves * half, length), jnp.bfloat16),
            jax.ShapeDtypeStruct((pairs, 2, length), jnp.float32),
        ],
        compiler_params=pltpu.CompilerParams(vmem_limit_bytes=VMEM_LIMIT),
        name="attend",
        cost_estimate=cost(8 * pairs * 2 * length * length * 128),
    )(valid, bias_rows, qkv, qkv, qkv)


def run_backward(valid, bias_rows, qkv, d_context, lse, head_size):
    halves, length, wide = qkv.shape
    half = wide // 3
    per = half // 128
    pairs = halves * per
    width = bias_rows.shape[-1]
    spec = lambda kind: pl.BlockSpec((1, length, 128), lambda p: (p // per, 0, kind * per + p % per))
    out_spec = pl.BlockSpec((1, length, 128), lambda p: (p // per, 0, p % per))
    grad = jax.ShapeDtypeStruct((halves, length, half), jnp.bfloat16)
    row = pl.BlockSpec((1, 2, width), lambda p: (p, 0, 0))
    return pl.pallas_call(
        functools.partial(attention_backward, head_size=head_size),
        grid=(pairs,),
        in_specs=[
            pl.BlockSpec(memory_space=pltpu.SMEM),
            row,
            spec(0), spec(1), spec(2),
            pl.BlockSpec((length, 128), lambda p: (0, p)),
            pl.BlockSpec((1, 2, length), lambda p: (p, 0, 0)),
        ],
        out_specs=[out_spec, out_spec, out_spec, row],
        out_shape=[grad, grad, grad, jax.ShapeDtypeStruct((pairs, 2, width), jnp.float32)],
        compiler_params=pltpu.CompilerParams(vmem_limit_bytes=VMEM_LIMIT),
        name="attend_back",
        cost_estimate=cost(16 * pairs * 2 * length * length * 128),
    )(valid, bias_rows, qkv, qkv, qkv, d_context, lse)


EPSILON = 1e-06
AXES = ("team", "wing", "plane", "core")


def split_kernel(at_ref, gate_ref, up_ref, keep_ref, send_ref, *, cuts, piece, padded):
    rows = gate_ref.shape[0]
    first_wing, first_core = at_ref[0] == 0, at_ref[1] == 0
    filler = jnp.zeros((rows, padded - piece), jnp.float32)
    for number, ref in enumerate((gate_ref, up_ref)):
        w = ref[...].astype(jnp.float32)
        for cut in range(cuts):
            sides = []
            for side in (0, 1):
                zero, one = [
                    w[:, (4 * cut + 2 * side + wing) * piece :][:, :piece] for wing in (0, 1)
                ]
                chosen = jnp.where(first_wing, zero, one)
                sides.append(jnp.concatenate([chosen, filler], axis=1).astype(jnp.bfloat16))
            start = (number * cuts + cut) * padded
            to = slice(start, start + padded)
            keep_ref[:, to] = jnp.where(first_core, sides[0], sides[1])
            send_ref[:, to] = jnp.where(first_core, sides[1], sides[0])


def split_columns(at, w_gate, w_up, piece, padded):
    rows, wide = w_gate.shape
    cuts = wide // (4 * piece)
    out = jax.ShapeDtypeStruct((rows, 2 * cuts * padded), jnp.bfloat16)
    whole = pl.BlockSpec(memory_space=pltpu.VMEM)
    return pl.pallas_call(
        functools.partial(split_kernel, cuts=cuts, piece=piece, padded=padded),
        in_specs=[pl.BlockSpec(memory_space=pltpu.SMEM), whole, whole],
        out_specs=[whole, whole],
        out_shape=[out, out],
        compiler_params=pltpu.CompilerParams(vmem_limit_bytes=VMEM_LIMIT),
        name="split",
        cost_estimate=cost(512 * w_gate.size),
    )(at, w_gate, w_up)


def join_kernel(core_ref, mine_ref, other_ref, gate_ref, up_ref, *, cuts, piece, padded):
    rows = gate_ref.shape[0]
    first_core = core_ref[0] == 0
    for number, out_ref in enumerate((gate_ref, up_ref)):
        for cut in range(cuts):
            start = (number * cuts + cut) * padded
            at = slice(start, start + padded)
            for wing in (0, 1):
                of = slice(wing * rows, (wing + 1) * rows)
                mine, other = mine_ref[of, at], other_ref[of, at]
                for side in (0, 1):
                    value = jnp.where(first_core, *((mine, other) if side == 0 else (other, mine)))
                    to = (4 * cut + 2 * side + wing) * piece
                    out_ref[:, to : to + piece] = value.astype(jnp.float32)[:, :piece]


def join_columns(core, mine, other, piece, padded):
    rows = mine.shape[0] // 2
    cuts = mine.shape[1] // (2 * padded)
    out = jax.ShapeDtypeStruct((rows, 4 * cuts * piece), jnp.float32)
    whole = pl.BlockSpec(memory_space=pltpu.VMEM)
    return pl.pallas_call(
        functools.partial(join_kernel, cuts=cuts, piece=piece, padded=padded),
        in_specs=[pl.BlockSpec(memory_space=pltpu.SMEM), whole, whole],
        out_specs=[whole, whole],
        out_shape=[out, out],
        compiler_params=pltpu.CompilerParams(vmem_limit_bytes=VMEM_LIMIT),
        name="join",
        cost_estimate=cost(512 * mine.size),
    )(core[None], mine, other)


def turn_kernel(owners_ref, x_ref, out_ref, turned_ref, *, slots, rows):
    turned_ref[...] = x_ref[...].T
    for slot in range(slots):
        start = pl.multiple_of(owners_ref[slot] * rows, 16)
        out_ref[slot, 0] = turned_ref[pl.ds(start, rows)]


def turn(x, owners, planes):
    tokens, width = x.shape
    slots = len(owners)
    plane = width // planes
    rows = plane // slots
    if plane % 128 or rows % 16:
        blocks = x.T.reshape(planes, slots, rows, tokens)
        picked = [lax.dynamic_slice_in_dim(blocks, owner, 1, axis=1) for owner in owners]
        return jnp.concatenate(picked, axis=1).transpose(1, 0, 2, 3).reshape(width, tokens)
    return pl.pallas_call(
        functools.partial(turn_kernel, slots=slots, rows=rows),
        grid=(planes,),
        in_specs=[
            pl.BlockSpec(memory_space=pltpu.SMEM),
            pl.BlockSpec((tokens, plane), lambda p: (0, p)),
        ],
        out_specs=pl.BlockSpec((slots, 1, rows, tokens), lambda p: (0, p, 0, 0)),
        out_shape=jax.ShapeDtypeStruct((slots, planes, rows, tokens), x.dtype),
        scratch_shapes=[pltpu.VMEM((plane, tokens), x.dtype)],
        compiler_params=pltpu.CompilerParams(vmem_limit_bytes=VMEM_LIMIT),
        name="turn",
        cost_estimate=cost(512 * x.size),
    )(jnp.stack(owners), x).reshape(width, tokens)


def turn_team_kernel(*refs):
    out_ref = refs[-1]
    for number, ref in enumerate(refs[:-1]):
        rows = ref.shape[0]
        out_ref[:, number * rows : (number + 1) * rows] = ref[...].T


def turn_team(blocks):
    rows, width = blocks[0].shape
    tile = tile_of(width, 256)
    tokens = rows * len(blocks)
    return pl.pallas_call(
        turn_team_kernel,
        grid=(width // tile,),
        in_specs=[pl.BlockSpec((rows, tile), lambda j: (0, j))] * len(blocks),
        out_specs=pl.BlockSpec((tile, tokens), lambda j: (j, 0)),
        out_shape=jax.ShapeDtypeStruct((width, tokens), blocks[0].dtype),
        compiler_params=pltpu.CompilerParams(vmem_limit_bytes=VMEM_LIMIT),
        name="turn_team",
        cost_estimate=cost(512 * tokens * width),
    )(*blocks)


def place_kernel(at_ref, *refs, cuts, outs):
    sources, out_refs, sems = refs[: -1 - outs], refs[-1 - outs : -1], refs[-1]
    copies = []
    for number, (source, start, rows, of, column, wide) in enumerate(cuts):
        row_to = pl.multiple_of(at_ref[0, number], 16)
        column_to = pl.multiple_of(at_ref[1, number], 128)
        copies.append(
            pltpu.make_async_copy(
                sources[source].at[pl.ds(start, rows), pl.ds(column, wide)],
                out_refs[of].at[pl.ds(row_to, rows), pl.ds(column_to, wide)],
                sems.at[number],
            )
        )
    for copy in copies:
        copy.start()
    for copy in copies:
        copy.wait()


def place(sources, cuts, shapes):
    low = sources[0].dtype
    if any(cut[1] % 16 or cut[2] % 16 or cut[4] % 128 or cut[5] % 128 for cut in cuts):
        outs = [jnp.zeros(shape, low) for shape in shapes]
        for source, start, rows, of, column, wide, row_to, column_to in cuts:
            part = sources[source][start : start + rows, column : column + wide]
            outs[of] = lax.dynamic_update_slice(outs[of], part, (row_to, column_to))
        return outs
    places = jnp.stack(
        [jnp.stack([jnp.asarray(cut[k], jnp.int32) for cut in cuts]) for k in (6, 7)]
    )
    return pl.pallas_call(
        functools.partial(place_kernel, cuts=[cut[:6] for cut in cuts], outs=len(shapes)),
        in_specs=[pl.BlockSpec(memory_space=pltpu.SMEM)]
        + [pl.BlockSpec(memory_space=pl.ANY)] * len(sources),
        out_specs=[pl.BlockSpec(memory_space=pltpu.VMEM)] * len(shapes),
        out_shape=[jax.ShapeDtypeStruct(shape, low) for shape in shapes],
        scratch_shapes=[pltpu.SemaphoreType.DMA((len(cuts),))],
        compiler_params=pltpu.CompilerParams(vmem_limit_bytes=VMEM_LIMIT),
        name="place",
        cost_estimate=cost(512 * sum(a * b for a, b in shapes)),
    )(places, *sources)


def tile_of(size, most):
    for count in range(1, size // 128 + 1):
        if size % count == 0 and size // count % 128 == 0 and size // count <= most:
            return size // count
    return size


def product_kernel(*refs, pairs, across, kind):
    total = None
    for number in range(pairs):
        left, right = refs[2 * number][...], refs[2 * number + 1][...]
        term = dot_nt(left, right) if across else dot_nn(left, right)
        total = term if total is None else total + term
    outs = refs[2 * pairs :]
    if kind == "team":
        rows = outs[0].shape[0]
        outs[0][...] = total[:rows]
        outs[1][...] = total[rows : 2 * rows]
        outs[2][...] = total[2 * rows :].astype(jnp.bfloat16)
    else:
        outs[0][...] = total.astype(outs[0].dtype)


def product(lefts, rights, across=False, kind="low", most=256):
    rows = lefts[0].shape[0]
    wide = rights[0].shape[0 if across else 1]
    tile = tile_of(wide, most)
    operands, specs = [], []
    for left, right in zip(lefts, rights):
        depth = left.shape[1]
        operands += [left, right]
        specs.append(pl.BlockSpec((rows, depth), lambda j: (0, 0)))
        if across:
            specs.append(pl.BlockSpec((tile, depth), lambda j: (j, 0)))
        else:
            specs.append(pl.BlockSpec((depth, tile), lambda j: (0, j)))
    if kind == "team":
        shapes = [(rows // 4, jnp.float32), (rows // 4, jnp.float32), (rows // 2, jnp.bfloat16)]
    else:
        shapes = [(rows, jnp.bfloat16 if kind == "low" else jnp.float32)]
    outs = pl.pallas_call(
        functools.partial(product_kernel, pairs=len(lefts), across=across, kind=kind),
        grid=(wide // tile,),
        in_specs=specs,
        out_specs=[pl.BlockSpec((size, tile), lambda j: (0, j)) for size, _ in shapes],
        out_shape=[jax.ShapeDtypeStruct((size, wide), kept) for size, kept in shapes],
        compiler_params=pltpu.CompilerParams(vmem_limit_bytes=VMEM_LIMIT),
        name="product",
        cost_estimate=cost(2 * rows * depth * wide * len(lefts)),
    )(*operands)
    return outs if kind == "team" else outs[0]


def column_slot_kernel(at_ref, left_ref, *refs, count, added):
    left = left_ref[...]
    depth = left.shape[1] // count
    total = None
    for number in range(count):
        term = dot_nn(left[:, number * depth : (number + 1) * depth], refs[number][...])
        total = term if total is None else total + term
    for ref in refs[count : count + added]:
        total = total + ref[...].astype(jnp.float32)
    refs[-1][...] = total.astype(jnp.bfloat16)


def column_slots(left, blocks, owners, wide, added=()):
    rows = left.shape[0]
    if wide % 128:
        whole = jnp.concatenate(blocks, axis=0)
        value = jnp.concatenate(
            [nn(left, lax.dynamic_slice_in_dim(whole, owner * wide, wide, axis=1)) for owner in owners],
            axis=1,
        )
        for array, first in added:
            value = value + array[:, first * wide : (first + len(owners)) * wide].astype(jnp.float32)
        return value.astype(jnp.bfloat16)
    tile = tile_of(wide, 256)
    per = wide // tile
    return pl.pallas_call(
        functools.partial(column_slot_kernel, count=len(blocks), added=len(added)),
        grid_spec=pltpu.PrefetchScalarGridSpec(
            num_scalar_prefetch=1,
            grid=(len(owners) * per,),
            in_specs=[pl.BlockSpec(left.shape, lambda j, at: (0, 0))]
            + [
                pl.BlockSpec((block.shape[0], tile), lambda j, at: (0, at[j // per] * per + j % per))
                for block in blocks
            ]
            + [
                pl.BlockSpec((rows, tile), lambda j, at, first=first: (0, first * per + j))
                for _, first in added
            ],
            out_specs=pl.BlockSpec((rows, tile), lambda j, at: (0, j)),
        ),
        out_shape=jax.ShapeDtypeStruct((rows, len(owners) * wide), jnp.bfloat16),
        compiler_params=pltpu.CompilerParams(vmem_limit_bytes=VMEM_LIMIT),
        name="column_slots",
        cost_estimate=cost(2 * left.size * wide * len(owners)),
    )(jnp.stack(owners), left, *blocks, *[array for array, _ in added])


def packed_slot_kernel(row_ref, at_ref, turned_ref, grad_ref, context_ref, branch_ref, *refs):
    out_ref = refs[-1]
    first = dot_nn(turned_ref[...], grad_ref[...])
    second = dot_nn(context_ref[...], branch_ref[...])
    wide = first.shape[1]
    for ref in refs[:-1]:
        first = first + ref[:, :wide].astype(jnp.float32)
        second = second + ref[:, wide:].astype(jnp.float32)
    out_ref[:, :wide] = first.astype(jnp.bfloat16)
    out_ref[:, wide:] = second.astype(jnp.bfloat16)


def packed_slots(turned, grad, context, branch, slots, owners, reps, planes, added=()):
    rows = turned.shape[0] // reps
    columns = branch.shape[1] // reps
    fold = context.shape[0] // rows
    wide = grad.shape[1] + fold * columns
    if fold != 1 or columns % 128:
        outs = []
        for slot, owner in zip(slots, owners):
            first = nn(turned[slot * rows : (slot + 1) * rows], grad)
            second = nn(context, lax.dynamic_slice_in_dim(branch, owner * columns, columns, axis=1))
            outs.append(jnp.concatenate([first, folded(second, planes, fold)], axis=1))
        value = jnp.concatenate(outs, axis=0)
        for array, start in added:
            value = value + array[start * rows :][: value.shape[0]].astype(jnp.float32)
        return value.astype(jnp.bfloat16)
    block = lambda start: pl.BlockSpec((rows, wide), lambda i, row, at: (start + i, 0))
    return pl.pallas_call(
        packed_slot_kernel,
        grid_spec=pltpu.PrefetchScalarGridSpec(
            num_scalar_prefetch=2,
            grid=(len(slots),),
            in_specs=[
                pl.BlockSpec((rows, turned.shape[1]), lambda i, row, at: (row[i], 0)),
                pl.BlockSpec(grad.shape, lambda i, row, at: (0, 0)),
                pl.BlockSpec(context.shape, lambda i, row, at: (0, 0)),
                pl.BlockSpec((branch.shape[0], columns), lambda i, row, at: (0, at[i])),
            ]
            + [block(start) for _, start in added],
            out_specs=block(0),
        ),
        out_shape=jax.ShapeDtypeStruct((len(slots) * rows, wide), jnp.bfloat16),
        compiler_params=pltpu.CompilerParams(vmem_limit_bytes=VMEM_LIMIT),
        name="packed_slots",
        cost_estimate=cost(2 * len(slots) * rows * turned.shape[1] * wide),
    )(
        jnp.array(slots, jnp.int32),
        jnp.stack(owners),
        turned,
        grad,
        context,
        branch,
        *[array for array, _ in added],
    )


def folded(value, planes, fold):
    rows, wide = value.shape
    split = value.reshape(planes, fold, rows // (planes * fold), wide)
    return split.transpose(0, 2, 1, 3).reshape(rows // fold, fold * wide)


def unfolded(value, fold):
    rows, wide = value.shape
    return value.reshape(rows, fold, wide // fold).transpose(1, 0, 2).reshape(rows * fold, -1)


GELU_RATE = 0.7978845608028654
GELU_CUBE = 0.044715


def gated_kernel(*refs, count):
    gate_ref, up_ref, hidden_ref, turned_ref, gate_slope_ref, up_slope_ref = refs[count:]
    for number in range(count):
        x = refs[number][...]
        rows = x.shape[0]
        at = slice(number * rows, (number + 1) * rows)
        gate = dot_nn(x, gate_ref[...])
        up = dot_nn(x, up_ref[...])
        square = gate * gate
        bent = jnp.tanh(GELU_RATE * gate * (1.0 + GELU_CUBE * square))
        share = 0.5 * (1.0 + bent)
        gelu = gate * share
        slope = share + 0.5 * gate * (1.0 - bent * bent) * (
            GELU_RATE * (1.0 + 3.0 * GELU_CUBE * square)
        )
        hidden = (gelu * up).astype(jnp.bfloat16)
        hidden_ref[at] = hidden
        turned_ref[:, at] = hidden.T
        gate_slope_ref[at] = (slope * up).astype(jnp.bfloat16)
        up_slope_ref[at] = gelu.astype(jnp.bfloat16)


def gated(blocks, f_both):
    rows, depth = blocks[0].shape
    tokens = rows * len(blocks)
    wide = f_both.shape[1] // 2
    tile = tile_of(wide, 256)
    steps = wide // tile
    out = pl.BlockSpec((tokens, tile), lambda j: (0, j))
    kept = jax.ShapeDtypeStruct((tokens, wide), jnp.bfloat16)
    return pl.pallas_call(
        functools.partial(gated_kernel, count=len(blocks)),
        grid=(steps,),
        in_specs=[pl.BlockSpec((rows, depth), lambda j: (0, 0))] * len(blocks)
        + [
            pl.BlockSpec((depth, tile), lambda j: (0, j)),
            pl.BlockSpec((depth, tile), lambda j: (0, steps + j)),
        ],
        out_specs=[out, pl.BlockSpec((tile, tokens), lambda j: (j, 0)), out, out],
        out_shape=[kept, jax.ShapeDtypeStruct((wide, tokens), jnp.bfloat16), kept, kept],
        compiler_params=pltpu.CompilerParams(vmem_limit_bytes=VMEM_LIMIT),
        name="gated",
        cost_estimate=cost(4 * tokens * depth * wide),
    )(*blocks, f_both, f_both)


def gated_back_kernel(*refs, count):
    down_ref, gate_slope_ref, up_slope_ref, out_ref = refs[count:]
    for number in range(count):
        rows = refs[number].shape[0]
        at = slice(number * rows, (number + 1) * rows)
        d_hidden = dot_nt(refs[number][...], down_ref[...])
        out_ref[0, at] = (d_hidden * gate_slope_ref[at].astype(jnp.float32)).astype(jnp.bfloat16)
        out_ref[1, at] = (d_hidden * up_slope_ref[at].astype(jnp.float32)).astype(jnp.bfloat16)


def gated_back(blocks, f_down, gate_slope, up_slope):
    rows, depth = blocks[0].shape
    tokens = rows * len(blocks)
    wide = f_down.shape[0]
    tile = tile_of(wide, 256)
    column = pl.BlockSpec((tokens, tile), lambda j: (0, j))
    return pl.pallas_call(
        functools.partial(gated_back_kernel, count=len(blocks)),
        grid=(wide // tile,),
        in_specs=[pl.BlockSpec((rows, depth), lambda j: (0, 0))] * len(blocks)
        + [pl.BlockSpec((tile, depth), lambda j: (j, 0)), column, column],
        out_specs=pl.BlockSpec((2, tokens, tile), lambda j: (0, 0, j)),
        out_shape=jax.ShapeDtypeStruct((2, tokens, wide), jnp.bfloat16),
        compiler_params=pltpu.CompilerParams(vmem_limit_bytes=VMEM_LIMIT),
        name="gated_back",
        cost_estimate=cost(2 * tokens * depth * wide),
    )(*blocks, f_down, gate_slope, up_slope)


def pair_grad_kernel(left_ref, right_ref, out_ref):
    out_ref[...] = dot_nn(left_ref[...], right_ref[0]).astype(jnp.bfloat16)


def pair_grad(left, pair):
    rows, depth = left.shape
    wide = pair.shape[2]
    tile = tile_of(wide, 256)
    steps = wide // tile
    return pl.pallas_call(
        pair_grad_kernel,
        grid=(2 * steps,),
        in_specs=[
            pl.BlockSpec((rows, depth), lambda j: (0, 0)),
            pl.BlockSpec((1, depth, tile), lambda j: (j // steps, 0, j % steps)),
        ],
        out_specs=pl.BlockSpec((rows, tile), lambda j: (0, j)),
        out_shape=jax.ShapeDtypeStruct((rows, 2 * wide), jnp.bfloat16),
        compiler_params=pltpu.CompilerParams(vmem_limit_bytes=VMEM_LIMIT),
        name="pair_grad",
        cost_estimate=cost(4 * rows * depth * wide),
    )(left, pair)


def pair_back_kernel(pair_ref, right_ref, own_ref, side_ref, sent_ref):
    wide = pair_ref.shape[2]
    rows = own_ref.shape[0]
    right = right_ref[...]
    total = dot_nt(pair_ref[0], right[:, :wide]) + dot_nt(pair_ref[1], right[:, wide:])
    own_ref[...] = total[:rows]
    side_ref[...] = total[rows : 2 * rows]
    sent_ref[...] = total[2 * rows :].astype(jnp.bfloat16)


def pair_back(pair, f_both):
    tokens, wide = pair.shape[1:]
    width = f_both.shape[0]
    tile = tile_of(width, 256)
    shapes = [(tokens // 4, jnp.float32), (tokens // 4, jnp.float32), (tokens // 2, jnp.bfloat16)]
    return pl.pallas_call(
        pair_back_kernel,
        grid=(width // tile,),
        in_specs=[
            pl.BlockSpec(pair.shape, lambda j: (0, 0, 0), pipeline_mode=pl.Buffered(1)),
            pl.BlockSpec((tile, 2 * wide), lambda j: (j, 0)),
        ],
        out_specs=[pl.BlockSpec((size, tile), lambda j: (0, j)) for size, _ in shapes],
        out_shape=[jax.ShapeDtypeStruct((size, width), kept) for size, kept in shapes],
        compiler_params=pltpu.CompilerParams(vmem_limit_bytes=VMEM_LIMIT),
        name="pair_back",
        cost_estimate=cost(4 * tokens * wide * width),
    )(pair, f_both)


def norm_back(upstream, unit_rows, scale_rows, gain_rows):
    scaled = upstream * gain_rows
    return scale_rows * (scaled - unit_rows * jnp.mean(scaled * unit_rows, axis=-1, keepdims=True))


def tied(value, *after):
    return lax.optimization_barrier((value, *after))[0]


class Order:
    def __init__(self):
        self.last = ()

    def __call__(self, value, *after):
        return tied(value, *self.last, *after) if self.last or after else value

    def mark(self, value):
        self.last = (value,)
        return value


class Links:
    def __init__(self, reps, group):
        self.reps, self.group, self.planes = reps, group, group // 2
        self.team, self.wing, self.plane, self.core = map(lax.axis_index, AXES)
        self.q = 2 * self.team + self.wing
        self.place = 2 * self.plane + self.core

    def move(self, value, target):
        pairs = []
        for r in range(self.reps):
            for s in range(self.group):
                to_r, to_s = target(r, s)
                pairs.append((r * self.group + s, to_r * self.group + to_s))
        return lax.ppermute(value, AXES, pairs)

    def across(self, value):
        return self.move(value, lambda r, s: (r, s ^ 1))

    def sideways(self, value):
        return self.move(value, lambda r, s: (r ^ 1, s))

    def along(self, value, step):
        return self.move(value, lambda r, s: (r, (s + 2 * step) % self.group))

    def along_parts(self, value, rows):
        parts = [lax.dynamic_slice_in_dim(value, self.plane * rows, rows)]
        for step in range(1, self.planes):
            to = (self.plane + step) % self.planes
            parts.append(self.along(lax.dynamic_slice_in_dim(value, to * rows, rows), step))
        return parts

    def along_steps(self, share):
        return [self.along(share, k) for k in range(1, self.planes)]

    def summed_everywhere(self, value):
        step = 1
        while step < self.reps:
            value = value + self.move(value, lambda r, s: (r ^ step, s))
            step *= 2
        step = 1
        while step < self.group:
            value = value + self.move(value, lambda r, s: (r, s ^ step))
            step *= 2
        return value


class Spread:
    def __init__(self, links, low):
        self.links, self.low = links, low
        self.count = links.reps >> low
        self.stages = self.count.bit_length() - 1
        self.own = links.q >> low

    def bit_of(self, stage, core):
        return 1 << (stage if core == 0 else self.stages - 1 - stage)

    def swap(self, value, stage):
        return self.links.move(
            value, lambda r, s: (r ^ (self.bit_of(stage, s % 2) << self.low), s)
        )

    def bit(self, stage):
        return jnp.where(self.links.core == 0, self.bit_of(stage, 0), self.bit_of(stage, 1))

    def gathered(self, value):
        parts, offsets = [value], [jnp.int32(0)]
        for stage in range(self.stages):
            parts += [self.swap(part, stage) for part in parts]
            offsets += [offset ^ self.bit(stage) for offset in offsets]
        return parts, [self.own ^ offset for offset in offsets]

    def turned_slot(self, slot):
        return sum(((slot >> k) & 1) << (self.stages - 1 - k) for k in range(self.stages))

    def slot_owners(self):
        owners = []
        for slot in range(self.count):
            owner = self.own
            for stage in range(self.stages):
                if (slot >> (self.stages - 1 - stage)) & 1:
                    owner = owner ^ self.bit(stage)
            owners.append(owner)
        return owners


def pick(blocks, index):
    value = blocks[0]
    for k in range(1, len(blocks)):
        value = jnp.where(index == k, blocks[k], value)
    return value


def in_order(parts, owners):
    ordered = []
    for k in range(len(parts)):
        value = parts[0]
        for part, owner in zip(parts[1:], owners[1:]):
            value = jnp.where(owner == k, part, value)
        ordered.append(value)
    return ordered


def nn(left, right):
    return jnp.dot(left, right, preferred_element_type=jnp.float32)


def layer(
    reps,
    group,
    tokens,
    lengths,
    buckets,
    w_query,
    w_key,
    w_value,
    w_out,
    w_gate,
    w_up,
    w_down,
    bias_table,
    norm_attn,
    norm_ffn,
    cotangent,
):
    links = Links(reps, group)
    planes, core, plane, wing, q = links.planes, links.core, links.plane, links.wing, links.q
    spread, team = Spread(links, 0), Spread(links, 1)
    first_core = core == 0
    length, width = tokens.shape
    shard_rows, inner = w_query.shape
    head_count = bias_table.shape[1]
    head_size = inner // head_count
    bucket_count = bias_table.shape[0] * group
    half = inner // 2
    piece = w_down.shape[0] // 2
    unit = max(128, 16 * team.count)
    padded = (piece + unit - 1) // unit * unit
    at = jnp.stack([wing, core])
    share_rows = 2 * shard_rows // reps
    team_rows = 2 * shard_rows // team.count
    down_rows = padded // team.count
    out_rows = w_out.shape[0]
    fold = out_rows // share_rows
    order = Order()
    mark = order.mark

    def by_core(zero, one):
        return jnp.where(first_core, zero, one)

    def row_share(over, keep, recv):
        rows = 2 * shard_rows // over.count
        per = max(over.count // 2, 1)
        return lax.dynamic_slice_in_dim(
            jnp.where(over.own // per == core, keep, recv), over.own % per * rows, rows
        )

    def plane_of(step):
        return (plane + planes - step) % planes

    def column_half(side):
        return jnp.concatenate(
            [w[:, side * half : (side + 1) * half] for w in (w_query, w_key, w_value)], axis=1
        )

    half_zero, half_one = column_half(0), column_half(1)
    qkv_keep, qkv_send = by_core(half_zero, half_one), by_core(half_one, half_zero)
    qkv_recv = links.across(mark(qkv_send))
    ffn_keep, ffn_send = split_columns(at, order(w_gate), w_up, piece, padded)
    ffn_recv = links.across(mark(ffn_send))
    columns = width // reps
    out_share = pick([w_out[:, k * columns : (k + 1) * columns] for k in range(reps)], q)
    out_share = folded(out_share, 1, fold)
    packed_share = jnp.concatenate(
        [row_share(spread, order(qkv_keep), qkv_recv), out_share], axis=1
    )
    packed_steps = links.along_steps(mark(packed_share))
    small = jnp.concatenate([norm_attn, norm_ffn, bias_table.reshape(-1)])
    small_size = small.shape[0]
    small = jnp.pad(small, (0, -small_size % 1024)).reshape(-1, 128)
    small = mark(order(small))
    small_steps = links.along_steps(small)

    floats_in = order(tokens).astype(jnp.float32)
    scale_one = mark(
        lax.rsqrt(jnp.mean(floats_in * floats_in, axis=-1, keepdims=True) + EPSILON)
    )
    down_half = jnp.pad(
        lax.dynamic_slice_in_dim(order(w_down), wing * piece, piece), ((0, padded - piece), (0, 0))
    )
    down_share = mark(lax.dynamic_slice_in_dim(down_half, team.own * down_rows, down_rows))
    positions = lax.broadcasted_iota(jnp.int32, (bucket_count, buckets.shape[0] + 1), 0)
    turned_buckets = jnp.concatenate([order(buckets)[::-1], jnp.full((1,), -1, jnp.int32)])
    one_hot = mark((turned_buckets[None, :] == positions).astype(jnp.float32))

    small = mark(jnp.stack([order(small)] + small_steps))
    small_recv = links.across(small)
    packed_others = mark(jnp.concatenate([order(packed_steps[0])] + packed_steps[1:], axis=0))
    packed_shares, packed_owners = spread.gathered(packed_others)
    ffn_share = mark(row_share(team, order(ffn_keep), ffn_recv))
    f_ffn = lax.all_gather(ffn_share, ("plane", "team"), axis=0, tiled=True)

    small = jnp.stack([order(small), small_recv])
    small = by_core(small, small[::-1])
    small = jnp.concatenate([small, small], axis=1)[:, ::-1]
    small = lax.dynamic_slice_in_dim(small, planes - 1 - plane, planes, axis=1)
    small = small.transpose(1, 0, 2, 3).reshape(group, -1)[:, :small_size]
    gain_one = small[:, :shard_rows].reshape(1, width).astype(jnp.float32)
    gain_two = small[:, shard_rows : 2 * shard_rows].reshape(1, width).astype(jnp.float32)
    full_table = small[:, 2 * shard_rows :].reshape(bucket_count, head_count)
    rel_bias = lax.dot_general(
        full_table.astype(jnp.float32),
        one_hot,
        (((0,), (0,)), ((), ())),
        precision=lax.Precision.HIGHEST,
    )
    bias_rows = mark(rel_bias.reshape(head_count // 2, 2, -1))
    normed_one = mark((order(floats_in) * scale_one * gain_one).astype(jnp.bfloat16))
    one_turned = mark(turn(normed_one, spread.slot_owners(), planes))

    wide = 3 * half
    cuts = [
        (0, 0, shard_rows, 0, 0, wide, (2 * plane + core) * shard_rows, 0),
        (1, 0, shard_rows, 0, 0, wide, (2 * plane + 1 - core) * shard_rows, 0),
        (2, 0, out_rows, 1, 0, width, plane * out_rows, 0),
    ]
    for number, owner in enumerate(packed_owners):
        for step in range(1, planes):
            start = (step - 1) * share_rows
            to = plane_of(step)
            row = to * 2 * shard_rows + owner * share_rows
            cuts.append((number + 3, start, share_rows, 0, 0, wide, row, 0))
            for k in range(fold):
                row = to * out_rows + k * share_rows
                cuts.append(
                    (
                        number + 3,
                        start,
                        share_rows,
                        1,
                        wide + k * columns,
                        columns,
                        row,
                        owner * columns,
                    )
                )
    qkv_half, out_mine = place(
        [order(qkv_keep), qkv_recv, w_out] + packed_shares,
        cuts,
        [(width, wide), (planes * out_rows, width)],
    )
    mark(qkv_half)
    qkv_other = links.across(qkv_half)
    out_theirs = links.across(out_mine)
    g_side = links.sideways(order(cotangent))
    own_qkv = mark(product([order(normed_one)], [qkv_half], most=384))
    other_qkv = mark(product([order(normed_one)], [qkv_other], most=384))
    qkv = mark(jnp.stack([by_core(order(own_qkv), other_qkv), by_core(other_qkv, own_qkv)]))
    context, context_turned, lse = run_forward(
        lengths, bias_rows, order(qkv, g_side), head_size
    )
    mark(context)
    (f_out,) = place(
        [order(out_mine), out_theirs],
        [
            (
                side,
                p * out_rows,
                out_rows,
                0,
                0,
                width,
                (2 * p + (core if side == 0 else 1 - core)) * out_rows,
                0,
            )
            for side in (0, 1)
            for p in range(planes)
        ],
        [(inner, width)],
    )
    attended = floats_in + nn(context, f_out)
    scale_two = lax.rsqrt(jnp.mean(attended * attended, axis=-1, keepdims=True) + EPSILON)
    unit_two = attended * scale_two
    normed_two = mark((unit_two * gain_two).astype(jnp.bfloat16))

    side_two = links.sideways(order(normed_two, g_side))
    core_two = links.across(normed_two)
    down_steps = links.along_steps(down_share)
    by_sides = context_turned.reshape(planes, 2, out_rows, length)
    context_own = by_core(order(by_sides)[:, 0], by_sides[:, 1]).reshape(-1, length)
    context_other = by_core(by_sides[:, 1], by_sides[:, 0]).reshape(-1, length)
    mark(context_own)
    g_core = links.across(order(cotangent))
    g_both = links.across(order(g_side))
    team_g = [cotangent, g_side, g_core, g_both]
    down_others = mark(jnp.concatenate([order(down_steps[0])] + down_steps[1:], axis=0))
    down_shares, down_owners = team.gathered(down_others)
    both_two = links.across(order(side_two))
    team_two = [normed_two, side_two, core_two, both_two]
    mark(order(both_two))
    hidden, hidden_turned, gate_slope, up_slope = gated([order(normed_two)] + team_two[1:], f_ffn)
    mark(hidden)

    cuts = [(0, 0, padded, 0, 0, width, plane * padded, 0)]
    for number, owner in enumerate(down_owners):
        for step in range(1, planes):
            row = plane_of(step) * padded + owner * down_rows
            cuts.append((number + 1, (step - 1) * down_rows, down_rows, 0, 0, width, row, 0))
    (f_down,) = place([order(down_half)] + down_shares, cuts, [(planes * padded, width)])
    mark(f_down)
    two_turned = mark(turn_team([order(normed_two)] + team_two[1:]))
    d_pair = mark(gated_back([order(cotangent)] + team_g[1:], f_down, gate_slope, up_slope))
    ffn_sum = lax.psum_scatter(
        mark(pair_grad(order(two_turned), d_pair)),
        ("plane", "team"),
        scatter_dimension=0,
        tiled=True,
    )
    d_own, d_side, d_sent = pair_back(order(d_pair), f_ffn)
    d_recv = links.across(mark(d_sent))

    team_owners = team.slot_owners()
    team_wide = width // team.count
    down_arrived = []

    def down_slots(low, high):
        return mark(
            column_slots(
                order(hidden_turned),
                team_g,
                team_owners[low:high],
                team_wide,
                [(value, low) for value in down_arrived],
            )
        )

    low, high = team.count // 2, team.count
    down_sent = down_slots(low, high)
    d_side = mark((order(d_side) + d_recv[length:].astype(jnp.float32)).astype(jnp.bfloat16))
    d_theirs = links.sideways(d_side)
    down_arrived.append(team.swap(order(down_sent), 0))
    ffn_own, ffn_side, ffn_sent = product([order(hidden)], [f_down], kind="team")
    ffn_their = links.across(mark(ffn_sent))
    ffn_side = mark((order(ffn_side) + ffn_their[length:].astype(jnp.float32)).astype(jnp.bfloat16))

    d_normed_two = (
        order(d_own) + d_recv[:length].astype(jnp.float32) + d_theirs.astype(jnp.float32)
    )
    ffn_theirs = links.sideways(order(ffn_side, d_theirs))
    ffn_gain_term = jnp.sum(d_normed_two * unit_two, axis=0)
    grad_in = cotangent.astype(jnp.float32)
    d_attended = grad_in + norm_back(d_normed_two, unit_two, scale_two, gain_two)
    d_branch = d_attended.astype(jnp.bfloat16)
    d_context = mark(product([d_branch], [f_out], across=True))

    d_query, d_key, d_value, d_lined = run_backward(
        lengths, bias_rows, qkv, order(d_context), lse, head_size
    )
    d_qkv = mark(jnp.concatenate([d_query, d_key, d_value], axis=2))
    d_mine = by_core(order(d_qkv)[0], d_qkv[1])
    d_other = by_core(d_qkv[1], d_qkv[0])
    owners = spread.slot_owners()

    def packed(slots, grad, context_rows, added):
        return mark(
            packed_slots(
                one_turned,
                order(grad),
                context_rows,
                d_branch,
                slots,
                [owners[slot] for slot in slots],
                reps,
                planes,
                added,
            )
        )

    output = mark(
        (
            order(attended)
            + ffn_own
            + ffn_their[:length].astype(jnp.float32)
            + ffn_theirs.astype(jnp.float32)
        ).astype(jnp.bfloat16)
    )
    for stage in range(1, team.stages):
        low, high = low // 2, low
        down_arrived.append(team.swap(down_slots(low, high), stage))
    down_parts = links.along_parts(down_slots(0, 1), padded)
    back = packed([spread.turned_slot(slot) for slot in range(reps)], d_other, context_other, [])
    arrived = [links.across(back)]
    mark(order(ffn_sum))
    packed_low, packed_high = reps // 2, reps
    sent = packed(
        range(packed_low, packed_high), d_mine, context_own, [(value, packed_low) for value in arrived]
    )
    arrived.append(spread.swap(sent, 0))
    ffn_shares = spread.gathered(order(ffn_sum))
    d_normed_one = product(
        [order(d_mine), d_other], [qkv_half, qkv_other], across=True, kind="wide"
    )
    unit_one = floats_in * scale_one
    attn_gain_term = jnp.sum(d_normed_one * unit_one, axis=0)
    grad_tokens = mark(
        (d_attended + norm_back(d_normed_one, unit_one, scale_one, gain_one)).astype(jnp.bfloat16)
    )
    table_term = lax.dot_general(
        one_hot,
        order(d_lined).reshape(head_count, -1),
        (((1,), (1,)), ((), ())),
        precision=lax.Precision.HIGHEST,
    )
    terms = jnp.concatenate([attn_gain_term, ffn_gain_term, table_term.reshape(-1)])
    terms = mark(jnp.pad(terms, (0, -terms.shape[0] % 1024)).reshape(-1, 128))
    for stage in range(1, spread.stages):
        packed_low, packed_high = packed_low // 2, packed_low
        sent = packed(
            range(packed_low, packed_high),
            d_mine,
            context_own,
            [(value, packed_low) for value in arrived],
        )
        arrived.append(spread.swap(sent, stage))
    down_total = sum(part.astype(jnp.float32) for part in [order(down_parts[0])] + down_parts[1:])
    down_total = mark(down_total.astype(jnp.bfloat16))
    down_shares = spread.gathered(down_total)
    sent = packed([0], d_mine, context_own, [(value, 0) for value in arrived])
    packed_parts = links.along_parts(sent, share_rows)
    packed_total = sum(part.astype(jnp.float32) for part in packed_parts).astype(jnp.bfloat16)

    parts = in_order(*down_shares)
    grad_down = jnp.concatenate(
        [jnp.concatenate(parts[w::2], axis=1)[:piece] for w in (0, 1)], axis=0
    ).astype(jnp.float32)
    terms = links.summed_everywhere(terms).reshape(-1)

    def by_owner(parts):
        per = len(parts) // 2
        low = jnp.concatenate(parts[:per], axis=0)
        high = jnp.concatenate(parts[per:], axis=0)
        return by_core(low, high), by_core(high, low)

    def wings_apart(parts):
        return parts[0::2] + parts[1::2]

    parts = in_order(*ffn_shares)
    per = reps // 2
    low, high = wings_apart(parts[:per]), wings_apart(parts[per:])
    low, high = jnp.concatenate(low, axis=0), jnp.concatenate(high, axis=0)
    ffn_mine, ffn_send = by_core(low, high), by_core(high, low)
    ffn_other = links.across(ffn_send)
    grad_gate, grad_up = join_columns(core, ffn_mine, ffn_other, piece, padded)

    parts = in_order(*spread.gathered(packed_total))
    grad_out = jnp.concatenate(
        [unfolded(part[:, wide:], fold) for part in parts], axis=1
    ).astype(jnp.float32)
    qkv_mine, qkv_send = by_owner([part[:, :wide] for part in parts])
    qkv_recv = links.across(qkv_send)
    grad_halves = (by_core(qkv_mine, qkv_recv), by_core(qkv_recv, qkv_mine))
    grad_query, grad_key, grad_value = [
        jnp.concatenate(
            [value[:, kind * half : (kind + 1) * half] for value in grad_halves], axis=1
        ).astype(jnp.float32)
        for kind in range(3)
    ]
    grad_norm_attn = lax.dynamic_slice_in_dim(terms, links.place * shard_rows, shard_rows)
    grad_norm_ffn = lax.dynamic_slice_in_dim(terms, width + links.place * shard_rows, shard_rows)
    table_size = bias_table.size
    grad_table = lax.dynamic_slice_in_dim(
        terms, 2 * width + links.place * table_size, table_size
    ).reshape(bias_table.shape)
    return (
        output,
        grad_tokens,
        grad_query,
        grad_key,
        grad_value,
        grad_out,
        grad_gate,
        grad_up,
        grad_down,
        grad_table,
        grad_norm_attn,
        grad_norm_ffn,
    )


def solution(mesh):
    reps, group = mesh.shape["rep"], mesh.shape["shard"]
    devices = mesh.devices.reshape(reps // 2, 2, group // 2, 2)
    rows, part = P(AXES[2:], None), P(AXES[2:])
    tokens = P(AXES, None)
    return jax.shard_map(
        functools.partial(layer, reps, group),
        mesh=jax.sharding.Mesh(devices, AXES),
        in_specs=(tokens, P(AXES), P()) + (rows,) * 8 + (part, part, tokens),
        out_specs=(tokens, tokens) + (rows,) * 8 + (part, part),
        check_vma=False,
    )
```

time: 772 us -> 609 us (0.79)
  matrix products: 161 us -> 4.12 us
  Pallas kernels: 67.9 us -> 212 us
  waiting for transfers between devices: 323 us -> 221 us
  starting transfers between devices: 87.1 us -> 53.9 us
  local copies, waits for them, and re-layouts: 53.2 us -> 31 us
  between operations: 3.05 us -> 15.9 us
  blocking collectives: 12.6 us -> 0 us
    pallas_call x5 -> x20, Pallas kernels: 27.1 us -> 175 us  [the longest x5 37.5 us: product(): pl.pallas_call(functools.partial(product_kernel, pairs=len(lefts), across...]
    ppermute x86 -> x54, waiting for transfers between devices: 323 us -> 208 us  [move(): return lax.ppermute(value, AXES, pairs)]
    dot_general x13 -> x1, matrix products: 82.4 us -> 0.19 us  [layer(): lax.dot_general(one_hot, order(d_lined).reshape(head_count, -1), (((1,),...]
    dot_general x16 -> x1, matrix products: 77.4 us -> 3.15 us  [nn(): return jnp.dot(left, right, preferred_element_type=jnp.float32)]
    ppermute x86 -> x54, starting transfers between devices: 87.1 us -> 53.9 us  [move(): return lax.ppermute(value, AXES, pairs)]
    unnamed x167 -> x81, local copies, waits for them, and re-layouts: 28.5 us -> 14.3 us
    all_gather x1 -> x0, blocking collectives: 12.6 us -> none  [layer(): small = lax.all_gather(small, 'shard', axis=0, tiled=True)[:, :small_size]]
    reduce_scatter x0 -> x1, waiting for transfers between devices: none -> 12.4 us  [layer(): lax.psum_scatter(mark(pair_grad(order(two_turned), d_pair)), ('plane', 't...]
  transfers between devices with their start and end apart: 86 -> 56, of which waited for: 40 -> 28; matrix products, arithmetic and copies ran while one was open for 26% -> 12% of each run, Pallas kernels for 9% -> 25%
where the time goes in v2:
time: 609 us; the launch traced here: 597 us
  waiting for transfers between devices  221 us (36%)
  Pallas kernels  212 us (35%)
  other arithmetic  60 us (10%)
  starting transfers between devices  53.9 us (9%)
  local copies, waits for them, and re-layouts  31 us (5%)
  between operations  15.9 us (3%)
    ppermute x54, waiting for transfers between devices, move(): return lax.ppermute(value, AXES, pairs)  208 us
    ppermute x54, starting transfers between devices, move(): return lax.ppermute(value, AXES, pairs)  53.9 us
    pallas_call x5, Pallas kernels, product(): pl.pallas_call(functools.partial(product_kernel, pairs=len(lefts), across...  37.5 us
    pallas_call x1, Pallas kernels, gated(): pl.pallas_call(functools.partial(gated_kernel, count=len(blocks)), grid=(...  22.9 us
    pallas_call x4, Pallas kernels, packed_slots(): pl.pallas_call(packed_slot_kernel, grid_spec=pltpu.PrefetchScalarGridSpec...  22.3 us
    pallas_call x1, Pallas kernels, pair_back(): pl.pallas_call(pair_back_kernel, grid=(width // tile,), in_specs=[pl.Bloc...  19 us
    pallas_call x1, Pallas kernels, pair_grad(): pl.pallas_call(pair_grad_kernel, grid=(2 * steps,), in_specs=[pl.BlockSpe...  18.8 us
    pallas_call x1, Pallas kernels, run_backward(): pl.pallas_call(functools.partial(attention_backward, head_size=head_size)...  16.7 us
  transfers between devices with their start and end apart: 56, of which 28 were waited for; matrix products, arithmetic and copies ran while one was open for 12% of the time, Pallas kernels for 25%

profile of v2, /device:TPU:10, one launch (start us, length us, event | category | flops | bytes accessed | tf_op | source)
XLA Modules:
  0.0 597.2 jit_solution(17105571439371259215)
XLA Ops:
  11.2 4.7 split.1
  28.9 3.9 collective-permute-done.1
  36.1 17.6 %collective-permute-done.5 = bf16[96,1536]{1,0:T(8,128)(2,1)S(1)} collective-permute-done((bf16[96,1536]{1,0:T(8,128)(2,1)S(1)}, bf16[96,1536]{1,0:T(8,128)(2,1)S(1)}, u32[]{:S(2)}, u32[]{:S(2)}) %collective-permute-start.5) | collective-permute-done | bytes 294944 | tf_op jit(solution)/shard_map/ppermute | solution.py:686
  61.3 11.4 %collective-permute-done.9.refs_4_ = bf16[288,1536]{1,0:T(8,128)(2,1)} collective-permute-done((bf16[288,1536]{1,0:T(8,128)(2,1)S(1)}, bf16[288,1536]{1,0:T(8,128)(2,1)}, u32[]{:S(2)}, u32[]{:S(2)}) %collective-permute-start.9) | collective-permute-done | bytes 884768 | tf_op jit(solution)/shard_map/ppermute | solution.py:686
  76.7 3.4 multiply_convert_fusion.1.x_ref.refs_0_
  80.1 3.9 turn.1
  84.7 9.5 %collective-permute-done.11.refs_6_ = bf16[288,1536]{1,0:T(8,128)(2,1)S(1)} collective-permute-done((bf16[288,1536]{1,0:T(8,128)(2,1)}, bf16[288,1536]{1,0:T(8,128)(2,1)S(1)}, u32[]{:S(2)}, u32[]{:S(2)}) %collective-permute-start.11) | collective-permute-done | bytes 884768 | tf_op jit(solution)/shard_map/ppermute | solution.py:686
  95.1 5.4 place.3
  104.9 5.9 product.5
  112.7 6.0 product.6
  121.8 15.9 %collective-permute-done.13.refs_1_ = bf16[512,1536]{1,0:T(8,128)(2,1)} collective-permute-done((bf16[512,1536]{1,0:T(8,128)(2,1)}, bf16[512,1536]{1,0:T(8,128)(2,1)}, u32[]{:S(2)}, u32[]{:S(2)}) %collective-permute-start.13) | collective-permute-done | bytes 1572896 | tf_op jit(solution)/shard_map/ppermute | solution.py:686
  137.7 10.5 %attend.1 = (bf16[512,768]{1,0:T(8,128)(2,1)}, bf16[768,512]{1,0:T(8,128)(2,1)}, f32[6,2,512]{2,1,0:T(2,128)}) custom-call(s32[1]{0:T(128)S(6)} %copy.60.valid_ref, f32[6,2,1024]{2,1,0:T(2,128)} %copy.38.bias_ref, bf16[2,512,1152]{2,1,0:T(8,128)(2,1)} %pad_maximum_fusion.q_ref.k_ref.v_ref, bf16[2,512,1152]{2,1,0:T(8,128)(2,1)} %pad_maximum_fusion.q_ref.k_ref.v_ref, ...), custom_call_target="tpu_custom_call" | custom-call | flops 805306368 | bytes 1572864 | tf_op jit(solution)/shard_map/attend/pallas_call | solution.py:128
  149.2 3.9 place.4.refs_1_
  153.2 3.2 multiply_reduce_fusion.4
  164.1 6.3 %collective-permute-done.17 = bf16[128,1536]{1,0:T(8,128)(2,1)S(1)} collective-permute-done((bf16[128,1536]{1,0:T(8,128)(2,1)S(1)}, bf16[128,1536]{1,0:T(8,128)(2,1)S(1)}, u32[]{:S(2)}, u32[]{:S(2)}) %collective-permute-start.17) | collective-permute-done | bytes 393248 | tf_op jit(solution)/shard_map/ppermute | solution.py:686
  171.2 20.6 %collective-permute-done.18 = bf16[128,1536]{1,0:T(8,128)(2,1)S(1)} collective-permute-done((bf16[128,1536]{1,0:T(8,128)(2,1)S(1)}, bf16[128,1536]{1,0:T(8,128)(2,1)S(1)}, u32[]{:S(2)}, u32[]{:S(2)}) %collective-permute-start.18) | collective-permute-done | bytes 393248 | tf_op jit(solution)/shard_map/ppermute | solution.py:686
  200.4 22.9 %gated.1 = (bf16[2048,1024]{1,0:T(8,128)(2,1)}, bf16[1024,2048]{1,0:T(8,128)(2,1)}, bf16[2048,1024]{1,0:T(8,128)(2,1)}, bf16[2048,1024]{1,0:T(8,128)(2,1)}) custom-call(bf16[512,1536]{1,0:T(8,128)(2,1)} %multiply_convert_fusion.refs_0_, bf16[512,1536]{1,0:T(8,128)(2,1)} %collective-permute-done.15.refs_1_, ...), custom_call_target="tpu_custom_call" | custom-call | flops 3221225472 | bytes 6291456 | tf_op jit(solution)/shard_map/gated/pallas_call | solution.py:553
  224.8 4.2 place.5.refs_4_.refs_1_
  229.1 7.6 %turn_team.1.left_ref = bf16[1536,2048]{1,0:T(8,128)(2,1)} custom-call(bf16[512,1536]{1,0:T(8,128)(2,1)} %multiply_convert_fusion.refs_0_, bf16[512,1536]{1,0:T(8,128)(2,1)} %collective-permute-done.15.refs_1_, bf16[512,1536]{1,0:T(8,128)(2,1)} %collective-permute-done.16.refs_2_, bf16[512,1536]{1,0:T(8,128)(2,1)} %collective-permute-done.20.refs_3_), custom_call_target="tpu_custom_call" | custom-call | flops 402653184 | bytes 786432 | tf_op jit(solution)/shard_map/turn_team/pallas_call | solution.py:295
  236.6 14.0 %gated_back.1.right_ref.pair_ref = bf16[2,2048,1024]{2,1,0:T(8,128)(2,1)} custom-call(bf16[512,1536]{1,0:T(8,128)(2,1)} %refs_0_.4, bf16[512,1536]{1,0:T(8,128)(2,1)} %collective-permute-done.13.refs_1_, bf16[512,1536]{1,0:T(8,128)(2,1)} %collective-permute-done.22.refs_2_, bf16[512,1536]{1,0:T(8,128)(2,1)} %collective-permute-done.23.refs_3_, ...), custom_call_target="tpu_custom_call" | custom-call | flops 1610612736 | bytes 3145728 | tf_op jit(solution)/shard_map/gated_back/pallas_call | solution.py:585
  250.6 18.8 %pair_grad.1 = bf16[1536,2048]{1,0:T(8,128)(2,1)} custom-call(bf16[1536,2048]{1,0:T(8,128)(2,1)} %turn_team.1.left_ref, bf16[2,2048,1024]{2,1,0:T(8,128)(2,1)} %gated_back.1.right_ref.pair_ref), custom_call_target="tpu_custom_call" | custom-call | flops 3221225472 | bytes 6291456 | tf_op jit(solution)/shard_map/pair_grad/pallas_call | solution.py:607
  269.4 19.0 %pair_back.1 = (f32[512,1536]{1,0:T(8,128)}, f32[512,1536]{1,0:T(8,128)}, bf16[1024,1536]{1,0:T(8,128)(2,1)}) custom-call(bf16[2,2048,1024]{2,1,0:T(8,128)(2,1)} %gated_back.1.right_ref.pair_ref, bf16[1536,2048]{1,0:T(8,128)(2,1)} %all-gather.2.cloned.1.call-done.refs_4_.refs_5_.right_ref), custom_call_target="tpu_custom_call" | custom-call | flops 3221225472 | bytes 6291456 | tf_op jit(solution)/shard_map/pair_back/pallas_call | solution.py:637
  288.4 7.5 %column_slots.2 = bf16[1024,768]{1,0:T(8,128)(2,1)} custom-call(s32[1]{0:T(128)} %bitcast.63.at_ref, bf16[1024,2048]{1,0:T(8,128)(2,1)} %get-tuple-element.134.left_ref, bf16[512,1536]{1,0:T(8,128)(2,1)} %refs_0_.4, bf16[512,1536]{1,0:T(8,128)(2,1)} %collective-permute-done.13.refs_1_, bf16[512,1536]{1,0:T(8,128)(2,1)} %collective-permute-done.22.refs_2_, ...), custom_call_target="tpu_custom_call" | custom-call | flops 805306368 | bytes 1572864 | tf_op jit(solution)/shard_map/column_slots/pallas_call | solution.py:428
  295.9 4.6 add_convert_fusion.3
  300.6 11.0 %product.7 = (f32[512,1536]{1,0:T(8,128)}, f32[512,1536]{1,0:T(8,128)}, bf16[1024,1536]{1,0:T(8,128)(2,1)}) custom-call(bf16[2048,1024]{1,0:T(8,128)(2,1)} %get-tuple-element.121.refs_0_, bf16[1024,1536]{1,0:T(8,128)(2,1)} %place.5.refs_4_.refs_1_), custom_call_target="tpu_custom_call" | custom-call | flops 1610612736 | bytes 3145728 | tf_op jit(solution)/shard_map/product/pallas_call | solution.py:390
  317.8 3.3 add_convert_fusion.2
  321.1 27.7 %collective-permute-done.26 = bf16[512,1536]{1,0:T(8,128)(2,1)S(1)} collective-permute-done((bf16[512,1536]{1,0:T(8,128)(2,1)}, bf16[512,1536]{1,0:T(8,128)(2,1)S(1)}, u32[]{:S(2)}, u32[]{:S(2)}) %collective-permute-start.26) | collective-permute-done | bytes 1572896 | tf_op jit(solution)/shard_map/ppermute | solution.py:686
  351.5 4.9 fusion.21
  356.4 4.8 product.8.dctx_ref
  361.2 16.7 %attend_back.1 = (bf16[2,512,384]{2,1,0:T(8,128)(2,1)}, bf16[2,512,384]{2,1,0:T(8,128)(2,1)}, bf16[2,512,384]{2,1,0:T(8,128)(2,1)}, f32[6,2,1024]{2,1,0:T(2,128)}) custom-call(s32[1]{0:T(128)S(6)} %copy.60.valid_ref, f32[6,2,1024]{2,1,0:T(2,128)} %copy.38.bias_ref, bf16[2,512,1152]{2,1,0:T(8,128)(2,1)} %pad_maximum_fusion.q_ref.k_ref.v_ref, ...), custom_call_target="tpu_custom_call" | custom-call | flops 1610612736 | bytes 3145728 | tf_op jit(solution)/shard_map/attend_back/pallas_call | solution.py:162
  384.4 3.6 add_convert_fusion.1
  389.1 7.8 %column_slots.3 = bf16[1024,768]{1,0:T(8,128)(2,1)} custom-call(s32[1]{0:T(128)} %bitcast.66.at_ref, bf16[1024,2048]{1,0:T(8,128)(2,1)} %get-tuple-element.134.left_ref, bf16[512,1536]{1,0:T(8,128)(2,1)} %refs_0_.4, bf16[512,1536]{1,0:T(8,128)(2,1)} %collective-permute-done.13.refs_1_, bf16[512,1536]{1,0:T(8,128)(2,1)} %collective-permute-done.22.refs_2_, ...), custom_call_target="tpu_custom_call" | custom-call | flops 805306368 | bytes 1572864 | tf_op jit(solution)/shard_map/column_slots/pallas_call | solution.py:428
  396.9 7.6 %packed_slots.4 = bf16[1536,1536]{1,0:T(8,128)(2,1)} custom-call(s32[4]{0:T(128)} %constant.196.clone.row_ref, s32[4]{0:T(128)} %add_add_fusion.1.at_ref, bf16[1536,512]{1,0:T(8,128)(2,1)} %bitcast.103, bf16[512,1152]{1,0:T(8,128)(2,1)} %get-tuple-element.136.grad_ref.refs_2_, bf16[384,512]{1,0:T(8,128)(2,1)} %bitcast.111, ...), custom_call_target="tpu_custom_call" | custom-call | flops 603979776 | bytes 1179648 | tf_op jit(solution)/shard_map/packed_slots/pallas_call | solution.py:479
  405.1 7.5 %collective-permute-done.29.refs_0_ = bf16[1536,1536]{1,0:T(8,128)(2,1)S(1)} collective-permute-done((bf16[1536,1536]{1,0:T(8,128)(2,1)}, bf16[1536,1536]{1,0:T(8,128)(2,1)S(1)}, u32[]{:S(2)}, u32[]{:S(2)}) %collective-permute-start.29) | collective-permute-done | bytes 4718624 | tf_op jit(solution)/shard_map/ppermute | solution.py:686
  414.9 5.6 packed_slots.5
  422.0 12.4 %reduce-scatter.2.cloned.1.call-done = bf16[192,2048]{1,0:T(8,128)(2,1)} async-done(((bf16[1536,2048]{1,0:T(8,128)(2,1)}), bf16[192,2048]{1,0:T(8,128)(2,1)}) %reduce-scatter.2.cloned.1.call-update) | async-done | bytes 786448 | tf_op jit(solution)/shard_map/reduce_scatter | solution.py:984
  436.5 9.7 %product.9 = f32[512,1536]{1,0:T(8,128)} custom-call(bf16[512,1152]{1,0:T(8,128)(2,1)} %get-tuple-element.142.grad_ref.refs_0_, bf16[1536,1152]{1,0:T(8,128)(2,1)} %get-tuple-element.91.refs_1_, bf16[512,1152]{1,0:T(8,128)(2,1)} %get-tuple-element.136.grad_ref.refs_2_, bf16[1536,1152]{1,0:T(8,128)(2,1)} %copy-done.7), custom_call_target="tpu_custom_call" | custom-call | flops 905969664 | bytes 1769472 | tf_op jit(solution)/shard_map/product/pallas_call | solution.py:390
  451.3 15.3 %collective-permute-done.42 = bf16[192,2048]{1,0:T(8,128)(2,1)} collective-permute-done((bf16[192,2048]{1,0:T(8,128)(2,1)}, bf16[192,2048]{1,0:T(8,128)(2,1)}, u32[]{:S(2)}, u32[]{:S(2)}) %collective-permute-start.42) | collective-permute-done | bytes 786464 | tf_op jit(solution)/shard_map/ppermute | solution.py:686
  473.0 4.3 packed_slots.6
  479.0 5.6 collective-permute-start.51
  494.5 19.3 %collective-permute-done.31 = bf16[256,768]{1,0:T(8,128)(2,1)S(1)} collective-permute-done((bf16[256,768]{1,0:T(8,128)(2,1)S(1)}, bf16[256,768]{1,0:T(8,128)(2,1)S(1)}, u32[]{:S(2)}, u32[]{:S(2)}) %collective-permute-start.31) | collective-permute-done | bytes 393248 | tf_op jit(solution)/shard_map/ppermute | solution.py:686
  513.9 7.9 %collective-permute-done.32 = bf16[256,768]{1,0:T(8,128)(2,1)S(1)} collective-permute-done((bf16[256,768]{1,0:T(8,128)(2,1)S(1)}, bf16[256,768]{1,0:T(8,128)(2,1)S(1)}, u32[]{:S(2)}, u32[]{:S(2)}) %collective-permute-start.32) | collective-permute-done | bytes 393248 | tf_op jit(solution)/shard_map/ppermute | solution.py:686
  526.6 4.8 packed_slots.7
  537.0 5.5 collective-permute-done.35
  543.1 15.0 %collective-permute-done.36 = bf16[96,1536]{1,0:T(8,128)(2,1)S(1)} collective-permute-done((bf16[96,1536]{1,0:T(8,128)(2,1)S(1)}, bf16[96,1536]{1,0:T(8,128)(2,1)S(1)}, u32[]{:S(2)}, u32[]{:S(2)}) %collective-permute-start.36) | collective-permute-done | bytes 294944 | tf_op jit(solution)/shard_map/ppermute | solution.py:686
  565.9 3.4 collective-permute-done.38
  572.9 3.5 collective-permute-done.39
  581.0 5.0 join.1
  (271 shorter events, 138.5 us)
Async XLA Ops:
  7.2 193.2 %all-gather.2.cloned.1.call-start = ((), (), s32[]{:S(2)}) async-start(), calls=%async_computation.1 | async-start | bytes 7077888 | tf_op jit(solution)/shard_map/all_gather | solution.py:872
  10.5 12.1 %collective-permute-start = (bf16[192,1152]{1,0:T(8,128)(2,1)}, bf16[192,1152]{1,0:T(8,128)(2,1)}, u32[]{:S(2)}, u32[]{:S(2)}) collective-permute-start(bf16[192,1152]{1,0:T(8,128)(2,1)} %get-tuple-element.180), channel_id=1, source_target_pairs={{0,1},{1,0},{2,3},{3,2},{4,5},{5,4},{6,7},{7,6},{8,9},{9,8},{10,11... | collective-permute-start | bytes 1327112 | tf_op jit(solution)/shard_map/ppermute | solution.py:686
  15.9 39.3 %collective-permute-start.7 = (bf16[192,2048]{1,0:T(8,128)(2,1)}, bf16[192,2048]{1,0:T(8,128)(2,1)}, u32[]{:S(2)}, u32[]{:S(2)}) collective-permute-start(bf16[192,2048]{1,0:T(8,128)(2,1)} %get-tuple-element.80), channel_id=1, source_target_pairs={{0,1},{1,0},{2,3},{3,2},{4,5},{5,4},{6,7},{7,6},{8,9},{9,8},{10,11... | collective-permute-start | bytes 2359304 | tf_op jit(solution)/shard_map/ppermute | solution.py:686
  23.6 12.4 %collective-permute-start.4 = (bf16[96,1536]{1,0:T(8,128)(2,1)S(1)}, bf16[96,1536]{1,0:T(8,128)(2,1)S(1)}, u32[]{:S(2)}, u32[]{:S(2)}) collective-permute-start(bf16[96,1536]{1,0:T(8,128)(2,1)S(1)} %pad_maximum_fusion.8), channel_id=1, source_target_pairs={{0,2},{1,3},{2,4},{3,5},{4,6},{5,7},{6,0},{7,1},{8,10},{9,11},{10,... | collective-permute-start | bytes 884744 | tf_op jit(solution)/shard_map/ppermute | solution.py:686
  25.3 7.6 %collective-permute-start.1 = (bf16[8,128]{1,0:T(8,128)(2,1)S(1)}, bf16[8,128]{1,0:T(8,128)(2,1)S(1)}, u32[]{:S(2)}, u32[]{:S(2)}) collective-permute-start(bf16[8,128]{1,0:T(8,128)(2,1)S(1)} %fusion.20), channel_id=1, source_target_pairs={{0,2},{1,3},{2,4},{3,5},{4,6},{5,7},{6,0},{7,1},{8,10},{9,11},{10,... | collective-permute-start | bytes 6152 | tf_op jit(solution)/shard_map/ppermute | solution.py:686
  26.8 8.6 %collective-permute-start.2 = (bf16[8,128]{1,0:T(8,128)(2,1)S(1)}, bf16[8,128]{1,0:T(8,128)(2,1)S(1)}, u32[]{:S(2)}, u32[]{:S(2)}) collective-permute-start(bf16[8,128]{1,0:T(8,128)(2,1)S(1)} %fusion.20), channel_id=1, source_target_pairs={{0,4},{1,5},{2,6},{3,7},{4,0},{5,1},{6,2},{7,3},{8,12},{9,13},{10,... | collective-permute-start | bytes 6152 | tf_op jit(solution)/shard_map/ppermute | solution.py:686
  28.1 7.9 %collective-permute-start.3 = (bf16[8,128]{1,0:T(8,128)(2,1)S(1)}, bf16[8,128]{1,0:T(8,128)(2,1)S(1)}, u32[]{:S(2)}, u32[]{:S(2)}) collective-permute-start(bf16[8,128]{1,0:T(8,128)(2,1)S(1)} %fusion.20), channel_id=1, source_target_pairs={{0,6},{1,7},{2,0},{3,1},{4,2},{5,3},{6,4},{7,5},{8,14},{9,15},{10,... | collective-permute-start | bytes 6152 | tf_op jit(solution)/shard_map/ppermute | solution.py:686
  32.8 20.9 %collective-permute-start.5 = (bf16[96,1536]{1,0:T(8,128)(2,1)S(1)}, bf16[96,1536]{1,0:T(8,128)(2,1)S(1)}, u32[]{:S(2)}, u32[]{:S(2)}) collective-permute-start(bf16[96,1536]{1,0:T(8,128)(2,1)S(1)} %pad_maximum_fusion.8), channel_id=1, source_target_pairs={{0,4},{1,5},{2,6},{3,7},{4,0},{5,1},{6,2},{7,3},{8,12},{9,13},{10,... | collective-permute-start | bytes 884744 | tf_op jit(solution)/shard_map/ppermute | solution.py:686
  35.4 19.2 %collective-permute-start.6 = (bf16[96,1536]{1,0:T(8,128)(2,1)S(1)}, bf16[96,1536]{1,0:T(8,128)(2,1)S(1)}, u32[]{:S(2)}, u32[]{:S(2)}) collective-permute-start(bf16[96,1536]{1,0:T(8,128)(2,1)S(1)} %pad_maximum_fusion.8), channel_id=1, source_target_pairs={{0,6},{1,7},{2,0},{3,1},{4,2},{5,3},{6,4},{7,5},{8,14},{9,15},{10,... | collective-permute-start | bytes 884744 | tf_op jit(solution)/shard_map/ppermute | solution.py:686
  35.9 25.1 %collective-permute-start.8 = (bf16[4,8,128]{2,1,0:T(8,128)(2,1)S(1)}, bf16[4,8,128]{2,1,0:T(8,128)(2,1)S(1)}, u32[]{:S(2)}, u32[]{:S(2)}) collective-permute-start(bf16[4,8,128]{2,1,0:T(8,128)(2,1)S(1)} %pad_maximum_fusion.11), channel_id=1, source_target_pairs={{0,1},{1,0},{2,3},{3,2},{4,5},{5,4},{6,7},{7,6},{8,9},{9,8},{10,11... | collective-permute-start | bytes 24584 | tf_op jit(solution)/shard_map/ppermute | solution.py:686
  54.6 18.1 %collective-permute-start.9 = (bf16[288,1536]{1,0:T(8,128)(2,1)S(1)}, bf16[288,1536]{1,0:T(8,128)(2,1)}, u32[]{:S(2)}, u32[]{:S(2)}) collective-permute-start(bf16[288,1536]{1,0:T(8,128)(2,1)S(1)} %constant_dynamic-update-slice_fusion.refs_3_), channel_id=1, source_target_pairs={{0,8},{1,17},{2,10},{3,19},{4,12},{5,21},{6,14},{7,23},{8,0},{9,25... | collective-permute-start | bytes 2654216 | tf_op jit(solution)/shard_map/ppermute | solution.py:686
  57.4 377.1 %reduce-scatter.2.cloned.1.call-start = ((), (), s32[]{:S(2)}) async-start(), calls=%async_computation.2 | async-start | bytes 7077888 | tf_op jit(solution)/shard_map/reduce_scatter | solution.py:984
  59.5 25.2 %collective-permute-start.10 = (bf16[288,1536]{1,0:T(8,128)(2,1)S(1)}, bf16[288,1536]{1,0:T(8,128)(2,1)S(1)}, u32[]{:S(2)}, u32[]{:S(2)}) collective-permute-start(bf16[288,1536]{1,0:T(8,128)(2,1)S(1)} %constant_dynamic-update-slice_fusion.refs_3_), channel_id=1, source_target_pairs={{0,16},{1,9},{2,18},{3,11},{4,20},{5,13},{6,22},{7,15},{8,24},{9,1... | collective-permute-start | bytes 2654216 | tf_op jit(solution)/shard_map/ppermute | solution.py:686
  72.7 21.5 %collective-permute-start.11 = (bf16[288,1536]{1,0:T(8,128)(2,1)}, bf16[288,1536]{1,0:T(8,128)(2,1)S(1)}, u32[]{:S(2)}, u32[]{:S(2)}) collective-permute-start(bf16[288,1536]{1,0:T(8,128)(2,1)} %collective-permute-done.9.refs_4_), channel_id=1, source_target_pairs={{0,16},{1,9},{2,18},{3,11},{4,20},{5,13},{6,22},{7,15},{8,24},{9,1... | collective-permute-start | bytes 2654216 | tf_op jit(solution)/shard_map/ppermute | solution.py:686
  100.5 10.4 %collective-permute-start.12 = (bf16[1536,1152]{1,0:T(8,128)(2,1)}, bf16[1536,1152]{1,0:T(8,128)(2,1)S(1)}, u32[]{:S(2)}, u32[]{:S(2)}) collective-permute-start(bf16[1536,1152]{1,0:T(8,128)(2,1)} %get-tuple-element.91.refs_1_), channel_id=1, source_target_pairs={{0,1},{1,0},{2,3},{3,2},{4,5},{5,4},{6,7},{7,6},{8,9},{9,8},{10,11... | collective-permute-start | bytes 10616840 | tf_op jit(solution)/shard_map/ppermute | solution.py:686
  100.6 37.1 %collective-permute-start.13 = (bf16[512,1536]{1,0:T(8,128)(2,1)}, bf16[512,1536]{1,0:T(8,128)(2,1)}, u32[]{:S(2)}, u32[]{:S(2)}) collective-permute-start(bf16[512,1536]{1,0:T(8,128)(2,1)} %refs_0_.4), channel_id=1, source_target_pairs={{0,8},{1,9},{2,10},{3,11},{4,12},{5,13},{6,14},{7,15},{8,0},{9,1},... | collective-permute-start | bytes 4718600 | tf_op jit(solution)/shard_map/ppermute | solution.py:686
  104.8 43.4 %collective-permute-start.14 = (bf16[384,1536]{1,0:T(8,128)(2,1)}, bf16[384,1536]{1,0:T(8,128)(2,1)S(1)}, u32[]{:S(2)}, u32[]{:S(2)}) collective-permute-start(bf16[384,1536]{1,0:T(8,128)(2,1)} %get-tuple-element.99.refs_0_), channel_id=1, source_target_pairs={{0,1},{1,0},{2,3},{3,2},{4,5},{5,4},{6,7},{7,6},{8,9},{9,8},{10,11... | collective-permute-start | bytes 3538952 | tf_op jit(solution)/shard_map/ppermute | solution.py:686
  157.8 37.8 %collective-permute-start.15 = (bf16[512,1536]{1,0:T(8,128)(2,1)}, bf16[512,1536]{1,0:T(8,128)(2,1)}, u32[]{:S(2)}, u32[]{:S(2)}) collective-permute-start(bf16[512,1536]{1,0:T(8,128)(2,1)} %multiply_convert_fusion.refs_0_), channel_id=1, source_target_pairs={{0,8},{1,9},{2,10},{3,11},{4,12},{5,13},{6,14},{7,15},{8,0},{9,1},... | collective-permute-start | bytes 4718600 | tf_op jit(solution)/shard_map/ppermute | solution.py:686
  158.3 12.1 %collective-permute-start.17 = (bf16[128,1536]{1,0:T(8,128)(2,1)S(1)}, bf16[128,1536]{1,0:T(8,128)(2,1)S(1)}, u32[]{:S(2)}, u32[]{:S(2)}) collective-permute-start(bf16[128,1536]{1,0:T(8,128)(2,1)S(1)} %copy-done.25), channel_id=1, source_target_pairs={{0,2},{1,3},{2,4},{3,5},{4,6},{5,7},{6,0},{7,1},{8,10},{9,11},{10,... | collective-permute-start | bytes 1179656 | tf_op jit(solution)/shard_map/ppermute | solution.py:686
  158.3 33.4 %collective-permute-start.18 = (bf16[128,1536]{1,0:T(8,128)(2,1)S(1)}, bf16[128,1536]{1,0:T(8,128)(2,1)S(1)}, u32[]{:S(2)}, u32[]{:S(2)}) collective-permute-start(bf16[128,1536]{1,0:T(8,128)(2,1)S(1)} %copy-done.25), channel_id=1, source_target_pairs={{0,4},{1,5},{2,6},{3,7},{4,0},{5,1},{6,2},{7,3},{8,12},{9,13},{10,... | collective-permute-start | bytes 1179656 | tf_op jit(solution)/shard_map/ppermute | solution.py:686
  160.9 34.0 %collective-permute-start.19 = (bf16[128,1536]{1,0:T(8,128)(2,1)S(1)}, bf16[128,1536]{1,0:T(8,128)(2,1)S(1)}, u32[]{:S(2)}, u32[]{:S(2)}) collective-permute-start(bf16[128,1536]{1,0:T(8,128)(2,1)S(1)} %copy-done.25), channel_id=1, source_target_pairs={{0,6},{1,7},{2,0},{3,1},{4,2},{5,3},{6,4},{7,5},{8,14},{9,15},{10,... | collective-permute-start | bytes 1179656 | tf_op jit(solution)/shard_map/ppermute | solution.py:686
  163.0 37.3 %collective-permute-start.16 = (bf16[512,1536]{1,0:T(8,128)(2,1)}, bf16[512,1536]{1,0:T(8,128)(2,1)}, u32[]{:S(2)}, u32[]{:S(2)}) collective-permute-start(bf16[512,1536]{1,0:T(8,128)(2,1)} %multiply_convert_fusion.refs_0_), channel_id=1, source_target_pairs={{0,1},{1,0},{2,3},{3,2},{4,5},{5,4},{6,7},{7,6},{8,9},{9,8},{10,11... | collective-permute-start | bytes 4718600 | tf_op jit(solution)/shard_map/ppermute | solution.py:686
  195.6 41.0 %collective-permute-start.23 = (bf16[512,1536]{1,0:T(8,128)(2,1)}, bf16[512,1536]{1,0:T(8,128)(2,1)}, u32[]{:S(2)}, u32[]{:S(2)}) collective-permute-start(bf16[512,1536]{1,0:T(8,128)(2,1)} %collective-permute-done.13.refs_1_), channel_id=1, source_target_pairs={{0,1},{1,0},{2,3},{3,2},{4,5},{5,4},{6,7},{7,6},{8,9},{9,8},{10,11... | collective-permute-start | bytes 4718600 | tf_op jit(solution)/shard_map/ppermute | solution.py:686
  196.1 40.5 %collective-permute-start.22 = (bf16[512,1536]{1,0:T(8,128)(2,1)}, bf16[512,1536]{1,0:T(8,128)(2,1)}, u32[]{:S(2)}, u32[]{:S(2)}) collective-permute-start(bf16[512,1536]{1,0:T(8,128)(2,1)} %refs_0_.4), channel_id=1, source_target_pairs={{0,1},{1,0},{2,3},{3,2},{4,5},{5,4},{6,7},{7,6},{8,9},{9,8},{10,11... | collective-permute-start | bytes 4718600 | tf_op jit(solution)/shard_map/ppermute | solution.py:686
  196.1 28.7 %collective-permute-start.21 = (bf16[384,1536]{1,0:T(8,128)(2,1)}, bf16[384,1536]{1,0:T(8,128)(2,1)}, u32[]{:S(2)}, u32[]{:S(2)}) collective-permute-start(bf16[384,1536]{1,0:T(8,128)(2,1)} %constant_dynamic-update-slice_fusion.3.refs_1_), channel_id=1, source_target_pairs={{0,16},{1,17},{2,18},{3,19},{4,20},{5,21},{6,22},{7,23},{8,24},{9,... | collective-permute-start | bytes 3538952 | tf_op jit(solution)/shard_map/ppermute | solution.py:686
  312.2 36.6 %collective-permute-start.26 = (bf16[512,1536]{1,0:T(8,128)(2,1)}, bf16[512,1536]{1,0:T(8,128)(2,1)S(1)}, u32[]{:S(2)}, u32[]{:S(2)}) collective-permute-start(bf16[512,1536]{1,0:T(8,128)(2,1)} %add_convert_fusion.3), channel_id=1, source_target_pairs={{0,8},{1,9},{2,10},{3,11},{4,12},{5,13},{6,14},{7,15},{8,0},{9,1},... | collective-permute-start | bytes 4718600 | tf_op jit(solution)/shard_map/ppermute | solution.py:686
  314.3 73.7 %collective-permute-start.28 = (bf16[1024,768]{1,0:T(8,128)(2,1)}, bf16[1024,768]{1,0:T(8,128)(2,1)S(1)}, u32[]{:S(2)}, u32[]{:S(2)}) collective-permute-start(bf16[1024,768]{1,0:T(8,128)(2,1)} %column_slots.2), channel_id=1, source_target_pairs={{0,16},{1,17},{2,18},{3,19},{4,20},{5,21},{6,22},{7,23},{8,24},{9,... | collective-permute-start | bytes 4718600 | tf_op jit(solution)/shard_map/ppermute | solution.py:686
  348.8 35.6 %collective-permute-start.27 = (bf16[512,1536]{1,0:T(8,128)(2,1)S(1)}, bf16[512,1536]{1,0:T(8,128)(2,1)S(1)}, u32[]{:S(2)}, u32[]{:S(2)}) collective-permute-start(bf16[512,1536]{1,0:T(8,128)(2,1)S(1)} %add_convert_fusion.2), channel_id=1, source_target_pairs={{0,8},{1,9},{2,10},{3,11},{4,12},{5,13},{6,14},{7,15},{8,0},{9,1},... | collective-permute-start | bytes 4718600 | tf_op jit(solution)/shard_map/ppermute | solution.py:686
  404.5 8.1 %collective-permute-start.29 = (bf16[1536,1536]{1,0:T(8,128)(2,1)}, bf16[1536,1536]{1,0:T(8,128)(2,1)S(1)}, u32[]{:S(2)}, u32[]{:S(2)}) collective-permute-start(bf16[1536,1536]{1,0:T(8,128)(2,1)} %packed_slots.4), channel_id=1, source_target_pairs={{0,1},{1,0},{2,3},{3,2},{4,5},{5,4},{6,7},{7,6},{8,9},{9,8},{10,11... | collective-permute-start | bytes 14155784 | tf_op jit(solution)/shard_map/ppermute | solution.py:686
  420.5 52.6 %collective-permute-start.30 = (bf16[768,1536]{1,0:T(8,128)(2,1)}, bf16[768,1536]{1,0:T(8,128)(2,1)}, u32[]{:S(2)}, u32[]{:S(2)}) collective-permute-start(bf16[768,1536]{1,0:T(8,128)(2,1)} %packed_slots.5), channel_id=1, source_target_pairs={{0,8},{1,17},{2,10},{3,19},{4,12},{5,21},{6,14},{7,23},{8,0},{9,25... | collective-permute-start | bytes 7077896 | tf_op jit(solution)/shard_map/ppermute | solution.py:686
  434.4 32.1 %collective-permute-start.42 = (bf16[192,2048]{1,0:T(8,128)(2,1)}, bf16[192,2048]{1,0:T(8,128)(2,1)}, u32[]{:S(2)}, u32[]{:S(2)}) collective-permute-start(bf16[192,2048]{1,0:T(8,128)(2,1)} %reduce-scatter.2.cloned.1.call-done), channel_id=1, source_target_pairs={{0,8},{1,17},{2,10},{3,19},{4,12},{5,21},{6,14},{7,23},{8,0},{9,25... | collective-permute-start | bytes 2359304 | tf_op jit(solution)/shard_map/ppermute | solution.py:686
  435.0 55.4 %collective-permute-start.44 = (bf16[192,2048]{1,0:T(8,128)(2,1)}, bf16[192,2048]{1,0:T(8,128)(2,1)}, u32[]{:S(2)}, u32[]{:S(2)}) collective-permute-start(bf16[192,2048]{1,0:T(8,128)(2,1)} %reduce-scatter.2.cloned.1.call-done), channel_id=1, source_target_pairs={{0,16},{1,9},{2,18},{3,11},{4,20},{5,13},{6,22},{7,15},{8,24},{9,1... | collective-permute-start | bytes 2359304 | tf_op jit(solution)/shard_map/ppermute | solution.py:686
  466.6 23.9 %collective-permute-start.43 = (bf16[192,2048]{1,0:T(8,128)(2,1)}, bf16[192,2048]{1,0:T(8,128)(2,1)}, u32[]{:S(2)}, u32[]{:S(2)}) collective-permute-start(bf16[192,2048]{1,0:T(8,128)(2,1)} %collective-permute-done.42), channel_id=1, source_target_pairs={{0,16},{1,9},{2,18},{3,11},{4,20},{5,13},{6,22},{7,15},{8,24},{9,1... | collective-permute-start | bytes 2359304 | tf_op jit(solution)/shard_map/ppermute | solution.py:686
  477.3 48.2 %collective-permute-start.34 = (bf16[384,1536]{1,0:T(8,128)(2,1)}, bf16[384,1536]{1,0:T(8,128)(2,1)S(1)}, u32[]{:S(2)}, u32[]{:S(2)}) collective-permute-start(bf16[384,1536]{1,0:T(8,128)(2,1)} %packed_slots.6), channel_id=1, source_target_pairs={{0,16},{1,9},{2,18},{3,11},{4,20},{5,13},{6,22},{7,15},{8,24},{9,1... | collective-permute-start | bytes 3538952 | tf_op jit(solution)/shard_map/ppermute | solution.py:686
  485.6 28.3 %collective-permute-start.31 = (bf16[256,768]{1,0:T(8,128)(2,1)S(1)}, bf16[256,768]{1,0:T(8,128)(2,1)S(1)}, u32[]{:S(2)}, u32[]{:S(2)}) collective-permute-start(bf16[256,768]{1,0:T(8,128)(2,1)S(1)} %get-tuple-element.167), channel_id=1, source_target_pairs={{0,2},{1,3},{2,4},{3,5},{4,6},{5,7},{6,0},{7,1},{8,10},{9,11},{10,... | collective-permute-start | bytes 1179656 | tf_op jit(solution)/shard_map/ppermute | solution.py:686
  489.2 32.5 %collective-permute-start.32 = (bf16[256,768]{1,0:T(8,128)(2,1)S(1)}, bf16[256,768]{1,0:T(8,128)(2,1)S(1)}, u32[]{:S(2)}, u32[]{:S(2)}) collective-permute-start(bf16[256,768]{1,0:T(8,128)(2,1)S(1)} %get-tuple-element.166), channel_id=1, source_target_pairs={{0,4},{1,5},{2,6},{3,7},{4,0},{5,1},{6,2},{7,3},{8,12},{9,13},{10,... | collective-permute-start | bytes 1179656 | tf_op jit(solution)/shard_map/ppermute | solution.py:686
  490.4 34.4 %collective-permute-start.33 = (bf16[256,768]{1,0:T(8,128)(2,1)S(1)}, bf16[256,768]{1,0:T(8,128)(2,1)S(1)}, u32[]{:S(2)}, u32[]{:S(2)}) collective-permute-start(bf16[256,768]{1,0:T(8,128)(2,1)S(1)} %get-tuple-element.165), channel_id=1, source_target_pairs={{0,6},{1,7},{2,0},{3,1},{4,2},{5,3},{6,4},{7,5},{8,14},{9,15},{10,... | collective-permute-start | bytes 1179656 | tf_op jit(solution)/shard_map/ppermute | solution.py:686
  490.5 71.3 %collective-permute-start.53 = (f32[32,128]{1,0:T(8,128)S(1)}, f32[32,128]{1,0:T(8,128)}, u32[]{:S(2)}, u32[]{:S(2)}) collective-permute-start(f32[32,128]{1,0:T(8,128)S(1)} %add.361), channel_id=1, source_target_pairs={{0,4},{1,5},{2,6},{3,7},{4,0},{5,1},{6,2},{7,3},{8,12},{9,13},{10,... | collective-permute-start | bytes 49160 | tf_op jit(solution)/shard_map/ppermute | solution.py:686
  525.0 12.0 %collective-permute-start.46 = (bf16[256,768]{1,0:T(8,128)(2,1)S(1)}, bf16[256,768]{1,0:T(8,128)(2,1)}, u32[]{:S(2)}, u32[]{:S(2)}) collective-permute-start(bf16[256,768]{1,0:T(8,128)(2,1)S(1)} %add_convert_fusion.4), channel_id=1, source_target_pairs={{0,8},{1,17},{2,10},{3,19},{4,12},{5,21},{6,14},{7,23},{8,0},{9,25... | collective-permute-start | bytes 1179656 | tf_op jit(solution)/shard_map/ppermute | solution.py:686
  532.5 10.0 %collective-permute-start.35 = (bf16[96,1536]{1,0:T(8,128)(2,1)S(1)}, bf16[96,1536]{1,0:T(8,128)(2,1)S(1)}, u32[]{:S(2)}, u32[]{:S(2)}) collective-permute-start(bf16[96,1536]{1,0:T(8,128)(2,1)S(1)} %get-tuple-element.174), channel_id=1, source_target_pairs={{0,2},{1,3},{2,4},{3,5},{4,6},{5,7},{6,0},{7,1},{8,10},{9,11},{10,... | collective-permute-start | bytes 884744 | tf_op jit(solution)/shard_map/ppermute | solution.py:686
  532.6 25.5 %collective-permute-start.36 = (bf16[96,1536]{1,0:T(8,128)(2,1)S(1)}, bf16[96,1536]{1,0:T(8,128)(2,1)S(1)}, u32[]{:S(2)}, u32[]{:S(2)}) collective-permute-start(bf16[96,1536]{1,0:T(8,128)(2,1)S(1)} %get-tuple-element.176), channel_id=1, source_target_pairs={{0,4},{1,5},{2,6},{3,7},{4,0},{5,1},{6,2},{7,3},{8,12},{9,13},{10,... | collective-permute-start | bytes 884744 | tf_op jit(solution)/shard_map/ppermute | solution.py:686
  533.0 26.4 %collective-permute-start.37 = (bf16[96,1536]{1,0:T(8,128)(2,1)S(1)}, bf16[96,1536]{1,0:T(8,128)(2,1)S(1)}, u32[]{:S(2)}, u32[]{:S(2)}) collective-permute-start(bf16[96,1536]{1,0:T(8,128)(2,1)S(1)} %get-tuple-element.175), channel_id=1, source_target_pairs={{0,6},{1,7},{2,0},{3,1},{4,2},{5,3},{6,4},{7,5},{8,14},{9,15},{10,... | collective-permute-start | bytes 884744 | tf_op jit(solution)/shard_map/ppermute | solution.py:686
  537.0 42.9 %collective-permute-start.45 = (bf16[384,2048]{1,0:T(8,128)(2,1)S(1)}, bf16[384,2048]{1,0:T(8,128)(2,1)S(1)}, u32[]{:S(2)}, u32[]{:S(2)}) collective-permute-start(bf16[384,2048]{1,0:T(8,128)(2,1)S(1)} %get-tuple-element.152), channel_id=1, source_target_pairs={{0,1},{1,0},{2,3},{3,2},{4,5},{5,4},{6,7},{7,6},{8,9},{9,8},{10,11... | collective-permute-start | bytes 4718600 | tf_op jit(solution)/shard_map/ppermute | solution.py:686
  542.5 29.0 %collective-permute-start.48 = (bf16[256,768]{1,0:T(8,128)(2,1)S(1)}, bf16[256,768]{1,0:T(8,128)(2,1)}, u32[]{:S(2)}, u32[]{:S(2)}) collective-permute-start(bf16[256,768]{1,0:T(8,128)(2,1)S(1)} %add_convert_fusion.4), channel_id=1, source_target_pairs={{0,16},{1,9},{2,18},{3,11},{4,20},{5,13},{6,22},{7,15},{8,24},{9,1... | collective-permute-start | bytes 1179656 | tf_op jit(solution)/shard_map/ppermute | solution.py:686
  558.1 13.4 %collective-permute-start.47 = (bf16[256,768]{1,0:T(8,128)(2,1)}, bf16[256,768]{1,0:T(8,128)(2,1)}, u32[]{:S(2)}, u32[]{:S(2)}) collective-permute-start(bf16[256,768]{1,0:T(8,128)(2,1)} %collective-permute-done.46), channel_id=1, source_target_pairs={{0,16},{1,9},{2,18},{3,11},{4,20},{5,13},{6,22},{7,15},{8,24},{9,1... | collective-permute-start | bytes 1179656 | tf_op jit(solution)/shard_map/ppermute | solution.py:686
  561.3 8.0 %collective-permute-start.38 = (bf16[96,1536]{1,0:T(8,128)(2,1)}, bf16[96,1536]{1,0:T(8,128)(2,1)}, u32[]{:S(2)}, u32[]{:S(2)}) collective-permute-start(bf16[96,1536]{1,0:T(8,128)(2,1)} %add_convert_fusion.5), channel_id=1, source_target_pairs={{0,8},{1,17},{2,10},{3,19},{4,12},{5,21},{6,14},{7,23},{8,0},{9,25... | collective-permute-start | bytes 884744 | tf_op jit(solution)/shard_map/ppermute | solution.py:686
  565.2 7.6 %collective-permute-start.40 = (bf16[96,1536]{1,0:T(8,128)(2,1)}, bf16[96,1536]{1,0:T(8,128)(2,1)S(1)}, u32[]{:S(2)}, u32[]{:S(2)}) collective-permute-start(bf16[96,1536]{1,0:T(8,128)(2,1)} %add_convert_fusion.5), channel_id=1, source_target_pairs={{0,16},{1,9},{2,18},{3,11},{4,20},{5,13},{6,22},{7,15},{8,24},{9,1... | collective-permute-start | bytes 884744 | tf_op jit(solution)/shard_map/ppermute | solution.py:686
  577.8 9.2 %collective-permute-start.41 = (bf16[192,1152]{1,0:T(8,128)(2,1)S(1)}, bf16[192,1152]{1,0:T(8,128)(2,1)S(1)}, u32[]{:S(2)}, u32[]{:S(2)}) collective-permute-start(bf16[192,1152]{1,0:T(8,128)(2,1)S(1)} %broadcast_select_fusion.5), channel_id=1, source_target_pairs={{0,1},{1,0},{2,3},{3,2},{4,5},{5,4},{6,7},{7,6},{8,9},{9,8},{10,11... | collective-permute-start | bytes 1327112 | tf_op jit(solution)/shard_map/ppermute | solution.py:686
  (44 other events, 422.8 us)
Sparse Core Ops, SparseCore 0:
  57.5 99.1 all-gather.1
  312.3 122.0 reduce-scatter.1
